TPU v7x, 512 devices: a whole 4x8x8 slice. The times are simulated.
512 devices in a mesh: samp: 32 (over z_hi, y, core), pen: 16 (over x, z_lo).
Axes of the slice: x: 4, y: 8, z: 8 (z_hi: 2, z_lo: 4; z = z_hi * 4 + z_lo), core: 2. Of those that a mesh axis runs over, the one named last changes fastest.
Arguments:
- activations: bfloat16 [32, 96, 32, 1024], P('samp', None, 'pen'), may hold values from -6 to 6
- cotangent: bfloat16 [32, 96, 32, 1024], P('samp', None, 'pen'), may hold values from -6 to 6
- depth_kernels: float32 [3, 96, 9], replicated, may hold values from -5 to 5
- dilations: int32 [3], replicated, may hold values from 1 to 3
- expand_weight: bfloat16 [96, 384], replicated, may hold values from -0.625 to 0.625
- reduce_weight: bfloat16 [384, 96], replicated, may hold values from -0.3125 to 0.3125
Outputs:
- grad_input: bfloat16 [32, 96, 32, 1024], P('samp', None, 'pen')
- grad_expand: float32 [96, 384], P(None, 'pen')
- grad_reduce: float32 [384, 96], P('pen')
- grad_kernels: float32 [3, 96, 9], replicated
All inputs are finite; a program needn't handle non-finite values.
Results may differ from a plain program's by a relative error of at most 0.0085.
Values may be sent and summed in bfloat16 or wider, within the bound.
No kernel may reach another device: no remote copies, remote signals or barrier semaphores. Data moves between devices by JAX's collectives and lax.ppermute only.
A program may use at most 64 MiB of HBM per device.

v0:
```python
import math

import jax
import jax.numpy as jnp
from jax import lax
from jax.sharding import PartitionSpec as P

C = 96
H = 384
L = 32
TAPS = 9


def settle(values):
    return lax.optimization_barrier(values.astype(jnp.bfloat16)).astype(jnp.float32)


def taps_apply(field, kernel_rows, spacing, direction, sign):
    shape = [1] * field.ndim
    shape[1] = kernel_rows.shape[0]
    total = jnp.zeros(field.shape, jnp.float32)
    for tap_index in range(TAPS):
        weight_col = kernel_rows[:, tap_index].reshape(shape)
        total = total + weight_col * jnp.roll(field, sign * (tap_index - 4) * spacing, direction)
    return total


def taps_grad(upstream, field, spacing, direction):
    columns = []
    for tap_index in range(TAPS):
        moved = jnp.roll(field, -(tap_index - 4) * spacing, direction)
        columns.append(jnp.sum(upstream * moved, axis=(0, 2, 3, 4)))
    return jnp.stack(columns, axis=-1)


def per_device(activations, cotangent, depth_kernels, dilations, expand_weight, reduce_weight):
    samples_here = activations.shape[0]
    planes = activations.shape[2]
    lattice = activations.reshape(samples_here, C, planes, L, L)
    lines_in = lax.all_to_all(lattice, "pen", split_axis=3, concat_axis=2, tiled=True)
    first_lines = taps_apply(
        lines_in.astype(jnp.float32), depth_kernels[0], dilations[0], 2, -1
    ).astype(jnp.bfloat16)
    first = lax.all_to_all(first_lines, "pen", split_axis=2, concat_axis=3, tiled=True)
    first_f = first.astype(jnp.float32)
    second_f = settle(taps_apply(first_f, depth_kernels[1], dilations[1], 3, -1))
    mixed = taps_apply(second_f, depth_kernels[2], dilations[2], 4, -1).astype(jnp.bfloat16)
    sites_here = planes * L * L
    mixed_flat = mixed.reshape(samples_here, C, sites_here)
    cot_flat = cotangent.reshape(samples_here, C, sites_here)
    pre = jnp.einsum("scp,ch->shp", mixed_flat, expand_weight, preferred_element_type=jnp.float32)
    hidden = jax.nn.gelu(pre, approximate=True).astype(jnp.bfloat16)
    d_hidden = jnp.einsum(
        "scp,hc->shp", cot_flat, reduce_weight, preferred_element_type=jnp.float32
    )
    pullback = jax.vjp(lambda values: jax.nn.gelu(values, approximate=True), pre)[1]
    d_pre = pullback(d_hidden)[0].astype(jnp.bfloat16)
    part_reduce = jnp.einsum("shp,scp->hc", hidden, cot_flat, preferred_element_type=jnp.float32)
    part_expand = jnp.einsum("scp,shp->ch", mixed_flat, d_pre, preferred_element_type=jnp.float32)
    d_mixed = jnp.einsum("shp,ch->scp", d_pre, expand_weight, preferred_element_type=jnp.float32)
    d_mixed = settle(d_mixed).reshape(samples_here, C, planes, L, L)
    d_second = settle(taps_apply(d_mixed, depth_kernels[2], dilations[2], 4, 1))
    d_first = taps_apply(d_second, depth_kernels[1], dilations[1], 3, 1).astype(jnp.bfloat16)
    kernel_two = taps_grad(d_mixed, second_f, dilations[2], 4)
    kernel_one = taps_grad(d_second, first_f, dilations[1], 3)
    d_first_lines = lax.all_to_all(d_first, "pen", split_axis=3, concat_axis=2, tiled=True)
    d_first_f = d_first_lines.astype(jnp.float32)
    d_conv_lines = taps_apply(d_first_f, depth_kernels[0], dilations[0], 2, 1).astype(jnp.bfloat16)
    kernel_zero = taps_grad(d_first_f, lines_in.astype(jnp.float32), dilations[0], 2)
    d_conv = lax.all_to_all(d_conv_lines, "pen", split_axis=2, concat_axis=3, tiled=True)
    grad_input = (
        cotangent.astype(jnp.float32) + d_conv.astype(jnp.float32).reshape(cotangent.shape)
    ).astype(jnp.bfloat16)
    part_kernels = jnp.stack([kernel_zero, kernel_one, kernel_two])
    norm_scale = 1.0 / math.sqrt(lax.axis_size("samp") * samples_here * L * L * L)
    block_hidden = H // lax.axis_size("pen")
    sum_expand, sum_reduce, sum_kernels = lax.psum(
        (part_expand, part_reduce, part_kernels), ("samp", "pen")
    )
    start_hidden = lax.axis_index("pen") * block_hidden
    own_expand = lax.dynamic_slice_in_dim(sum_expand, start_hidden, block_hidden, 1)
    own_reduce = lax.dynamic_slice_in_dim(sum_reduce, start_hidden, block_hidden, 0)
    return (grad_input, own_expand * norm_scale, own_reduce * norm_scale, sum_kernels * norm_scale)


def solution(mesh):
    return jax.shard_map(
        per_device,
        mesh=mesh,
        in_specs=(P("samp", None, "pen", None), P("samp", None, "pen", None), P(), P(), P(), P()),
        out_specs=(P("samp", None, "pen", None), P(None, "pen"), P("pen", None), P()),
        check_vma=False,
    )
```

profile of v0, /device:TPU:1, one launch (start us, length us, event | category | flops | bytes accessed | tf_op | source)
XLA Modules:
  0.0 502.5 jit_solution(588211937751552351)
XLA Ops:
  7.2 1.4 copy.58
  9.4 10.4 %all-to-all-start = ((bf16[1,96,2,32,32]{1,4,2,0,3:T(8,128)(2,1)}), bf16[1,96,2,32,32]{1,4,2,0,3:T(8,128)(2,1)S(1)}, u32[]{:S(2)}, u32[]{:S(2)}) async-start(bf16[1,96,2,32,32]{1,4,2,0,3:T(8,128)(2,1)} %copy.59), calls=%async_computation | async-start | bytes 1048576 | tf_op jit(solution)/shard_map/all_to_all | solution.py:40
  27.2 8.4 %all-to-all-done = bf16[1,96,2,32,32]{1,4,2,0,3:T(8,128)(2,1)S(1)} async-done(((bf16[1,96,2,32,32]{1,4,2,0,3:T(8,128)(2,1)}), bf16[1,96,2,32,32]{1,4,2,0,3:T(8,128)(2,1)S(1)}, u32[]{:S(2)}, u32[]{:S(2)}) %all-to-all-start) | async-done | bytes 393248 | tf_op jit(solution)/shard_map/all_to_all | solution.py:40
  35.8 5.0 fusion.122
  40.8 4.1 all-to-all-start.1
  61.8 2.9 add_convert_fusion.1
  64.9 5.0 add_convert_fusion
  70.5 1.8 fusion.11
  72.3 2.6 fusion.6
  76.1 1.2 fusion.133
  77.3 2.6 fusion.10
  81.1 5.1 %fusion.75 = bf16[1,96,2,32,32]{1,4,3,2,0:T(8,128)(2,1)S(1)} fusion(s32[]{:T(128)S(6)} %select_n.161, f32[1,96,2,32,32]{1,4,3,2,0:T(8,128)S(1)} %bitcast.162, s32[]{:T(128)S(6)} %select_n.175, s32[]{:T(128)S(6)} %select_n.173, s32[]{:T(128)S(6)} %select_n.171, s32[]{:T(128)S(6)} %select_n.169, s32[]{:T(128)S(6)} %select_n.167, s32[]{:T(128)S(6)} %select_n.165, ...), kind=kLoop, calls=%fused_computation.185 | loop fusion | flops 5111808 | bytes 1183136 | tf_op jit(solution)/shard_map/convert_element_type | solution.py:15
  87.3 2.0 fusion.13
  89.5 3.2 fusion.21
  93.6 6.1 %all-to-all-start.2 = ((bf16[1,96,2,32,32]{1,4,2,0,3:T(8,128)(2,1)}), bf16[1,96,2,32,32]{1,4,2,0,3:T(8,128)(2,1)}, u32[]{:S(2)}, u32[]{:S(2)}) async-start(bf16[1,96,2,32,32]{1,4,2,0,3:T(8,128)(2,1)} %copy.67), calls=%async_computation.2 | async-start | bytes 1048576 | tf_op jit(solution)/shard_map/all_to_all | solution.py:66
  100.4 3.1 multiply_reduce_fusion
  104.7 272.5 %all-reduce.3.cloned.1.call-done = (f32[96,384]{0,1:T(8,128)}, f32[384,96]{1,0:T(8,128)}) async-done(((f32[96,384]{0,1:T(8,128)}, f32[384,96]{1,0:T(8,128)}), (f32[96,384]{0,1:T(8,128)}, f32[384,96]{1,0:T(8,128)})) %all-reduce.3.cloned.1.call-update) | async-done | bytes 294928 | tf_op jit(solution)/shard_map/psum | solution.py:77
  377.1 1.3 fusion.125
  378.4 1.3 fusion.124
  381.0 1.7 multiply_reduce_fusion.10
  382.8 5.0 fusion.123
  387.8 5.4 %all-to-all-start.3 = ((bf16[1,96,32,2,32]{1,4,3,0,2:T(8,128)(2,1)}), bf16[1,96,32,2,32]{1,4,3,0,2:T(8,128)(2,1)S(1)}, u32[]{:S(2)}, u32[]{:S(2)}) async-start(bf16[1,96,32,2,32]{1,4,3,0,2:T(8,128)(2,1)} %fusion.123), calls=%async_computation.3 | async-start | bytes 1048576 | tf_op jit(solution)/shard_map/all_to_all | solution.py:70
  393.2 3.1 multiply_reduce_fusion.9
  396.3 97.0 %psum.23 = f32[3,96,9]{1,2,0:T(8,128)S(1)} all-reduce(f32[3,96,9]{1,2,0:T(8,128)S(1)} %pad_maximum_fusion), channel_id=1, replica_groups=mesh['samp'=32,'pen'=16] {'samp','pen'}, use_global_device_ids=true, to_apply=%region_29.36 | all-reduce | flops 2592 | bytes 20736 | tf_op jit(solution)/shard_map/psum | solution.py:77
  (62 shorter events, 15.6 us)
Async XLA Ops:
  7.2 62.7 %copy-start = (bf16[96,384]{1,0:T(8,128)(2,1)S(1)}, bf16[96,384]{1,0:T(8,128)(2,1)}, u32[]{:S(2)}) copy-start(bf16[96,384]{1,0:T(8,128)(2,1)} %param.22) | copy-start | bytes 221188
  7.2 12.7 %copy-start.9 = (s32[3]{0:T(128)S(1)}, s32[3]{0:T(128)}, u32[]{:S(2)}) copy-start(s32[3]{0:T(128)} %param.21) | copy-start | bytes 40
  7.2 19.9 %copy-start.8 = (f32[3,96,9]{1,0,2:T(4,128)S(1)}, f32[3,96,9]{1,0,2:T(4,128)}, u32[]{:S(2)}) copy-start(f32[3,96,9]{1,0,2:T(4,128)} %param.20) | copy-start | bytes 31108
  9.4 26.1 %all-to-all-start = ((bf16[1,96,2,32,32]{1,4,2,0,3:T(8,128)(2,1)}), bf16[1,96,2,32,32]{1,4,2,0,3:T(8,128)(2,1)S(1)}, u32[]{:S(2)}, u32[]{:S(2)}) async-start(bf16[1,96,2,32,32]{1,4,2,0,3:T(8,128)(2,1)} %copy.59), calls=%async_computation | async-start | bytes 1048576 | tf_op jit(solution)/shard_map/all_to_all | solution.py:40
  35.7 22.5 %copy-start.7 = (bf16[1,96,2,1024]{3,2,1,0:T(2,128)(2,1)S(1)}, bf16[1,96,2,1024]{3,2,1,0:T(2,128)(2,1)}, u32[]{:S(2)}) copy-start(bf16[1,96,2,1024]{3,2,1,0:T(2,128)(2,1)} %param.19) | copy-start | bytes 1179652
  40.8 19.7 %all-to-all-start.1 = ((bf16[1,96,32,2,32]{1,4,3,0,2:T(8,128)(2,1)}), bf16[1,96,32,2,32]{1,4,3,0,2:T(8,128)(2,1)S(1)}, u32[]{:S(2)}, u32[]{:S(2)}) async-start(bf16[1,96,32,2,32]{1,4,3,0,2:T(8,128)(2,1)} %fusion.122), calls=%async_computation.1 | async-start | bytes 1048576 | tf_op jit(solution)/shard_map/all_to_all | solution.py:44
  60.8 1.0 copy-start.1
  64.7 5.8 %copy-start.3 = (bf16[1,96,2,32,32]{1,4,3,2,0:T(8,128)(2,1)}, bf16[1,96,2,32,32]{1,4,3,2,0:T(8,128)(2,1)S(1)}, u32[]{:S(2)}) copy-start(bf16[1,96,2,32,32]{1,4,3,2,0:T(8,128)(2,1)S(1)} %add_convert_fusion.1) | copy-start | bytes 1179652
  70.5 1.8 copy-start.10
  74.9 1.2 copy-start.5
  81.1 5.1 %copy-start.2 = (f32[1,96,2,16,2,32]{1,5,4,3,2,0:T(8,128)S(1)}, f32[1,96,2,16,2,32]{1,5,4,3,2,0:T(8,128)}, u32[]{:S(2)}) copy-start(f32[1,96,2,16,2,32]{1,5,4,3,2,0:T(8,128)} %copy-done.1) | copy-start | bytes 2359300
  93.6 286.2 %all-to-all-start.2 = ((bf16[1,96,2,32,32]{1,4,2,0,3:T(8,128)(2,1)}), bf16[1,96,2,32,32]{1,4,2,0,3:T(8,128)(2,1)}, u32[]{:S(2)}, u32[]{:S(2)}) async-start(bf16[1,96,2,32,32]{1,4,2,0,3:T(8,128)(2,1)} %copy.67), calls=%async_computation.2 | async-start | bytes 1048576 | tf_op jit(solution)/shard_map/all_to_all | solution.py:66
  99.6 277.5 %all-reduce.3.cloned.1.call-start = ((), (), s32[]{:S(2)}) async-start(), calls=%async_computation.4 | async-start | bytes 786432 | tf_op jit(solution)/shard_map/psum | solution.py:77
  100.4 3.1 copy-start.4
  387.8 106.2 %all-to-all-start.3 = ((bf16[1,96,32,2,32]{1,4,3,0,2:T(8,128)(2,1)}), bf16[1,96,32,2,32]{1,4,3,0,2:T(8,128)(2,1)S(1)}, u32[]{:S(2)}, u32[]{:S(2)}) async-start(bf16[1,96,32,2,32]{1,4,3,0,2:T(8,128)(2,1)} %fusion.123), calls=%async_computation.3 | async-start | bytes 1048576 | tf_op jit(solution)/shard_map/all_to_all | solution.py:70
  396.3 97.9 %copy-start.6 = (bf16[1,96,2,1024]{1,3,2,0:T(8,128)(2,1)S(1)}, bf16[1,96,2,1024]{1,3,2,0:T(8,128)(2,1)}, u32[]{:S(2)}) copy-start(bf16[1,96,2,1024]{1,3,2,0:T(8,128)(2,1)} %copy.54) | copy-start | bytes 1179652
Sparse Core Ops, SparseCore 0:
  105.7 271.3 all-reduce.2
where the time goes:
time: 508 us; the launch traced here: 503 us
  waiting for transfers between devices  283 us (56%)
  blocking collectives  97 us (19%)
  other arithmetic  41.8 us (8%)
  between operations  34.7 us (7%)
  starting transfers between devices  26 us (5%)
  local copies, waits for them, and re-layouts  11.6 us (2%)
  matrix products  8.85 us (2%)
    psum x1, waiting for transfers between devices, per_device(): lax.psum((part_expand, part_reduce, part_kernels), ('samp', 'pen'))  272 us
    psum x1, blocking collectives, per_device(): lax.psum((part_expand, part_reduce, part_kernels), ('samp', 'pen'))  97 us
    reduce_sum x6, other arithmetic, taps_grad(): columns.append(jnp.sum(upstream * moved, axis=(0, 2, 3, 4)))  12.2 us
    all_to_all x1, starting transfers between devices, per_device(): lax.all_to_all(lattice, 'pen', split_axis=3, concat_axis=2, tiled=True)  10.4 us
  transfers between devices with their start and end apart: 5, of which 3 were waited for; matrix products, arithmetic and copies ran while one was open for 2% of the time, Pallas kernels for 0%

commit v1 on v0

v1 whole, which is shorter than its diff:
```python
import math

import jax
import jax.numpy as jnp
import numpy as np
from jax import lax
from jax.experimental import pallas as pl
from jax.experimental.pallas import tpu as pltpu
from jax.sharding import Mesh
from jax.sharding import PartitionSpec as P

C = 96
H = 384
L = 32
TAPS = 9
GROUPS = 16
CH = C // GROUPS
ROWS = C * L * L * 2 // 128
STRIDE = 16
HALO = 16
F32 = jnp.float32
BF16 = jnp.bfloat16
SAMP = ("zh", "y", "core")


def delta_table():
    r = np.arange(256)
    plane, rest = r // 128, r % 128
    x, c = 2 * (rest // CH) + plane, rest % CH
    valid = rest < C
    delta = (x[:, None] - x[None, :]) % L
    same = (c[:, None] == c[None, :]) & valid[:, None] & valid[None, :]
    return np.where(same, delta, -1).astype(np.int32)


def channel_table():
    r = np.arange(256) % 128
    out = np.zeros((8, 256), np.float32)
    for c in range(CH):
        out[c] = (r % CH == c) & (r < C)
    return out


def contract(a, b, da, db):
    return lax.dot_general(a, b, (((da,), (db,)), ((), ())), preferred_element_type=F32)


def pieces(stage, j, p):
    return stage[pl.ds(2 * j + p, C, stride=STRIDE), :]


def for_each_dilation(spacing):
    def run(body):
        for d in (1, 2, 3):
            @pl.when(spacing == d)
            def _():
                @pl.loop(0, L)
                def _(y):
                    body(d, y)
    return run


def conv_fwd(dil, a_ref, coef, delta, mixed_ref, first_ref, second_ref, field_ref, hi_ref, lo_ref,
             stage, fir, sec, mix):
    d0, d1, d2 = dil[0], dil[1], dil[2]
    stage[...] = a_ref[...].astype(F32)
    m = jnp.zeros((256, 256), F32)
    for t in range(TAPS):
        m = m + jnp.where(delta[...] == (((t - 4) * d0) & (L - 1)), coef[t:t + 1, :], 0.0)
    hi = m.astype(BF16)
    lo = (m - hi.astype(F32)).astype(BF16)
    hi_ref[...] = hi
    lo_ref[...] = lo
    eye = jnp.where(delta[...] == 0, 1.0, 0.0).astype(BF16)
    gap = jnp.zeros((32, 128), F32)
    for j in range(8):
        parts = []
        for p in range(2):
            parts += [pieces(stage, j, p), gap]
        f = jnp.concatenate(parts, axis=0).astype(BF16)
        field_ref[:, j * 128:(j + 1) * 128] = f
        out = contract(f, hi, 0, 0) + contract(f, lo, 0, 0)
        out = out.astype(BF16)
        first_ref[j * 128:(j + 1) * 128, :] = out
        fir[4 * j:4 * j + 4] = out.astype(F32).reshape(4, L, 256)

    @pl.loop(0, L)
    def _(y):
        acc = jnp.zeros((L, 256), F32)
        for t in range(TAPS):
            acc = acc + coef[16 + t:17 + t, :] * fir[(y + (t - 4) * d1) & (L - 1)]
        acc = acc.astype(BF16)
        second_ref[pl.ds(pl.multiple_of(y * L, L), L), :] = acc
        acc = acc.astype(F32)
        sec[y, HALO:HALO + L, :] = acc
        sec[y, 0:HALO, :] = acc[L - HALO:, :]
        sec[y, HALO + L:, :] = acc[:HALO, :]

    @for_each_dilation(d2)
    def _(d, y):
        acc = jnp.zeros((L, 256), F32)
        for t in range(TAPS):
            at = HALO + (t - 4) * d
            acc = acc + coef[32 + t:33 + t, :] * sec[y, at:at + L, :]
        mix[pl.ds(pl.multiple_of(y * L, L), L), :] = acc.astype(BF16)

    for j in range(8):
        turned = contract(eye, mix[j * 128:(j + 1) * 128, :], 1, 1)
        for p in range(2):
            stage[pl.ds(2 * j + p, C, stride=STRIDE), :] = turned[p * 128:p * 128 + C, :]
    mixed_ref[...] = stage[...].astype(BF16)


def conv_bwd(dil, d_ref, coef, delta, table, first_ref, second_ref, field_ref, hi_ref, lo_ref,
             out_ref, kern_ref, stage, dmh, dse, dfi, acc_ref):
    d0, d1, d2 = dil[0], dil[1], dil[2]
    stage[...] = d_ref[...].astype(F32)
    acc_ref[...] = jnp.zeros_like(acc_ref)
    eye = jnp.where(delta[...] == 0, 1.0, 0.0).astype(BF16)
    gap = jnp.zeros((32, 128), F32)
    for j in range(8):
        parts = []
        for p in range(2):
            parts += [pieces(stage, j, p), gap]
        f = jnp.concatenate(parts, axis=0).astype(BF16)
        out = contract(f, eye, 0, 0).reshape(4, L, 256)
        dmh[4 * j:4 * j + 4, HALO:HALO + L, :] = out
        dmh[4 * j:4 * j + 4, 0:HALO, :] = out[:, L - HALO:, :]
        dmh[4 * j:4 * j + 4, HALO + L:, :] = out[:, :HALO, :]

    def fold(v):
        return v[0:8] + v[8:16] + v[16:24] + v[24:32]

    @for_each_dilation(d2)
    def _(d, y):
        row = pl.ds(pl.multiple_of(y * L, L), L)
        field = second_ref[row, :].astype(F32)
        acc = jnp.zeros((L, 256), F32)
        for t in range(TAPS):
            at = HALO - (t - 4) * d
            moved = dmh[y, at:at + L, :]
            acc = acc + coef[32 + t:33 + t, :] * moved
            acc_ref[18 + t] += fold(moved * field)
        dse[y] = acc.astype(BF16).astype(F32)

    @pl.loop(0, L)
    def _(y):
        row = pl.ds(pl.multiple_of(y * L, L), L)
        field = first_ref[row, :].astype(F32)
        acc = jnp.zeros((L, 256), F32)
        for t in range(TAPS):
            moved = dse[(y - (t - 4) * d1) & (L - 1)]
            acc = acc + coef[16 + t:17 + t, :] * moved
            acc_ref[9 + t] += fold(moved * field)
        dfi[row, :] = acc.astype(BF16)

    hi, lo = hi_ref[...], lo_ref[...]
    for j in range(8):
        block = dfi[j * 128:(j + 1) * 128, :]
        out = contract(hi, block, 1, 1) + contract(lo, block, 1, 1)
        for p in range(2):
            stage[pl.ds(2 * j + p, C, stride=STRIDE), :] = out[p * 128:p * 128 + C, :]
    out_ref[...] = stage[...].astype(BF16)
    cross = contract(field_ref[...], dfi[...], 1, 0)
    for t in range(TAPS):
        keep = jnp.where(delta[...] == (((t - 4) * d0) & (L - 1)), cross, 0.0)
        acc_ref[t] = jnp.sum(keep.reshape(32, 8, 256), axis=0)
    sums = jnp.sum(acc_ref[...], axis=1)
    kern_ref[...] = jnp.zeros_like(kern_ref)
    kern_ref[:, 0:32] = lax.dot_general(
        table[...], sums, (((1,), (1,)), ((), ())),
        precision=lax.Precision.HIGHEST, preferred_element_type=F32)


BLOCK = 256


def middle(m_ref, c_ref, we, wr, out_ref, expand_ref, reduce_ref, stage, stage_c, mix, cot):
    stage[...] = m_ref[...].astype(F32)
    stage_c[...] = c_ref[...].astype(F32)
    for j in range(8):
        for p in range(2):
            k = 2 * j + p
            mix[:, k * 128:(k + 1) * 128] = pieces(stage, j, p).astype(BF16)
            cot[:, k * 128:(k + 1) * 128] = pieces(stage_c, j, p).astype(BF16)
    expand_ref[...] = jnp.zeros_like(expand_ref)
    reduce_ref[...] = jnp.zeros_like(reduce_ref)
    root = math.sqrt(2.0 / math.pi)

    for b in range(2 * L * L // BLOCK):
        cols = slice(b * BLOCK, (b + 1) * BLOCK)
        mb, cb = mix[:, cols], cot[:, cols]
        pre = contract(we[...], mb, 0, 0)
        d_hidden = contract(wr[...], cb, 1, 0)
        square = pre * pre
        inner = root * pre * (1.0 + 0.044715 * square)
        half = 0.5 + 0.5 * jnp.tanh(inner)
        hidden = (pre * half).astype(BF16)
        slope = half + pre * (2.0 * half * (1.0 - half)) * (root * (1.0 + 3.0 * 0.044715 * square))
        d_pre = (d_hidden * slope).astype(BF16)
        reduce_ref[...] += contract(hidden, cb, 1, 1)
        expand_ref[...] += contract(d_pre, mb, 1, 1)
        out = contract(we[...], d_pre, 1, 0)
        for i in range(BLOCK // 128):
            k = b * (BLOCK // 128) + i
            stage[pl.ds(k, C, stride=STRIDE), :] = out[:, i * 128:(i + 1) * 128]
    out_ref[...] = stage[...].astype(BF16)


VMEM = pl.BlockSpec(memory_space=pltpu.VMEM)
SMEM = pl.BlockSpec(memory_space=pltpu.SMEM)
PARAMS = pltpu.CompilerParams(vmem_limit_bytes=28 * 1024 * 1024)


def shape(*dims, dtype=BF16):
    return jax.ShapeDtypeStruct(dims, dtype)


def run_conv_fwd(dilations, rows, coef, delta):
    return pl.pallas_call(
        conv_fwd,
        out_shape=(shape(ROWS, 128), shape(1024, 256), shape(1024, 256), shape(256, 1024),
                   shape(256, 256), shape(256, 256)),
        in_specs=[SMEM, VMEM, VMEM, VMEM],
        out_specs=(VMEM,) * 6,
        scratch_shapes=[pltpu.VMEM((ROWS, 128), F32), pltpu.VMEM((L, L, 256), F32),
                        pltpu.VMEM((L, L + 2 * HALO, 256), F32), pltpu.VMEM((1024, 256), BF16)],
        compiler_params=PARAMS,
        cost_estimate=pl.CostEstimate(flops=10**9, bytes_accessed=4 * 10**6, transcendentals=0),
        name="conv_fwd",
    )(dilations, rows, coef, delta)


def run_conv_bwd(dilations, rows, coef, delta, table, first, second, field, hi, lo):
    return pl.pallas_call(
        conv_bwd,
        out_shape=(shape(ROWS, 128), shape(8, 128, dtype=F32)),
        in_specs=[SMEM] + [VMEM] * 9,
        out_specs=(VMEM,) * 2,
        scratch_shapes=[pltpu.VMEM((ROWS, 128), F32), pltpu.VMEM((L, L + 2 * HALO, 256), F32),
                        pltpu.VMEM((L, L, 256), F32), pltpu.VMEM((1024, 256), BF16),
                        pltpu.VMEM((32, 8, 256), F32)],
        compiler_params=PARAMS,
        cost_estimate=pl.CostEstimate(flops=10**9, bytes_accessed=4 * 10**6, transcendentals=0),
        name="conv_bwd",
    )(dilations, rows, coef, delta, table, first, second, field, hi, lo)


def run_middle(rows, cot_rows, expand_weight, reduce_weight):
    return pl.pallas_call(
        middle,
        out_shape=(shape(ROWS, 128), shape(H, C, dtype=F32), shape(H, C, dtype=F32)),
        in_specs=[VMEM] * 4,
        out_specs=(VMEM,) * 3,
        scratch_shapes=[pltpu.VMEM((ROWS, 128), F32), pltpu.VMEM((ROWS, 128), F32),
                        pltpu.VMEM((C, 2048), BF16), pltpu.VMEM((C, 2048), BF16)],
        compiler_params=PARAMS,
        cost_estimate=pl.CostEstimate(flops=10**9, bytes_accessed=4 * 10**6, transcendentals=10**6),
        name="middle",
    )(rows, cot_rows, expand_weight, reduce_weight)


def to_rows(field):
    return field.reshape(C, 2, 8, 128).transpose(0, 2, 1, 3).reshape(ROWS, 128)


def from_rows(rows):
    return rows.reshape(C, 8, 2, 128).transpose(0, 2, 1, 3).reshape(1, C, 2, 1024)


def swap(rows):
    parts = rows.reshape(GROUPS, ROWS // GROUPS, 128)
    return lax.all_to_all(parts, "pen", 0, 0, tiled=True).reshape(ROWS, 128)


def sum_over(values, axes, size):
    copies = jnp.broadcast_to(values[None], (size,) + values.shape)
    return jnp.sum(lax.all_to_all(copies, axes, 0, 0, tiled=True), axis=0)


def per_device(activations, cotangent, depth_kernels, dilations, expand_weight, reduce_weight):
    delta = jnp.asarray(delta_table())
    table = jnp.asarray(channel_table())
    own = lax.dynamic_slice_in_dim(depth_kernels, lax.axis_index("pen") * CH, CH, 1)
    coef = jnp.tile(own.transpose(0, 2, 1), (1, 1, GROUPS))
    coef = jnp.pad(coef, ((0, 0), (0, 16 - TAPS), (0, 128 - C)))
    coef = jnp.concatenate([coef, coef], axis=2).reshape(48, 256)

    lines = swap(to_rows(activations))
    mixed, first, second, field, hi, lo = run_conv_fwd(dilations, lines, coef, delta)
    cot_rows = to_rows(cotangent)
    d_mixed, part_expand, part_reduce = run_middle(
        swap(mixed), cot_rows, expand_weight, reduce_weight)
    d_lines = swap(d_mixed)
    weights = jnp.concatenate(
        [part_expand.reshape(GROUPS, 24, C), part_reduce.reshape(GROUPS, 24, C)], axis=1)
    weights = lax.all_to_all(weights.astype(BF16), "pen", 0, 0, tiled=True)
    weights = jnp.sum(weights.astype(F32), axis=0)
    d_conv, kern = run_conv_bwd(
        dilations, d_lines, coef, delta, table, first, second, field, hi, lo)
    total = jnp.concatenate([jnp.pad(weights, ((0, 0), (0, 128 - C))), kern], axis=0)
    total = sum_over(total, "y", lax.axis_size("y"))
    total = sum_over(total, ("zh", "core"), lax.axis_size("zh") * lax.axis_size("core"))
    d_input = swap(d_conv)
    grad_input = from_rows((cot_rows.astype(F32) + d_input.astype(F32)).astype(BF16))

    samples = lax.axis_size("zh") * lax.axis_size("y") * lax.axis_size("core")
    total = total * (1.0 / math.sqrt(samples * L * L * L))
    own_expand = total[0:24, 0:C].T
    own_reduce = total[24:48, 0:C]
    kern = jnp.broadcast_to(total[None, 48:56, :], (GROUPS, 8, 128))
    kern = lax.all_to_all(kern, "pen", 0, 0, tiled=True)
    kern = kern[:, :CH, :3 * TAPS].reshape(C, 3, TAPS).transpose(1, 0, 2)
    return grad_input, own_expand, own_reduce, kern


def solution(mesh):
    samp = mesh.devices.shape[0]
    split = (2, samp // 4, 2) if samp % 4 == 0 else (1, samp, 1)
    fine = Mesh(mesh.devices.reshape(*split, GROUPS), (*SAMP, "pen"))
    field = P(SAMP, None, "pen", None)
    return jax.shard_map(
        per_device,
        mesh=fine,
        in_specs=(field, field, P(), P(), P(), P()),
        out_specs=(field, P(None, "pen"), P("pen", None), P()),
        check_vma=False,
    )
```

time: 508 us -> 149 us (0.29); the launches traced: 503 us -> 149 us
  waiting for transfers between devices: 283 us -> 46.8 us
  blocking collectives: 97 us -> 55.6 us
  other arithmetic: 41.8 us -> 1.32 us
  between operations: 34.7 us -> 0.84 us
  Pallas kernels: 0 us -> 18 us
  matrix products: 8.85 us -> 0 us
  local copies, waits for them, and re-layouts: 11.6 us -> 4.88 us
    psum x1 -> x0, waiting for transfers between devices: 272 us -> none  [per_device(): lax.psum((part_expand, part_reduce, part_kernels), ('samp', 'pen'))]
    psum x1 -> x0, blocking collectives: 97 us -> none  [per_device(): lax.psum((part_expand, part_reduce, part_kernels), ('samp', 'pen'))]
    all_to_all x0 -> x4, blocking collectives: none -> 55.6 us  [the longest x2 34.8 us: sum_over(): return jnp.sum(lax.all_to_all(copies, axes, 0, 0, tiled=True), axis=0)]
    all_to_all x4, waiting for transfers between devices: 9.37 us -> 46.8 us  [swap(): return lax.all_to_all(parts, 'pen', 0, 0, tiled=True).reshape(ROWS, 128)]
    convert_element_type x13 -> x0, other arithmetic: 27 us -> none  [the longest x2 7.98 us: settle(): values.astype(jnp.bfloat16)]
    pallas_call x0 -> x3, Pallas kernels: none -> 18 us  [the longest x1 7.75 us: run_conv_bwd(): pl.pallas_call(conv_bwd, out_shape=(shape(ROWS, 128), shape(8, 128, dtype...]
    reduce_sum x6 -> x3, other arithmetic: 12.2 us -> 0.07 us  [the longest x1 0.05 us: per_device(): weights = jnp.sum(weights.astype(F32), axis=0)]
    dot_general x5 -> x0, matrix products: 8.85 us -> none  [the longest x1 2.59 us: per_device(): jnp.einsum('scp,hc->shp', cot_flat, reduce_weight, preferred_element_type...]
  transfers between devices with their start and end apart: 5 -> 4, of which waited for: 3 -> 4; matrix products, arithmetic and copies ran while one was open for 2% -> 1% of each run, Pallas kernels for 0% -> 0%
where the time goes in v1:
time: 149 us
  blocking collectives  55.6 us (37%)
  waiting for transfers between devices  46.8 us (31%)
  starting transfers between devices  21.2 us (14%)
  Pallas kernels  18 us (12%)
  local copies, waits for them, and re-layouts  4.88 us (3%)
    all_to_all x4, waiting for transfers between devices, swap(): return lax.all_to_all(parts, 'pen', 0, 0, tiled=True).reshape(ROWS, 128)  46.8 us
    all_to_all x2, blocking collectives, sum_over(): return jnp.sum(lax.all_to_all(copies, axes, 0, 0, tiled=True), axis=0)  34.8 us
    all_to_all x4, starting transfers between devices, swap(): return lax.all_to_all(parts, 'pen', 0, 0, tiled=True).reshape(ROWS, 128)  21.2 us
    all_to_all x1, blocking collectives, per_device(): weights = lax.all_to_all(weights.astype(BF16), 'pen', 0, 0, tiled=True)  11 us
    all_to_all x1, blocking collectives, per_device(): kern = lax.all_to_all(kern, 'pen', 0, 0, tiled=True)  9.93 us
    pallas_call x1, Pallas kernels, run_conv_bwd(): pl.pallas_call(conv_bwd, out_shape=(shape(ROWS, 128), shape(8, 128, dtype...  7.75 us
    pallas_call x1, Pallas kernels, run_conv_fwd(): pl.pallas_call(conv_fwd, out_shape=(shape(ROWS, 128), shape(1024, 256), s...  5.4 us
    pallas_call x1, Pallas kernels, run_middle(): pl.pallas_call(middle, out_shape=(shape(ROWS, 128), shape(H, C, dtype=F32...  4.82 us
  transfers between devices with their start and end apart: 4, of which 4 were waited for; matrix products, arithmetic and copies ran while one was open for 1% of the time, Pallas kernels for 0%

profile of v1, /device:TPU:1, one launch (start us, length us, event | category | flops | bytes accessed | tf_op | source)
XLA Modules:
  0.0 148.6 jit_solution(16424786636416056343)
XLA Ops:
  0.6 1.3 reshape.65
  1.9 1.1 copy.32
  3.0 10.4 %all-to-all-start = ((bf16[16,96,128]{2,1,0:T(8,128)(2,1)}), bf16[16,96,128]{2,1,0:T(8,128)(2,1)S(1)}, u32[]{:S(2)}, u32[]{:S(2)}) async-start(bf16[16,96,128]{2,1,0:T(8,128)(2,1)} %bitcast.3), calls=%async_computation | async-start | bytes 786432 | tf_op jit(solution)/shard_map/all_to_all | solution.py:273
  13.5 0.1 tile.10
  13.7 12.6 %all-to-all-done = bf16[16,96,128]{2,1,0:T(8,128)(2,1)S(1)} async-done(((bf16[16,96,128]{2,1,0:T(8,128)(2,1)}), bf16[16,96,128]{2,1,0:T(8,128)(2,1)S(1)}, u32[]{:S(2)}, u32[]{:S(2)}) %all-to-all-start) | async-done | bytes 393248 | tf_op jit(solution)/shard_map/all_to_all | solution.py:273
  26.3 0.7 copy-done.3
  26.9 5.4 %conv_fwd.1 = (bf16[1536,128]{1,0:T(8,128)(2,1)}, bf16[1024,256]{1,0:T(8,128)(2,1)S(1)}, bf16[1024,256]{1,0:T(8,128)(2,1)S(1)}, bf16[256,1024]{1,0:T(8,128)(2,1)...) custom-call(s32[3]{0:T(128)S(1)} %copy-done.3, bf16[1536,128]{1,0:T(8,128)(2,1)S(1)} %bitcast.33, ...), custom_call_target="tpu_custom_call" | custom-call | flops 1000000000 | bytes 4000000 | tf_op jit(solution)/shard_map/conv_fwd/pallas_call | solution.py:220
  32.3 3.7 %all-to-all-start.1 = ((bf16[16,96,128]{2,1,0:T(8,128)(2,1)}), bf16[16,96,128]{2,1,0:T(8,128)(2,1)S(1)}, u32[]{:S(2)}, u32[]{:S(2)}) async-start(bf16[16,96,128]{2,1,0:T(8,128)(2,1)} %bitcast.7), calls=%async_computation.1 | async-start | bytes 786432 | tf_op jit(solution)/shard_map/all_to_all | solution.py:273
  36.0 0.1 copy.34.wr
  36.2 12.3 %all-to-all-done.1 = bf16[16,96,128]{2,1,0:T(8,128)(2,1)S(1)} async-done(((bf16[16,96,128]{2,1,0:T(8,128)(2,1)}), bf16[16,96,128]{2,1,0:T(8,128)(2,1)S(1)}, u32[]{:S(2)}, u32[]{:S(2)}) %all-to-all-start.1) | async-done | bytes 393248 | tf_op jit(solution)/shard_map/all_to_all | solution.py:273
  48.5 4.8 %middle.1 = (bf16[1536,128]{1,0:T(8,128)(2,1)}, f32[384,96]{1,0:T(8,128)S(1)}, f32[384,96]{1,0:T(8,128)S(1)}) custom-call(bf16[1536,128]{1,0:T(8,128)(2,1)S(1)} %bitcast.35, bf16[1536,128]{1,0:T(8,128)(2,1)S(1)} %bitcast.36, bf16[96,384]{1,0:T(8,128)(2,1)S(1)} %copy-done.2, bf16[384,96]{1,0:T(8,128)(2,1)S(1)} %copy.34.wr), custom_call_target="tpu_custom_call" | custom-call | flops 1000000000 | bytes 4000000 | tf_op jit(solution)/shard_map/middle/pallas_call | solution.py:250
  53.4 11.0 %all_to_all.40 = bf16[16,48,96]{2,1,0:T(8,128)(2,1)S(1)} all-to-all(bf16[16,48,96]{2,1,0:T(8,128)(2,1)S(1)} %pad_maximum_fusion), channel_id=1, replica_groups=mesh['zh'=2,'y'=8,'core'=2,'pen'=16] {'pen'}, dimensions={0} | all-to-all | bytes 294912 | tf_op jit(solution)/shard_map/all_to_all | solution.py:297
  64.3 3.6 %all-to-all-start.2 = ((bf16[16,96,128]{2,1,0:T(8,128)(2,1)}), bf16[16,96,128]{2,1,0:T(8,128)(2,1)S(1)}, u32[]{:S(2)}, u32[]{:S(2)}) async-start(bf16[16,96,128]{2,1,0:T(8,128)(2,1)} %bitcast.11), calls=%async_computation.2 | async-start | bytes 786432 | tf_op jit(solution)/shard_map/all_to_all | solution.py:273
  67.9 11.6 %all-to-all-done.2 = bf16[16,96,128]{2,1,0:T(8,128)(2,1)S(1)} async-done(((bf16[16,96,128]{2,1,0:T(8,128)(2,1)}), bf16[16,96,128]{2,1,0:T(8,128)(2,1)S(1)}, u32[]{:S(2)}, u32[]{:S(2)}) %all-to-all-start.2) | async-done | bytes 393248 | tf_op jit(solution)/shard_map/all_to_all | solution.py:273
  79.5 7.7 %conv_bwd.1 = (bf16[1536,128]{1,0:T(8,128)(2,1)}, f32[8,128]{1,0:T(8,128)S(1)}) custom-call(s32[3]{0:T(128)S(1)} %copy-done.3, bf16[1536,128]{1,0:T(8,128)(2,1)S(1)} %bitcast.34, f32[48,256]{1,0:T(8,128)S(1)} %bitcast.38, s32[256,256]{1,0:T(8,128)S(1)} %copy-done.4, f32[8,256]{1,0:T(8,128)S(1)} %copy-done.5, ...), custom_call_target="tpu_custom_call" | custom-call | flops 1000000000 | bytes 4000000 | tf_op jit(solution)/shard_map/conv_bwd/pallas_call | solution.py:235
  87.3 15.7 %all_to_all.41 = f32[8,56,128]{2,1,0:T(8,128)S(1)} all-to-all(f32[8,56,128]{2,1,0:T(8,128)S(1)} %broadcast_in_dim.6), channel_id=1, replica_groups=mesh['zh'=2,'y'=8,'core'=2,'pen'=16] {'y'}, dimensions={0} | all-to-all | bytes 458752 | tf_op jit(solution)/shard_map/all_to_all | solution.py:278
  103.1 19.0 %all_to_all.42 = f32[4,56,128]{2,1,0:T(8,128)S(1)} all-to-all(f32[4,56,128]{2,1,0:T(8,128)S(1)} %broadcast_in_dim.7), channel_id=1, replica_groups=mesh['zh'=2,'y'=8,'core'=2,'pen'=16] {'zh','core'}, dimensions={0} | all-to-all | bytes 229376 | tf_op jit(solution)/shard_map/all_to_all | solution.py:278
  122.1 9.9 %all_to_all.43 = f32[16,8,128]{2,1,0:T(8,128)S(1)} all-to-all(f32[16,8,128]{2,1,0:T(8,128)S(1)} %broadcast_in_dim.8), channel_id=1, replica_groups=mesh['zh'=2,'y'=8,'core'=2,'pen'=16] {'pen'}, dimensions={0} | all-to-all | bytes 131072 | tf_op jit(solution)/shard_map/all_to_all | solution.py:312
  132.1 3.6 %all-to-all-start.3 = ((bf16[16,96,128]{2,1,0:T(8,128)(2,1)}), bf16[16,96,128]{2,1,0:T(8,128)(2,1)S(1)}, u32[]{:S(2)}, u32[]{:S(2)}) async-start(bf16[16,96,128]{2,1,0:T(8,128)(2,1)} %bitcast.13), calls=%async_computation.3 | async-start | bytes 786432 | tf_op jit(solution)/shard_map/all_to_all | solution.py:273
  135.6 0.6 fusion.2
  136.2 0.1 reshape.79
  136.5 0.6 copy.37
  137.1 10.4 %all-to-all-done.3 = bf16[16,96,128]{2,1,0:T(8,128)(2,1)S(1)} async-done(((bf16[16,96,128]{2,1,0:T(8,128)(2,1)}), bf16[16,96,128]{2,1,0:T(8,128)(2,1)S(1)}, u32[]{:S(2)}, u32[]{:S(2)}) %all-to-all-start.3) | async-done | bytes 393248 | tf_op jit(solution)/shard_map/all_to_all | solution.py:273
  147.5 1.2 fusion.1
  (31 shorter events, 0.4 us)
Async XLA Ops:
  0.6 12.7 %copy-start = (f32[3,96,9]{1,0,2:T(4,128)S(1)}, f32[3,96,9]{1,0,2:T(4,128)}, u32[]{:S(2)}) copy-start(f32[3,96,9]{1,0,2:T(4,128)} %param.10) | copy-start | bytes 31108
  3.0 23.3 %all-to-all-start = ((bf16[16,96,128]{2,1,0:T(8,128)(2,1)}), bf16[16,96,128]{2,1,0:T(8,128)(2,1)S(1)}, u32[]{:S(2)}, u32[]{:S(2)}) async-start(bf16[16,96,128]{2,1,0:T(8,128)(2,1)} %bitcast.3), calls=%async_computation | async-start | bytes 786432 | tf_op jit(solution)/shard_map/all_to_all | solution.py:273
  13.5 12.8 %copy-start.4 = (s32[256,256]{1,0:T(8,128)S(1)}, s32[256,256]{1,0:T(8,128)}, u32[]{:S(2)}) copy-start(s32[256,256]{1,0:T(8,128)} %constant.19.clone.delta) | copy-start | bytes 786436
  26.2 0.7 copy-start.3
  32.3 3.7 %copy-start.6 = (bf16[384,96]{0,1:T(8,128)(2,1)S(1)}, bf16[384,96]{0,1:T(8,128)(2,1)}, u32[]{:S(2)}) copy-start(bf16[384,96]{0,1:T(8,128)(2,1)} %param.13) | copy-start | bytes 221188
  32.3 16.1 %copy-start.1 = (bf16[1,96,2,1024]{3,2,1,0:T(2,128)(2,1)S(1)}, bf16[1,96,2,1024]{3,2,1,0:T(2,128)(2,1)}, u32[]{:S(2)}) copy-start(bf16[1,96,2,1024]{3,2,1,0:T(2,128)(2,1)} %param.9) | copy-start | bytes 1179652
  32.3 16.1 %all-to-all-start.1 = ((bf16[16,96,128]{2,1,0:T(8,128)(2,1)}), bf16[16,96,128]{2,1,0:T(8,128)(2,1)S(1)}, u32[]{:S(2)}, u32[]{:S(2)}) async-start(bf16[16,96,128]{2,1,0:T(8,128)(2,1)} %bitcast.7), calls=%async_computation.1 | async-start | bytes 786432 | tf_op jit(solution)/shard_map/all_to_all | solution.py:273
  36.0 12.4 %copy-start.2 = (bf16[96,384]{1,0:T(8,128)(2,1)S(1)}, bf16[96,384]{1,0:T(8,128)(2,1)}, u32[]{:S(2)}) copy-start(bf16[96,384]{1,0:T(8,128)(2,1)} %we.1) | copy-start | bytes 221188
  64.3 15.2 %all-to-all-start.2 = ((bf16[16,96,128]{2,1,0:T(8,128)(2,1)}), bf16[16,96,128]{2,1,0:T(8,128)(2,1)S(1)}, u32[]{:S(2)}, u32[]{:S(2)}) async-start(bf16[16,96,128]{2,1,0:T(8,128)(2,1)} %bitcast.11), calls=%async_computation.2 | async-start | bytes 786432 | tf_op jit(solution)/shard_map/all_to_all | solution.py:273
  67.9 11.6 %copy-start.5 = (f32[8,256]{1,0:T(8,128)S(1)}, f32[8,256]{1,0:T(8,128)}, u32[]{:S(2)}) copy-start(f32[8,256]{1,0:T(8,128)} %constant.20.clone.table) | copy-start | bytes 24580
  132.1 15.4 %all-to-all-start.3 = ((bf16[16,96,128]{2,1,0:T(8,128)(2,1)}), bf16[16,96,128]{2,1,0:T(8,128)(2,1)S(1)}, u32[]{:S(2)}, u32[]{:S(2)}) async-start(bf16[16,96,128]{2,1,0:T(8,128)(2,1)} %bitcast.13), calls=%async_computation.3 | async-start | bytes 786432 | tf_op jit(solution)/shard_map/all_to_all | solution.py:273

commit v2 on v1

--- a/solution.py
+++ b/solution.py
@@ -17,6 +17,10 @@
 CH = C // GROUPS
 ROWS = C * L * L * 2 // 128
 STRIDE = 16
+PIECE = ROWS // GROUPS
+BH = H // GROUPS
+EXTRA_W = 2 * BH
+EXTRA_K = 16
 HALO = 16
 F32 = jnp.float32
 BF16 = jnp.bfloat16
@@ -112,9 +116,13 @@
 
 
 def conv_bwd(dil, d_ref, coef, delta, table, first_ref, second_ref, field_ref, hi_ref, lo_ref,
-             out_ref, kern_ref, stage, dmh, dse, dfi, acc_ref):
+             out_ref, weight_ref, stage, dmh, dse, dfi, acc_ref):
     d0, d1, d2 = dil[0], dil[1], dil[2]
-    stage[...] = d_ref[...].astype(F32)
+    weights = jnp.zeros((EXTRA_W, 128), F32)
+    for g in range(GROUPS):
+        stage[g * PIECE:(g + 1) * PIECE, :] = d_ref[g, 0:PIECE, :].astype(F32)
+        weights = weights + d_ref[g, PIECE:PIECE + EXTRA_W, :].astype(F32)
+    weight_ref[...] = weights
     acc_ref[...] = jnp.zeros_like(acc_ref)
     eye = jnp.where(delta[...] == 0, 1.0, 0.0).astype(BF16)
     gap = jnp.zeros((32, 128), F32)
@@ -160,22 +168,28 @@
         out = contract(hi, block, 1, 1) + contract(lo, block, 1, 1)
         for p in range(2):
             stage[pl.ds(2 * j + p, C, stride=STRIDE), :] = out[p * 128:p * 128 + C, :]
-    out_ref[...] = stage[...].astype(BF16)
     cross = contract(field_ref[...], dfi[...], 1, 0)
     for t in range(TAPS):
         keep = jnp.where(delta[...] == (((t - 4) * d0) & (L - 1)), cross, 0.0)
         acc_ref[t] = jnp.sum(keep.reshape(32, 8, 256), axis=0)
     sums = jnp.sum(acc_ref[...], axis=1)
-    kern_ref[...] = jnp.zeros_like(kern_ref)
-    kern_ref[:, 0:32] = lax.dot_general(
+    kern = lax.dot_general(
         table[...], sums, (((1,), (1,)), ((), ())),
         precision=lax.Precision.HIGHEST, preferred_element_type=F32)
+    lane = lax.broadcasted_iota(jnp.int32, (8, 128), 1)
+    kern = jnp.concatenate([kern] * 4, axis=1)
+    kern = jnp.where(lane // 32 == dil[3], kern, 0.0)
+    high = kern.astype(BF16).astype(F32)
+    extra = jnp.concatenate([high, kern - high], axis=0).astype(BF16)
+    for g in range(GROUPS):
+        out_ref[g, 0:PIECE, :] = stage[g * PIECE:(g + 1) * PIECE, :].astype(BF16)
+        out_ref[g, PIECE:PIECE + EXTRA_K, :] = extra
 
 
 BLOCK = 256
 
 
-def middle(m_ref, c_ref, we, wr, out_ref, expand_ref, reduce_ref, stage, stage_c, mix, cot):
+def middle(m_ref, c_ref, we, wr, out_ref, stage, stage_c, mix, cot, expand_ref, reduce_ref):
     stage[...] = m_ref[...].astype(F32)
     stage_c[...] = c_ref[...].astype(F32)
     for j in range(8):
@@ -204,7 +218,12 @@
         for i in range(BLOCK // 128):
             k = b * (BLOCK // 128) + i
             stage[pl.ds(k, C, stride=STRIDE), :] = out[:, i * 128:(i + 1) * 128]
-    out_ref[...] = stage[...].astype(BF16)
+    gap = jnp.zeros((EXTRA_W, 128 - C), F32)
+    for g in range(GROUPS):
+        own = slice(g * BH, (g + 1) * BH)
+        terms = jnp.concatenate([expand_ref[own, :], reduce_ref[own, :]], axis=0)
+        out_ref[g, 0:PIECE, :] = stage[g * PIECE:(g + 1) * PIECE, :].astype(BF16)
+        out_ref[g, PIECE:PIECE + EXTRA_W, :] = jnp.concatenate([terms, gap], axis=1).astype(BF16)
 
 
 VMEM = pl.BlockSpec(memory_space=pltpu.VMEM)
@@ -234,7 +253,7 @@
 def run_conv_bwd(dilations, rows, coef, delta, table, first, second, field, hi, lo):
     return pl.pallas_call(
         conv_bwd,
-        out_shape=(shape(ROWS, 128), shape(8, 128, dtype=F32)),
+        out_shape=(shape(GROUPS, PIECE + EXTRA_K, 128), shape(EXTRA_W, 128, dtype=F32)),
         in_specs=[SMEM] + [VMEM] * 9,
         out_specs=(VMEM,) * 2,
         scratch_shapes=[pltpu.VMEM((ROWS, 128), F32), pltpu.VMEM((L, L + 2 * HALO, 256), F32),
@@ -249,11 +268,12 @@
 def run_middle(rows, cot_rows, expand_weight, reduce_weight):
     return pl.pallas_call(
         middle,
-        out_shape=(shape(ROWS, 128), shape(H, C, dtype=F32), shape(H, C, dtype=F32)),
+        out_shape=shape(GROUPS, PIECE + EXTRA_W, 128),
         in_specs=[VMEM] * 4,
-        out_specs=(VMEM,) * 3,
+        out_specs=VMEM,
         scratch_shapes=[pltpu.VMEM((ROWS, 128), F32), pltpu.VMEM((ROWS, 128), F32),
-                        pltpu.VMEM((C, 2048), BF16), pltpu.VMEM((C, 2048), BF16)],
+                        pltpu.VMEM((C, 2048), BF16), pltpu.VMEM((C, 2048), BF16),
+                        pltpu.VMEM((H, C), F32), pltpu.VMEM((H, C), F32)],
         compiler_params=PARAMS,
         cost_estimate=pl.CostEstimate(flops=10**9, bytes_accessed=4 * 10**6, transcendentals=10**6),
         name="middle",
@@ -268,14 +288,23 @@
     return rows.reshape(C, 8, 2, 128).transpose(0, 2, 1, 3).reshape(1, C, 2, 1024)
 
 
-def swap(rows):
-    parts = rows.reshape(GROUPS, ROWS // GROUPS, 128)
-    return lax.all_to_all(parts, "pen", 0, 0, tiled=True).reshape(ROWS, 128)
-
-
-def sum_over(values, axes, size):
-    copies = jnp.broadcast_to(values[None], (size,) + values.shape)
-    return jnp.sum(lax.all_to_all(copies, axes, 0, 0, tiled=True), axis=0)
+def swap(parts):
+    return lax.all_to_all(parts, "pen", 0, 0, tiled=True)
+
+
+def sum_over_samples(terms):
+    half = terms.shape[0] // 2
+    zh, y = lax.axis_size("zh"), lax.axis_size("y")
+    cores = lax.axis_size("core")
+    if cores == 1:
+        parts = jnp.broadcast_to(terms.astype(BF16)[None], (zh * y,) + terms.shape)
+        return jnp.sum(lax.all_to_all(parts, SAMP, 0, 0, tiled=True).astype(F32), axis=0)
+    parts = terms.astype(BF16).reshape(1, 2, half, 128)
+    parts = jnp.broadcast_to(parts, (zh * y, 2, half, 128)).reshape(zh * y * 2, half, 128)
+    mine = jnp.sum(lax.all_to_all(parts, SAMP, 0, 0, tiled=True).astype(F32), axis=0)
+    other = lax.ppermute(mine, "core", [(0, 1), (1, 0)])
+    first = lax.axis_index("core") == 0
+    return jnp.concatenate([jnp.where(first, mine, other), jnp.where(first, other, mine)], axis=0)
 
 
 def per_device(activations, cotangent, depth_kernels, dilations, expand_weight, reduce_weight):
@@ -286,31 +315,29 @@
     coef = jnp.pad(coef, ((0, 0), (0, 16 - TAPS), (0, 128 - C)))
     coef = jnp.concatenate([coef, coef], axis=2).reshape(48, 256)
 
-    lines = swap(to_rows(activations))
-    mixed, first, second, field, hi, lo = run_conv_fwd(dilations, lines, coef, delta)
+    group = lax.axis_index("pen").astype(jnp.int32)
+    scalars = jnp.concatenate([dilations, jnp.mod(group, 4)[None]])
+    lines = swap(to_rows(activations).reshape(GROUPS, PIECE, 128)).reshape(ROWS, 128)
+    mixed, first, second, field, hi, lo = run_conv_fwd(scalars, lines, coef, delta)
     cot_rows = to_rows(cotangent)
-    d_mixed, part_expand, part_reduce = run_middle(
-        swap(mixed), cot_rows, expand_weight, reduce_weight)
-    d_lines = swap(d_mixed)
-    weights = jnp.concatenate(
-        [part_expand.reshape(GROUPS, 24, C), part_reduce.reshape(GROUPS, 24, C)], axis=1)
-    weights = lax.all_to_all(weights.astype(BF16), "pen", 0, 0, tiled=True)
-    weights = jnp.sum(weights.astype(F32), axis=0)
-    d_conv, kern = run_conv_bwd(
-        dilations, d_lines, coef, delta, table, first, second, field, hi, lo)
-    total = jnp.concatenate([jnp.pad(weights, ((0, 0), (0, 128 - C))), kern], axis=0)
-    total = sum_over(total, "y", lax.axis_size("y"))
-    total = sum_over(total, ("zh", "core"), lax.axis_size("zh") * lax.axis_size("core"))
-    d_input = swap(d_conv)
+    mixed = swap(mixed.reshape(GROUPS, PIECE, 128)).reshape(ROWS, 128)
+    d_lines = swap(run_middle(mixed, cot_rows, expand_weight, reduce_weight))
+    d_conv, weights = run_conv_bwd(
+        scalars, d_lines, coef, delta, table, first, second, field, hi, lo)
+    arrived = swap(d_conv)
+
+    kern = arrived[:, PIECE:, :].astype(F32).reshape(4, 4, 2, 8, 128)
+    kern = jnp.sum(kern, axis=(1, 2)).reshape(32, 128)
+    total = sum_over_samples(jnp.concatenate([weights, kern], axis=0))
+    d_input = arrived[:, :PIECE, :].reshape(ROWS, 128)
     grad_input = from_rows((cot_rows.astype(F32) + d_input.astype(F32)).astype(BF16))
 
     samples = lax.axis_size("zh") * lax.axis_size("y") * lax.axis_size("core")
     total = total * (1.0 / math.sqrt(samples * L * L * L))
-    own_expand = total[0:24, 0:C].T
-    own_reduce = total[24:48, 0:C]
-    kern = jnp.broadcast_to(total[None, 48:56, :], (GROUPS, 8, 128))
-    kern = lax.all_to_all(kern, "pen", 0, 0, tiled=True)
-    kern = kern[:, :CH, :3 * TAPS].reshape(C, 3, TAPS).transpose(1, 0, 2)
+    own_expand = total[0:BH, 0:C].T
+    own_reduce = total[BH:EXTRA_W, 0:C]
+    kern = total[EXTRA_W:].reshape(4, 8, 4, 32)[:, :CH, :, :3 * TAPS]
+    kern = kern.transpose(0, 2, 1, 3).reshape(C, 3, TAPS).transpose(1, 0, 2)
     return grad_input, own_expand, own_reduce, kern
 
 

time: 149 us -> 139 us (0.933)
  blocking collectives: 55.6 us -> 20.4 us
  starting transfers between devices: 21.2 us -> 36.2 us
  waiting for transfers between devices: 46.8 us -> 55.2 us
  local copies, waits for them, and re-layouts: 4.88 us -> 6.64 us
    all_to_all x4 -> x1, blocking collectives: 55.6 us -> 20.4 us  [swap(): return lax.all_to_all(parts, 'pen', 0, 0, tiled=True)]
    all_to_all x4, starting transfers between devices: 21.2 us -> 32.5 us  [the longest x3 17.7 us: swap(): return lax.all_to_all(parts, 'pen', 0, 0, tiled=True)]
    all_to_all x4, waiting for transfers between devices: 46.8 us -> 55.2 us  [the longest x3 38.4 us: swap(): return lax.all_to_all(parts, 'pen', 0, 0, tiled=True)]
    ppermute x0 -> x1, starting transfers between devices: none -> 3.71 us  [sum_over_samples(): other = lax.ppermute(mine, 'core', [(0, 1), (1, 0)])]
  transfers between devices with their start and end apart: 4 -> 5, of which waited for: 4 -> 4; matrix products, arithmetic and copies ran while one was open for 1% -> 1% of each run, Pallas kernels for 0% -> 0%
where the time goes in v2:
time: 139 us; the launch traced here: 138 us
  waiting for transfers between devices  55.2 us (40%)
  starting transfers between devices  36.2 us (26%)
  blocking collectives  20.4 us (15%)
  Pallas kernels  17.5 us (13%)
  local copies, waits for them, and re-layouts  6.64 us (5%)
    all_to_all x3, waiting for transfers between devices, swap(): return lax.all_to_all(parts, 'pen', 0, 0, tiled=True)  38.4 us
    all_to_all x1, blocking collectives, swap(): return lax.all_to_all(parts, 'pen', 0, 0, tiled=True)  20.4 us
    all_to_all x3, starting transfers between devices, swap(): return lax.all_to_all(parts, 'pen', 0, 0, tiled=True)  17.7 us
    all_to_all x1, waiting for transfers between devices, sum_over_samples(): lax.all_to_all(parts, SAMP, 0, 0, tiled=True).astype(F32)  16.8 us
    all_to_all x1, starting transfers between devices, sum_over_samples(): lax.all_to_all(parts, SAMP, 0, 0, tiled=True).astype(F32)  14.8 us
    pallas_call x1, Pallas kernels, run_conv_bwd(): pl.pallas_call(conv_bwd, out_shape=(shape(GROUPS, PIECE + EXTRA_K, 128),...  8.07 us
    pallas_call x1, Pallas kernels, run_conv_fwd(): pl.pallas_call(conv_fwd, out_shape=(shape(ROWS, 128), shape(1024, 256), s...  5.34 us
    pallas_call x1, Pallas kernels, run_middle(): pl.pallas_call(middle, out_shape=shape(GROUPS, PIECE + EXTRA_W, 128), in_...  4.1 us
  transfers between devices with their start and end apart: 5, of which 4 were waited for; matrix products, arithmetic and copies ran while one was open for 1% of the time, Pallas kernels for 0%

profile of v2, /device:TPU:1, one launch (start us, length us, event | category | flops | bytes accessed | tf_op | source)
XLA Modules:
  0.0 138.2 jit_solution(1373933868720819112)
XLA Ops:
  0.6 1.3 reshape.68
  1.9 1.1 copy.25
  3.0 10.4 %all-to-all-start = ((bf16[16,96,128]{2,1,0:T(8,128)(2,1)}), bf16[16,96,128]{2,1,0:T(8,128)(2,1)S(1)}, u32[]{:S(2)}, u32[]{:S(2)}) async-start(bf16[16,96,128]{2,1,0:T(8,128)(2,1)} %bitcast.4), calls=%async_computation | async-start | bytes 786432 | tf_op jit(solution)/shard_map/all_to_all | solution.py:292
  13.5 0.1 tile.10
  13.7 0.6 copy-done.6
  14.4 11.8 %all-to-all-done = bf16[16,96,128]{2,1,0:T(8,128)(2,1)S(1)} async-done(((bf16[16,96,128]{2,1,0:T(8,128)(2,1)}), bf16[16,96,128]{2,1,0:T(8,128)(2,1)S(1)}, u32[]{:S(2)}, u32[]{:S(2)}) %all-to-all-start) | async-done | bytes 393248 | tf_op jit(solution)/shard_map/all_to_all | solution.py:292
  26.3 5.3 %conv_fwd.1 = (bf16[1536,128]{1,0:T(8,128)(2,1)}, bf16[1024,256]{1,0:T(8,128)(2,1)S(1)}, bf16[1024,256]{1,0:T(8,128)(2,1)S(1)}, bf16[256,1024]{1,0:T(8,128)(2,1)...) custom-call(s32[4]{0:T(128)S(1)} %pad_add_fusion.dil, bf16[1536,128]{1,0:T(8,128)(2,1)S(1)} %bitcast.35, ...), custom_call_target="tpu_custom_call" | custom-call | flops 1000000000 | bytes 4000000 | tf_op jit(solution)/shard_map/conv_fwd/pallas_call | solution.py:239
  31.6 3.7 %all-to-all-start.1 = ((bf16[16,96,128]{2,1,0:T(8,128)(2,1)}), bf16[16,96,128]{2,1,0:T(8,128)(2,1)S(1)}, u32[]{:S(2)}, u32[]{:S(2)}) async-start(bf16[16,96,128]{2,1,0:T(8,128)(2,1)} %bitcast.8), calls=%async_computation.1 | async-start | bytes 786432 | tf_op jit(solution)/shard_map/all_to_all | solution.py:292
  35.4 12.3 %all-to-all-done.1 = bf16[16,96,128]{2,1,0:T(8,128)(2,1)S(1)} async-done(((bf16[16,96,128]{2,1,0:T(8,128)(2,1)}), bf16[16,96,128]{2,1,0:T(8,128)(2,1)S(1)}, u32[]{:S(2)}, u32[]{:S(2)}) %all-to-all-start.1) | async-done | bytes 393248 | tf_op jit(solution)/shard_map/all_to_all | solution.py:292
  47.7 4.1 %middle.1 = bf16[16,144,128]{2,1,0:T(8,128)(2,1)S(1)} custom-call(bf16[1536,128]{1,0:T(8,128)(2,1)S(1)} %bitcast.36, bf16[1536,128]{1,0:T(8,128)(2,1)S(1)} %bitcast.37, bf16[96,384]{1,0:T(8,128)(2,1)S(1)} %copy-done.2, bf16[384,96]{1,0:T(8,128)(2,1)S(1)} %copy.27.wr), custom_call_target="tpu_custom_call" | custom-call | flops 1000000000 | bytes 4000000 | tf_op jit(solution)/shard_map/middle/pallas_call | solution.py:269
  51.8 20.4 %all_to_all.25.d_ref = bf16[16,144,128]{2,1,0:T(8,128)(2,1)S(1)} all-to-all(bf16[16,144,128]{2,1,0:T(8,128)(2,1)S(1)} %middle.1), channel_id=1, replica_groups=mesh['zh'=2,'y'=8,'core'=2,'pen'=16] {'pen'}, dimensions={0} | all-to-all | bytes 1179648 | tf_op jit(solution)/shard_map/all_to_all | solution.py:292
  72.3 0.7 copy-done.4
  73.0 8.1 %conv_bwd.1 = (bf16[16,112,128]{2,1,0:T(8,128)(2,1)}, f32[48,128]{1,0:T(8,128)S(1)}) custom-call(s32[4]{0:T(128)S(1)} %pad_add_fusion.dil, bf16[16,144,128]{2,1,0:T(8,128)(2,1)S(1)} %all_to_all.25.d_ref, f32[48,256]{1,0:T(8,128)S(1)} %bitcast.39, s32[256,256]{1,0:T(8,128)S(1)} %copy-done.3, f32[8,256]{1,0:T(8,128)S(1)} %copy-done.4, ...), custom_call_target="tpu_custom_call" | custom-call | flops 1000000000 | bytes 4000000 | tf_op jit(solution)/shard_map/conv_bwd/pallas_call | solution.py:254
  81.1 3.7 %all-to-all-start.3 = ((bf16[16,112,128]{2,1,0:T(8,128)(2,1)}), bf16[16,112,128]{2,1,0:T(8,128)(2,1)S(1)}, u32[]{:S(2)}, u32[]{:S(2)}) async-start(bf16[16,112,128]{2,1,0:T(8,128)(2,1)} %get-tuple-element.18), calls=%async_computation.3 | async-start | bytes 917504 | tf_op jit(solution)/shard_map/all_to_all | solution.py:292
  84.7 14.3 %all-to-all-done.3 = bf16[16,112,128]{2,1,0:T(8,128)(2,1)S(1)} async-done(((bf16[16,112,128]{2,1,0:T(8,128)(2,1)}), bf16[16,112,128]{2,1,0:T(8,128)(2,1)S(1)}, u32[]{:S(2)}, u32[]{:S(2)}) %all-to-all-start.3) | async-done | bytes 458784 | tf_op jit(solution)/shard_map/all_to_all | solution.py:292
  99.1 0.8 broadcast_in_dim.9
  99.8 14.8 %all-to-all-start.4 = ((bf16[32,40,128]{2,1,0:T(8,128)(2,1)}), bf16[32,40,128]{2,1,0:T(8,128)(2,1)S(1)}, u32[]{:S(2)}, u32[]{:S(2)}) async-start(bf16[32,40,128]{2,1,0:T(8,128)(2,1)} %bitcast.18), calls=%async_computation.4 | async-start | bytes 655360 | tf_op jit(solution)/shard_map/all_to_all | solution.py:304
  114.6 16.8 %all-to-all-done.4 = bf16[32,40,128]{2,1,0:T(8,128)(2,1)S(1)} async-done(((bf16[32,40,128]{2,1,0:T(8,128)(2,1)}), bf16[32,40,128]{2,1,0:T(8,128)(2,1)S(1)}, u32[]{:S(2)}, u32[]{:S(2)}) %all-to-all-start.4) | async-done | bytes 327712 | tf_op jit(solution)/shard_map/all_to_all | solution.py:304
  131.5 3.7 %collective-permute-start = (f32[40,128]{1,0:T(8,128)S(1)}, f32[40,128]{1,0:T(8,128)S(1)}, u32[]{:S(2)}, u32[]{:S(2)}) collective-permute-start(f32[40,128]{1,0:T(8,128)S(1)} %convert_reduce_fusion), channel_id=1, source_target_pairs={{0,16},{16,0},{1,17},{17,1},{2,18},{18,2},{3,19},{19,3},{4,20},{20... | collective-permute-start | bytes 61448 | tf_op jit(solution)/shard_map/ppermute | solution.py:305
  135.2 1.2 fusion.1
  136.4 0.6 fusion.2
  137.2 0.2 copy.31
  137.4 0.2 reshape.80
  137.6 0.6 copy.30
  (31 shorter events, 0.6 us)
Async XLA Ops:
  0.6 12.7 %copy-start = (f32[3,96,9]{1,0,2:T(4,128)S(1)}, f32[3,96,9]{1,0,2:T(4,128)}, u32[]{:S(2)}) copy-start(f32[3,96,9]{1,0,2:T(4,128)} %param.10) | copy-start | bytes 31108
  3.0 23.3 %all-to-all-start = ((bf16[16,96,128]{2,1,0:T(8,128)(2,1)}), bf16[16,96,128]{2,1,0:T(8,128)(2,1)S(1)}, u32[]{:S(2)}, u32[]{:S(2)}) async-start(bf16[16,96,128]{2,1,0:T(8,128)(2,1)} %bitcast.4), calls=%async_computation | async-start | bytes 786432 | tf_op jit(solution)/shard_map/all_to_all | solution.py:292
  13.5 12.8 %copy-start.3 = (s32[256,256]{1,0:T(8,128)S(1)}, s32[256,256]{1,0:T(8,128)}, u32[]{:S(2)}) copy-start(s32[256,256]{1,0:T(8,128)} %constant.36.clone.delta) | copy-start | bytes 786436
  13.7 0.7 copy-start.6
  31.6 3.7 %copy-start.5 = (bf16[384,96]{0,1:T(8,128)(2,1)S(1)}, bf16[384,96]{0,1:T(8,128)(2,1)}, u32[]{:S(2)}) copy-start(bf16[384,96]{0,1:T(8,128)(2,1)} %param.13) | copy-start | bytes 221188
  31.6 16.1 %copy-start.1 = (bf16[1,96,2,1024]{3,2,1,0:T(2,128)(2,1)S(1)}, bf16[1,96,2,1024]{3,2,1,0:T(2,128)(2,1)}, u32[]{:S(2)}) copy-start(bf16[1,96,2,1024]{3,2,1,0:T(2,128)(2,1)} %param.9) | copy-start | bytes 1179652
  31.6 16.1 %all-to-all-start.1 = ((bf16[16,96,128]{2,1,0:T(8,128)(2,1)}), bf16[16,96,128]{2,1,0:T(8,128)(2,1)S(1)}, u32[]{:S(2)}, u32[]{:S(2)}) async-start(bf16[16,96,128]{2,1,0:T(8,128)(2,1)} %bitcast.8), calls=%async_computation.1 | async-start | bytes 786432 | tf_op jit(solution)/shard_map/all_to_all | solution.py:292
  35.3 12.4 %copy-start.2 = (bf16[96,384]{1,0:T(8,128)(2,1)S(1)}, bf16[96,384]{1,0:T(8,128)(2,1)}, u32[]{:S(2)}) copy-start(bf16[96,384]{1,0:T(8,128)(2,1)} %we.1) | copy-start | bytes 221188
  72.3 0.7 copy-start.4
  81.1 18.0 %all-to-all-start.3 = ((bf16[16,112,128]{2,1,0:T(8,128)(2,1)}), bf16[16,112,128]{2,1,0:T(8,128)(2,1)S(1)}, u32[]{:S(2)}, u32[]{:S(2)}) async-start(bf16[16,112,128]{2,1,0:T(8,128)(2,1)} %get-tuple-element.18), calls=%async_computation.3 | async-start | bytes 917504 | tf_op jit(solution)/shard_map/all_to_all | solution.py:292
  99.8 31.6 %all-to-all-start.4 = ((bf16[32,40,128]{2,1,0:T(8,128)(2,1)}), bf16[32,40,128]{2,1,0:T(8,128)(2,1)S(1)}, u32[]{:S(2)}, u32[]{:S(2)}) async-start(bf16[32,40,128]{2,1,0:T(8,128)(2,1)} %bitcast.18), calls=%async_computation.4 | async-start | bytes 655360 | tf_op jit(solution)/shard_map/all_to_all | solution.py:304
  131.5 4.9 %collective-permute-start = (f32[40,128]{1,0:T(8,128)S(1)}, f32[40,128]{1,0:T(8,128)S(1)}, u32[]{:S(2)}, u32[]{:S(2)}) collective-permute-start(f32[40,128]{1,0:T(8,128)S(1)} %convert_reduce_fusion), channel_id=1, source_target_pairs={{0,16},{16,0},{1,17},{17,1},{2,18},{18,2},{3,19},{19,3},{4,20},{20... | collective-permute-start | bytes 61448 | tf_op jit(solution)/shard_map/ppermute | solution.py:305

commit v3 on v2

v3 whole, which is shorter than its diff:
```python
import math

import jax
import jax.numpy as jnp
import numpy as np
from jax import lax
from jax.experimental import pallas as pl
from jax.experimental.pallas import tpu as pltpu
from jax.sharding import Mesh
from jax.sharding import PartitionSpec as P

C = 96
H = 384
L = 32
TAPS = 9
GROUPS = 16
CH = C // GROUPS
ROWS = C * L * L * 2 // 128
STRIDE = 16
PIECE = ROWS // GROUPS
BH = H // GROUPS
EXTRA_W = 2 * BH
HALO = 16
F32 = jnp.float32
BF16 = jnp.bfloat16
SAMP = ("zh", "y", "core")


def delta_table():
    r = np.arange(256)
    plane, rest = r // 128, r % 128
    x, c = 2 * (rest // CH) + plane, rest % CH
    valid = rest < C
    delta = (x[:, None] - x[None, :]) % L
    same = (c[:, None] == c[None, :]) & valid[:, None] & valid[None, :]
    return np.where(same, delta, -1).astype(np.int32)


def channel_table():
    r = np.arange(128)
    out = np.zeros((8, 128), np.float32)
    for c in range(CH):
        out[c] = (r % CH == c) & (r < C)
    return out


def contract(a, b, da, db):
    return lax.dot_general(a, b, (((da,), (db,)), ((), ())), preferred_element_type=F32)


def pieces(stage, j, p):
    return stage[pl.ds(2 * j + p, C, stride=STRIDE), :]


def spread(coef, base):
    return [jnp.broadcast_to(coef[base + t:base + t + 1, :], (8, 128)) for t in range(TAPS)]


def tiles(v):
    return v.reshape(4, 8, 128)


def load_field(stage, j):
    gap = jnp.zeros((128 - C, 128), F32)
    parts = []
    for p in range(2):
        parts += [pieces(stage, j, p), gap]
    return jnp.concatenate(parts, axis=0).astype(BF16)


def put_halo(ref, p, y, v):
    ref[p, y, HALO:HALO + L, :] = v
    ref[p, y, 0:HALO, :] = v[L - HALO:, :]
    ref[p, y, HALO + L:, :] = v[:HALO, :]


def conv_fwd(dil, a_ref, coef, delta, wide, mixed_ref, first_ref, second_ref, field_ref, hi_ref,
             lo_ref, stage, fir, sec, mix):
    d0, d1, d2 = dil[0], dil[1], dil[2]
    stage[...] = a_ref[...].astype(F32)
    m = jnp.zeros((256, 256), F32)
    for t in range(TAPS):
        m = m + jnp.where(delta[...] == (((t - 4) * d0) & (L - 1)), wide[t:t + 1, :], 0.0)
    hi = m.astype(BF16)
    lo = (m - hi.astype(F32)).astype(BF16)
    hi_ref[...] = hi
    lo_ref[...] = lo
    eye = jnp.where(delta[...] == 0, 1.0, 0.0).astype(BF16)
    for j in range(8):
        f = load_field(stage, j)
        field_ref[:, j * 128:(j + 1) * 128] = f
        out = (contract(f, hi, 0, 0) + contract(f, lo, 0, 0)).astype(BF16)
        for p in range(2):
            half = out[:, p * 128:(p + 1) * 128]
            first_ref[p, j * 128:(j + 1) * 128, :] = half
            fir[p, 4 * j:4 * j + 4] = half.astype(F32).reshape(4, L, 128)

    taps = spread(coef, 16)

    @pl.loop(0, L)
    def _(y):
        row = pl.ds(pl.multiple_of(y * L, L), L)
        for p in range(2):
            acc = jnp.zeros((4, 8, 128), F32)
            for t in range(TAPS):
                acc = acc + taps[t] * tiles(fir[p, (y + (t - 4) * d1) & (L - 1)])
            acc = acc.reshape(L, 128).astype(BF16)
            second_ref[p, row, :] = acc
            put_halo(sec, p, y, acc.astype(F32))

    taps_z = spread(coef, 32)

    @pl.loop(0, L)
    def _(y):
        row = pl.ds(pl.multiple_of(y * L, L), L)
        for p in range(2):
            acc = jnp.zeros((4, 8, 128), F32)
            for t in range(TAPS):
                acc = acc + taps_z[t] * tiles(sec[p, y, pl.ds(HALO + (t - 4) * d2, L), :])
            mix[row, p * 128:(p + 1) * 128] = acc.reshape(L, 128).astype(BF16)

    for j in range(8):
        turned = contract(eye, mix[j * 128:(j + 1) * 128, :], 1, 1)
        for p in range(2):
            stage[pl.ds(2 * j + p, C, stride=STRIDE), :] = turned[p * 128:p * 128 + C, :]
    mixed_ref[...] = stage[...].astype(BF16)


def conv_bwd(dil, d_ref, coef, delta, table, first_ref, second_ref, field_ref, hi_ref, lo_ref,
             out_ref, sums_ref, stage, dmh, dse, dfi, acc_ref):
    d0, d1, d2 = dil[0], dil[1], dil[2]
    weights = jnp.zeros((EXTRA_W, 128), F32)
    for g in range(GROUPS):
        stage[g * PIECE:(g + 1) * PIECE, :] = d_ref[g, 0:PIECE, :].astype(F32)
        weights = weights + d_ref[g, PIECE:PIECE + EXTRA_W, :].astype(F32)
    sums_ref[0:EXTRA_W, :] = weights
    eye = jnp.where(delta[...] == 0, 1.0, 0.0).astype(BF16)
    for j in range(8):
        out = contract(load_field(stage, j), eye, 0, 0)
        for p in range(2):
            for i in range(4):
                put_halo(dmh, p, 4 * j + i, out[i * L:(i + 1) * L, p * 128:(p + 1) * 128])

    def fold(v):
        return (v[0] + v[1]) + (v[2] + v[3])

    taps_z = spread(coef, 32)
    empty = (jnp.zeros((8, 128), F32),) * TAPS

    def along_z(y, sums):
        row = pl.ds(pl.multiple_of(y * L, L), L)
        sums = list(sums)
        for p in range(2):
            field = tiles(second_ref[p, row, :].astype(F32))
            acc = jnp.zeros((4, 8, 128), F32)
            for t in range(TAPS):
                moved = tiles(dmh[p, y, pl.ds(HALO - (t - 4) * d2, L), :])
                acc = acc + taps_z[t] * moved
                sums[t] = sums[t] + fold(moved * field)
            dse[p, y] = acc.reshape(L, 128).astype(BF16).astype(F32)
        return tuple(sums)

    sums = lax.fori_loop(0, L, along_z, empty)
    for t in range(TAPS):
        acc_ref[18 + t] = sums[t]
    taps = spread(coef, 16)

    def along_y(y, sums):
        row = pl.ds(pl.multiple_of(y * L, L), L)
        sums = list(sums)
        for p in range(2):
            field = tiles(first_ref[p, row, :].astype(F32))
            acc = jnp.zeros((4, 8, 128), F32)
            for t in range(TAPS):
                moved = tiles(dse[p, (y - (t - 4) * d1) & (L - 1)])
                acc = acc + taps[t] * moved
                sums[t] = sums[t] + fold(moved * field)
            dfi[row, p * 128:(p + 1) * 128] = acc.reshape(L, 128).astype(BF16)
        return tuple(sums)

    sums = lax.fori_loop(0, L, along_y, empty)
    for t in range(TAPS):
        acc_ref[9 + t] = sums[t]
    for t in range(27, 32):
        acc_ref[t] = jnp.zeros((8, 128), F32)

    hi, lo = hi_ref[...], lo_ref[...]
    for j in range(8):
        block = dfi[j * 128:(j + 1) * 128, :]
        out = contract(hi, block, 1, 1) + contract(lo, block, 1, 1)
        for p in range(2):
            stage[pl.ds(2 * j + p, C, stride=STRIDE), :] = out[p * 128:p * 128 + C, :]
    cross = contract(field_ref[...], dfi[...], 1, 0)
    for t in range(TAPS):
        keep = jnp.where(delta[...] == (((t - 4) * d0) & (L - 1)), cross, 0.0)
        keep = jnp.sum(keep.reshape(32, 8, 256), axis=0)
        acc_ref[t] = keep[:, :128] + keep[:, 128:]
    sums_ref[EXTRA_W:EXTRA_W + 8, :] = jnp.zeros((8, 128), F32)
    sums_ref[EXTRA_W:EXTRA_W + 8, 0:32] = lax.dot_general(
        table[...], jnp.sum(acc_ref[...], axis=1), (((1,), (1,)), ((), ())),
        precision=lax.Precision.HIGHEST, preferred_element_type=F32)
    out_ref[...] = stage[...].astype(BF16)


BLOCK = 256


def middle(m_ref, c_ref, we, wr, out_ref, stage, stage_c, mix, cot, expand_ref, reduce_ref):
    stage[...] = m_ref[...].astype(F32)
    stage_c[...] = c_ref[...].astype(F32)
    for j in range(8):
        for p in range(2):
            k = 2 * j + p
            mix[:, k * 128:(k + 1) * 128] = pieces(stage, j, p).astype(BF16)
            cot[:, k * 128:(k + 1) * 128] = pieces(stage_c, j, p).astype(BF16)
    expand_ref[...] = jnp.zeros_like(expand_ref)
    reduce_ref[...] = jnp.zeros_like(reduce_ref)
    root = math.sqrt(2.0 / math.pi)

    for b in range(2 * L * L // BLOCK):
        cols = slice(b * BLOCK, (b + 1) * BLOCK)
        mb, cb = mix[:, cols], cot[:, cols]
        pre = contract(we[...], mb, 0, 0)
        d_hidden = contract(wr[...], cb, 1, 0)
        square = pre * pre
        inner = root * pre * (1.0 + 0.044715 * square)
        half = 0.5 + 0.5 * jnp.tanh(inner)
        hidden = (pre * half).astype(BF16)
        slope = half + pre * (2.0 * half * (1.0 - half)) * (root * (1.0 + 3.0 * 0.044715 * square))
        d_pre = (d_hidden * slope).astype(BF16)
        reduce_ref[...] += contract(hidden, cb, 1, 1)
        expand_ref[...] += contract(d_pre, mb, 1, 1)
        out = contract(we[...], d_pre, 1, 0)
        for i in range(BLOCK // 128):
            k = b * (BLOCK // 128) + i
            stage[pl.ds(k, C, stride=STRIDE), :] = out[:, i * 128:(i + 1) * 128]
    gap = jnp.zeros((EXTRA_W, 128 - C), F32)
    for g in range(GROUPS):
        own = slice(g * BH, (g + 1) * BH)
        terms = jnp.concatenate([expand_ref[own, :], reduce_ref[own, :]], axis=0)
        out_ref[g, 0:PIECE, :] = stage[g * PIECE:(g + 1) * PIECE, :].astype(BF16)
        out_ref[g, PIECE:PIECE + EXTRA_W, :] = jnp.concatenate([terms, gap], axis=1).astype(BF16)


VMEM = pl.BlockSpec(memory_space=pltpu.VMEM)
SMEM = pl.BlockSpec(memory_space=pltpu.SMEM)
PARAMS = pltpu.CompilerParams(vmem_limit_bytes=28 * 1024 * 1024)


def shape(*dims, dtype=BF16):
    return jax.ShapeDtypeStruct(dims, dtype)


def run_conv_fwd(dilations, rows, coef, delta, wide):
    return pl.pallas_call(
        conv_fwd,
        out_shape=(shape(ROWS, 128), shape(2, 1024, 128), shape(2, 1024, 128), shape(256, 1024),
                   shape(256, 256), shape(256, 256)),
        in_specs=[SMEM] + [VMEM] * 4,
        out_specs=(VMEM,) * 6,
        scratch_shapes=[pltpu.VMEM((ROWS, 128), F32), pltpu.VMEM((2, L, L, 128), F32),
                        pltpu.VMEM((2, L, L + 2 * HALO, 128), F32), pltpu.VMEM((1024, 256), BF16)],
        compiler_params=PARAMS,
        cost_estimate=pl.CostEstimate(flops=10**9, bytes_accessed=4 * 10**6, transcendentals=0),
        name="conv_fwd",
    )(dilations, rows, coef, delta, wide)


def run_conv_bwd(dilations, rows, coef, delta, table, first, second, field, hi, lo):
    return pl.pallas_call(
        conv_bwd,
        out_shape=(shape(ROWS, 128), shape(EXTRA_W + 8, 128, dtype=F32)),
        in_specs=[SMEM] + [VMEM] * 9,
        out_specs=(VMEM,) * 2,
        scratch_shapes=[pltpu.VMEM((ROWS, 128), F32),
                        pltpu.VMEM((2, L, L + 2 * HALO, 128), F32),
                        pltpu.VMEM((2, L, L, 128), F32), pltpu.VMEM((1024, 256), BF16),
                        pltpu.VMEM((32, 8, 128), F32)],
        compiler_params=PARAMS,
        cost_estimate=pl.CostEstimate(flops=10**9, bytes_accessed=4 * 10**6, transcendentals=0),
        name="conv_bwd",
    )(dilations, rows, coef, delta, table, first, second, field, hi, lo)


def run_middle(rows, cot_rows, expand_weight, reduce_weight):
    return pl.pallas_call(
        middle,
        out_shape=shape(GROUPS, PIECE + EXTRA_W, 128),
        in_specs=[VMEM] * 4,
        out_specs=VMEM,
        scratch_shapes=[pltpu.VMEM((ROWS, 128), F32), pltpu.VMEM((ROWS, 128), F32),
                        pltpu.VMEM((C, 2048), BF16), pltpu.VMEM((C, 2048), BF16),
                        pltpu.VMEM((H, C), F32), pltpu.VMEM((H, C), F32)],
        compiler_params=PARAMS,
        cost_estimate=pl.CostEstimate(flops=10**9, bytes_accessed=4 * 10**6, transcendentals=10**6),
        name="middle",
    )(rows, cot_rows, expand_weight, reduce_weight)


def to_rows(field):
    return field.reshape(C, 2, 8, 128).transpose(0, 2, 1, 3).reshape(ROWS, 128)


def from_rows(rows):
    return rows.reshape(C, 8, 2, 128).transpose(0, 2, 1, 3).reshape(1, C, 2, 1024)


def swap(parts):
    return lax.all_to_all(parts, "pen", 0, 0, tiled=True)


def sum_over_partners(terms):
    total = terms
    if lax.axis_size("zh") == 2:
        flips = [[(0, 2), (1, 3), (2, 0), (3, 1)], [(0, 3), (1, 2), (2, 1), (3, 0)],
                 [(0, 1), (1, 0), (2, 3), (3, 2)]]
        for flip in flips:
            total = total + lax.ppermute(terms, ("zh", "core"), flip)
    return total


def sum_over_y(terms):
    size = lax.axis_size("y")
    parts = jnp.broadcast_to(terms.astype(BF16)[None], (size,) + terms.shape)
    return jnp.sum(lax.all_to_all(parts, "y", 0, 0, tiled=True).astype(F32), axis=0)


def per_device(activations, cotangent, depth_kernels, dilations, expand_weight, reduce_weight):
    delta = jnp.asarray(delta_table())
    table = jnp.asarray(channel_table())
    own = lax.dynamic_slice_in_dim(depth_kernels, lax.axis_index("pen") * CH, CH, 1)
    coef = jnp.tile(own.transpose(0, 2, 1), (1, 1, GROUPS))
    coef = jnp.pad(coef, ((0, 0), (0, 16 - TAPS), (0, 128 - C))).reshape(48, 128)
    wide = jnp.concatenate([coef[0:16], coef[0:16]], axis=1)

    lines = swap(to_rows(activations).reshape(GROUPS, PIECE, 128)).reshape(ROWS, 128)
    mixed, first, second, field, hi, lo = run_conv_fwd(dilations, lines, coef, delta, wide)
    cot_rows = to_rows(cotangent)
    mixed = swap(mixed.reshape(GROUPS, PIECE, 128)).reshape(ROWS, 128)
    d_lines = swap(run_middle(mixed, cot_rows, expand_weight, reduce_weight))
    d_conv, sums = run_conv_bwd(
        dilations, d_lines, coef, delta, table, first, second, field, hi, lo)
    d_input = swap(d_conv.reshape(GROUPS, PIECE, 128)).reshape(ROWS, 128)
    sums = sum_over_partners(sums)
    sums, d_input = lax.optimization_barrier((sums, d_input))
    sums = sum_over_y(sums)
    grad_input = from_rows((cot_rows.astype(F32) + d_input.astype(F32)).astype(BF16))

    samples = lax.axis_size("zh") * lax.axis_size("y") * lax.axis_size("core")
    sums = sums * (1.0 / math.sqrt(samples * L * L * L))
    kern = jnp.broadcast_to(sums[None, EXTRA_W:, :], (GROUPS, 8, 128))
    kern = swap(kern)[:, :CH, :3 * TAPS].reshape(C, 3, TAPS).transpose(1, 0, 2)
    own_expand = sums[0:BH, 0:C].T
    own_reduce = sums[BH:EXTRA_W, 0:C]
    return grad_input, own_expand, own_reduce, kern


def solution(mesh):
    samp = mesh.devices.shape[0]
    split = (2, samp // 4, 2) if samp % 4 == 0 else (1, samp, 1)
    fine = Mesh(mesh.devices.reshape(*split, GROUPS), (*SAMP, "pen"))
    field = P(SAMP, None, "pen", None)
    return jax.shard_map(
        per_device,
        mesh=fine,
        in_specs=(field, field, P(), P(), P(), P()),
        out_specs=(field, P(None, "pen"), P("pen", None), P()),
        check_vma=False,
    )
```

time: 139 us -> 137 us (0.986); the launches traced: 138 us -> 134 us
  waiting for transfers between devices: 55.2 us -> 44.8 us
  starting transfers between devices: 36.2 us -> 45.2 us
  Pallas kernels: 17.5 us -> 14.9 us
    all_to_all x1, waiting for transfers between devices: 16.8 us -> 7.01 us  [sum_over_y(): lax.all_to_all(parts, 'y', 0, 0, tiled=True).astype(F32)]
    ppermute x1 -> x3, starting transfers between devices: 3.71 us -> 13.4 us  [sum_over_partners(): total = total + lax.ppermute(terms, ('zh', 'core'), flip)]
    all_to_all x1, starting transfers between devices: 14.8 us -> 6.82 us  [sum_over_y(): lax.all_to_all(parts, 'y', 0, 0, tiled=True).astype(F32)]
    all_to_all x3 -> x4, starting transfers between devices: 17.7 us -> 24.9 us  [swap(): return lax.all_to_all(parts, 'pen', 0, 0, tiled=True)]
    all_to_all x3 -> x4, waiting for transfers between devices: 38.4 us -> 31.3 us  [swap(): return lax.all_to_all(parts, 'pen', 0, 0, tiled=True)]
    ppermute x1 -> x3, waiting for transfers between devices: 0.01 us -> 6.49 us  [sum_over_partners(): total = total + lax.ppermute(terms, ('zh', 'core'), flip)]
    pallas_call x2, Pallas kernels: 13.4 us -> 10.8 us  [the longest x1 5.98 us: run_conv_bwd(): pl.pallas_call(conv_bwd, out_shape=(shape(ROWS, 128), shape(EXTRA_W + 8,...]
  transfers between devices with their start and end apart: 5 -> 8, of which waited for: 4 -> 6; matrix products, arithmetic and copies ran while one was open for 1% -> 1% of each run, Pallas kernels for 0% -> 0%
where the time goes in v3:
time: 137 us; the launch traced here: 134 us
  starting transfers between devices  45.2 us (33%)
  waiting for transfers between devices  44.8 us (33%)
  blocking collectives  20.4 us (15%)
  Pallas kernels  14.9 us (11%)
  local copies, waits for them, and re-layouts  6.8 us (5%)
    all_to_all x4, waiting for transfers between devices, swap(): return lax.all_to_all(parts, 'pen', 0, 0, tiled=True)  31.3 us
    all_to_all x4, starting transfers between devices, swap(): return lax.all_to_all(parts, 'pen', 0, 0, tiled=True)  24.9 us
    all_to_all x1, blocking collectives, swap(): return lax.all_to_all(parts, 'pen', 0, 0, tiled=True)  20.4 us
    ppermute x3, starting transfers between devices, sum_over_partners(): total = total + lax.ppermute(terms, ('zh', 'core'), flip)  13.4 us
    all_to_all x1, waiting for transfers between devices, sum_over_y(): lax.all_to_all(parts, 'y', 0, 0, tiled=True).astype(F32)  7.01 us
    all_to_all x1, starting transfers between devices, sum_over_y(): lax.all_to_all(parts, 'y', 0, 0, tiled=True).astype(F32)  6.82 us
    ppermute x3, waiting for transfers between devices, sum_over_partners(): total = total + lax.ppermute(terms, ('zh', 'core'), flip)  6.49 us
    pallas_call x1, Pallas kernels, run_conv_bwd(): pl.pallas_call(conv_bwd, out_shape=(shape(ROWS, 128), shape(EXTRA_W + 8,...  5.98 us
  transfers between devices with their start and end apart: 8, of which 6 were waited for; matrix products, arithmetic and copies ran while one was open for 1% of the time, Pallas kernels for 0%

profile of v3, /device:TPU:1, one launch (start us, length us, event | category | flops | bytes accessed | tf_op | source)
XLA Modules:
  0.0 133.8 jit_solution(9441875537105752392)
XLA Ops:
  0.6 1.3 reshape.53
  1.9 1.1 copy.32
  3.0 10.4 %all-to-all-start = ((bf16[16,96,128]{2,1,0:T(8,128)(2,1)}), bf16[16,96,128]{2,1,0:T(8,128)(2,1)S(1)}, u32[]{:S(2)}, u32[]{:S(2)}) async-start(bf16[16,96,128]{2,1,0:T(8,128)(2,1)} %bitcast.4), calls=%async_computation | async-start | bytes 786432 | tf_op jit(solution)/shard_map/all_to_all | solution.py:309
  13.7 12.6 %all-to-all-done = bf16[16,96,128]{2,1,0:T(8,128)(2,1)S(1)} async-done(((bf16[16,96,128]{2,1,0:T(8,128)(2,1)}), bf16[16,96,128]{2,1,0:T(8,128)(2,1)S(1)}, u32[]{:S(2)}, u32[]{:S(2)}) %all-to-all-start) | async-done | bytes 393248 | tf_op jit(solution)/shard_map/all_to_all | solution.py:309
  26.3 0.7 copy-done.3
  26.9 4.8 %conv_fwd.1 = (bf16[1536,128]{1,0:T(8,128)(2,1)}, bf16[2,1024,128]{2,1,0:T(8,128)(2,1)S(1)}, bf16[2,1024,128]{2,1,0:T(8,128)(2,1)S(1)}, bf16[256,1024]{1,0:T(8,1...) custom-call(s32[3]{0:T(128)S(1)} %copy-done.3, bf16[1536,128]{1,0:T(8,128)(2,1)S(1)} %bitcast.30, ...), custom_call_target="tpu_custom_call" | custom-call | flops 1000000000 | bytes 4000000 | tf_op jit(solution)/shard_map/conv_fwd/pallas_call | solution.py:255
  31.7 3.7 %all-to-all-start.1 = ((bf16[16,96,128]{2,1,0:T(8,128)(2,1)}), bf16[16,96,128]{2,1,0:T(8,128)(2,1)S(1)}, u32[]{:S(2)}, u32[]{:S(2)}) async-start(bf16[16,96,128]{2,1,0:T(8,128)(2,1)} %bitcast.9), calls=%async_computation.1 | async-start | bytes 786432 | tf_op jit(solution)/shard_map/all_to_all | solution.py:309
  35.6 12.3 %all-to-all-done.1 = bf16[16,96,128]{2,1,0:T(8,128)(2,1)S(1)} async-done(((bf16[16,96,128]{2,1,0:T(8,128)(2,1)}), bf16[16,96,128]{2,1,0:T(8,128)(2,1)S(1)}, u32[]{:S(2)}, u32[]{:S(2)}) %all-to-all-start.1) | async-done | bytes 393248 | tf_op jit(solution)/shard_map/all_to_all | solution.py:309
  47.9 4.1 %middle.1 = bf16[16,144,128]{2,1,0:T(8,128)(2,1)S(1)} custom-call(bf16[1536,128]{1,0:T(8,128)(2,1)S(1)} %bitcast.31, bf16[1536,128]{1,0:T(8,128)(2,1)S(1)} %bitcast.32, bf16[96,384]{1,0:T(8,128)(2,1)S(1)} %copy-done.2, bf16[384,96]{1,0:T(8,128)(2,1)S(1)} %copy.34.wr), custom_call_target="tpu_custom_call" | custom-call | flops 1000000000 | bytes 4000000 | tf_op jit(solution)/shard_map/middle/pallas_call | solution.py:286
  52.0 20.4 %all_to_all.30.d_ref = bf16[16,144,128]{2,1,0:T(8,128)(2,1)S(1)} all-to-all(bf16[16,144,128]{2,1,0:T(8,128)(2,1)S(1)} %middle.1), channel_id=1, replica_groups=mesh['zh'=2,'y'=8,'core'=2,'pen'=16] {'pen'}, dimensions={0} | all-to-all | bytes 1179648 | tf_op jit(solution)/shard_map/all_to_all | solution.py:309
  72.4 0.7 copy-done.5
  73.1 6.0 %conv_bwd.1 = (bf16[1536,128]{1,0:T(8,128)(2,1)}, f32[56,128]{1,0:T(8,128)S(1)}) custom-call(s32[3]{0:T(128)S(1)} %copy-done.3, bf16[16,144,128]{2,1,0:T(8,128)(2,1)S(1)} %all_to_all.30.d_ref, f32[48,128]{1,0:T(8,128)S(1)} %bitcast.35, s32[256,256]{1,0:T(8,128)S(1)} %copy-done.4, f32[8,128]{1,0:T(8,128)S(1)} %copy-done.5, ...), custom_call_target="tpu_custom_call" | custom-call | flops 1000000000 | bytes 4000000 | tf_op jit(solution)/shard_map/conv_bwd/pallas_call | solution.py:270
  79.1 3.7 %all-to-all-start.3 = ((bf16[16,96,128]{2,1,0:T(8,128)(2,1)}), bf16[16,96,128]{2,1,0:T(8,128)(2,1)S(1)}, u32[]{:S(2)}, u32[]{:S(2)}) async-start(bf16[16,96,128]{2,1,0:T(8,128)(2,1)} %bitcast.13), calls=%async_computation.3 | async-start | bytes 786432 | tf_op jit(solution)/shard_map/all_to_all | solution.py:309
  82.8 3.6 %collective-permute-start.2 = (f32[56,128]{1,0:T(8,128)S(1)}, f32[56,128]{1,0:T(8,128)S(1)}, u32[]{:S(2)}, u32[]{:S(2)}) collective-permute-start(f32[56,128]{1,0:T(8,128)S(1)} %get-tuple-element.20), channel_id=1, source_target_pairs={{0,16},{16,0},{256,272},{272,256},{1,17},{17,1},{257,273},{273,257... | collective-permute-start | bytes 86024 | tf_op jit(solution)/shard_map/ppermute | solution.py:318
  86.3 7.8 %collective-permute-start.1 = (f32[56,128]{1,0:T(8,128)S(1)}, f32[56,128]{1,0:T(8,128)S(1)}, u32[]{:S(2)}, u32[]{:S(2)}) collective-permute-start(f32[56,128]{1,0:T(8,128)S(1)} %get-tuple-element.20), channel_id=1, source_target_pairs={{0,272},{16,256},{256,16},{272,0},{1,273},{17,257},{257,17},{273,1... | collective-permute-start | bytes 86024 | tf_op jit(solution)/shard_map/ppermute | solution.py:318
  94.2 2.0 %collective-permute-start = (f32[56,128]{1,0:T(8,128)S(1)}, f32[56,128]{1,0:T(8,128)S(1)}, u32[]{:S(2)}, u32[]{:S(2)}) collective-permute-start(f32[56,128]{1,0:T(8,128)S(1)} %get-tuple-element.20), channel_id=1, source_target_pairs={{0,256},{16,272},{256,0},{272,16},{1,257},{17,273},{257,1},{273,17... | collective-permute-start | bytes 86024 | tf_op jit(solution)/shard_map/ppermute | solution.py:318
  96.8 5.9 %collective-permute-done = f32[56,128]{1,0:T(8,128)S(1)} collective-permute-done((f32[56,128]{1,0:T(8,128)S(1)}, f32[56,128]{1,0:T(8,128)S(1)}, u32[]{:S(2)}, u32[]{:S(2)}) %collective-permute-start) | collective-permute-done | bytes 28704 | tf_op jit(solution)/shard_map/ppermute | solution.py:318
  102.8 0.7 broadcast_in_dim.4
  103.4 6.8 %all-to-all-start.4 = ((bf16[8,56,128]{2,1,0:T(8,128)(2,1)}), bf16[8,56,128]{2,1,0:T(8,128)(2,1)S(1)}, u32[]{:S(2)}, u32[]{:S(2)}) async-start(bf16[8,56,128]{2,1,0:T(8,128)(2,1)} %broadcast_in_dim.4), calls=%async_computation.4 | async-start | bytes 229376 | tf_op jit(solution)/shard_map/all_to_all | solution.py:325
  110.2 0.8 add_convert_fusion
  111.1 7.0 %all-to-all-done.4 = bf16[8,56,128]{2,1,0:T(8,128)(2,1)S(1)} async-done(((bf16[8,56,128]{2,1,0:T(8,128)(2,1)}), bf16[8,56,128]{2,1,0:T(8,128)(2,1)S(1)}, u32[]{:S(2)}, u32[]{:S(2)}) %all-to-all-start.4) | async-done | bytes 114720 | tf_op jit(solution)/shard_map/all_to_all | solution.py:325
  118.8 7.2 %all-to-all-start.5 = ((f32[16,8,128]{2,1,0:T(8,128)}), f32[16,8,128]{2,1,0:T(8,128)S(1)}, u32[]{:S(2)}, u32[]{:S(2)}) async-start(f32[16,8,128]{2,1,0:T(8,128)} %broadcast_in_dim.5), calls=%async_computation.5 | async-start | bytes 131072 | tf_op jit(solution)/shard_map/all_to_all | solution.py:309
  126.6 6.4 %all-to-all-done.5 = f32[16,8,128]{2,1,0:T(8,128)S(1)} async-done(((f32[16,8,128]{2,1,0:T(8,128)}), f32[16,8,128]{2,1,0:T(8,128)S(1)}, u32[]{:S(2)}, u32[]{:S(2)}) %all-to-all-start.5) | async-done | bytes 65568 | tf_op jit(solution)/shard_map/all_to_all | solution.py:309
  133.2 0.6 copy.37
  (31 shorter events, 2.4 us)
Async XLA Ops:
  0.6 12.7 %copy-start = (f32[3,96,9]{1,0,2:T(4,128)S(1)}, f32[3,96,9]{1,0,2:T(4,128)}, u32[]{:S(2)}) copy-start(f32[3,96,9]{1,0,2:T(4,128)} %param.10) | copy-start | bytes 31108
  3.0 23.3 %all-to-all-start = ((bf16[16,96,128]{2,1,0:T(8,128)(2,1)}), bf16[16,96,128]{2,1,0:T(8,128)(2,1)S(1)}, u32[]{:S(2)}, u32[]{:S(2)}) async-start(bf16[16,96,128]{2,1,0:T(8,128)(2,1)} %bitcast.4), calls=%async_computation | async-start | bytes 786432 | tf_op jit(solution)/shard_map/all_to_all | solution.py:309
  13.4 12.8 %copy-start.4 = (s32[256,256]{1,0:T(8,128)S(1)}, s32[256,256]{1,0:T(8,128)}, u32[]{:S(2)}) copy-start(s32[256,256]{1,0:T(8,128)} %constant.19.clone.delta) | copy-start | bytes 786436
  26.2 0.7 copy-start.3
  31.7 3.7 %copy-start.6 = (bf16[384,96]{0,1:T(8,128)(2,1)S(1)}, bf16[384,96]{0,1:T(8,128)(2,1)}, u32[]{:S(2)}) copy-start(bf16[384,96]{0,1:T(8,128)(2,1)} %param.13) | copy-start | bytes 221188
  31.7 16.1 %copy-start.1 = (bf16[1,96,2,1024]{3,2,1,0:T(2,128)(2,1)S(1)}, bf16[1,96,2,1024]{3,2,1,0:T(2,128)(2,1)}, u32[]{:S(2)}) copy-start(bf16[1,96,2,1024]{3,2,1,0:T(2,128)(2,1)} %param.9) | copy-start | bytes 1179652
  31.7 16.1 %all-to-all-start.1 = ((bf16[16,96,128]{2,1,0:T(8,128)(2,1)}), bf16[16,96,128]{2,1,0:T(8,128)(2,1)S(1)}, u32[]{:S(2)}, u32[]{:S(2)}) async-start(bf16[16,96,128]{2,1,0:T(8,128)(2,1)} %bitcast.9), calls=%async_computation.1 | async-start | bytes 786432 | tf_op jit(solution)/shard_map/all_to_all | solution.py:309
  35.4 12.4 %copy-start.2 = (bf16[96,384]{1,0:T(8,128)(2,1)S(1)}, bf16[96,384]{1,0:T(8,128)(2,1)}, u32[]{:S(2)}) copy-start(bf16[96,384]{1,0:T(8,128)(2,1)} %we.1) | copy-start | bytes 221188
  72.4 0.7 copy-start.5
  79.1 23.7 %all-to-all-start.3 = ((bf16[16,96,128]{2,1,0:T(8,128)(2,1)}), bf16[16,96,128]{2,1,0:T(8,128)(2,1)S(1)}, u32[]{:S(2)}, u32[]{:S(2)}) async-start(bf16[16,96,128]{2,1,0:T(8,128)(2,1)} %bitcast.13), calls=%async_computation.3 | async-start | bytes 786432 | tf_op jit(solution)/shard_map/all_to_all | solution.py:309
  82.8 13.5 %collective-permute-start.2 = (f32[56,128]{1,0:T(8,128)S(1)}, f32[56,128]{1,0:T(8,128)S(1)}, u32[]{:S(2)}, u32[]{:S(2)}) collective-permute-start(f32[56,128]{1,0:T(8,128)S(1)} %get-tuple-element.20), channel_id=1, source_target_pairs={{0,16},{16,0},{256,272},{272,256},{1,17},{17,1},{257,273},{273,257... | collective-permute-start | bytes 86024 | tf_op jit(solution)/shard_map/ppermute | solution.py:318
  86.3 10.4 %collective-permute-start.1 = (f32[56,128]{1,0:T(8,128)S(1)}, f32[56,128]{1,0:T(8,128)S(1)}, u32[]{:S(2)}, u32[]{:S(2)}) collective-permute-start(f32[56,128]{1,0:T(8,128)S(1)} %get-tuple-element.20), channel_id=1, source_target_pairs={{0,272},{16,256},{256,16},{272,0},{1,273},{17,257},{257,17},{273,1... | collective-permute-start | bytes 86024 | tf_op jit(solution)/shard_map/ppermute | solution.py:318
  94.2 8.5 %collective-permute-start = (f32[56,128]{1,0:T(8,128)S(1)}, f32[56,128]{1,0:T(8,128)S(1)}, u32[]{:S(2)}, u32[]{:S(2)}) collective-permute-start(f32[56,128]{1,0:T(8,128)S(1)} %get-tuple-element.20), channel_id=1, source_target_pairs={{0,256},{16,272},{256,0},{272,16},{1,257},{17,273},{257,1},{273,17... | collective-permute-start | bytes 86024 | tf_op jit(solution)/shard_map/ppermute | solution.py:318
  103.4 14.7 %all-to-all-start.4 = ((bf16[8,56,128]{2,1,0:T(8,128)(2,1)}), bf16[8,56,128]{2,1,0:T(8,128)(2,1)S(1)}, u32[]{:S(2)}, u32[]{:S(2)}) async-start(bf16[8,56,128]{2,1,0:T(8,128)(2,1)} %broadcast_in_dim.4), calls=%async_computation.4 | async-start | bytes 229376 | tf_op jit(solution)/shard_map/all_to_all | solution.py:325
  118.8 14.2 %all-to-all-start.5 = ((f32[16,8,128]{2,1,0:T(8,128)}), f32[16,8,128]{2,1,0:T(8,128)S(1)}, u32[]{:S(2)}, u32[]{:S(2)}) async-start(f32[16,8,128]{2,1,0:T(8,128)} %broadcast_in_dim.5), calls=%async_computation.5 | async-start | bytes 131072 | tf_op jit(solution)/shard_map/all_to_all | solution.py:309

commit v4 on v3

--- a/solution.py
+++ b/solution.py
@@ -20,6 +20,7 @@
 PIECE = ROWS // GROUPS
 BH = H // GROUPS
 EXTRA_W = 2 * BH
+EXTRA_K = 16
 HALO = 16
 F32 = jnp.float32
 BF16 = jnp.bfloat16
@@ -36,14 +37,6 @@
     return np.where(same, delta, -1).astype(np.int32)
 
 
-def channel_table():
-    r = np.arange(128)
-    out = np.zeros((8, 128), np.float32)
-    for c in range(CH):
-        out[c] = (r % CH == c) & (r < C)
-    return out
-
-
 def contract(a, b, da, db):
     return lax.dot_general(a, b, (((da,), (db,)), ((), ())), preferred_element_type=F32)
 
@@ -74,18 +67,25 @@
     ref[p, y, HALO + L:, :] = v[:HALO, :]
 
 
-def conv_fwd(dil, a_ref, coef, delta, wide, mixed_ref, first_ref, second_ref, field_ref, hi_ref,
-             lo_ref, stage, fir, sec, mix):
-    d0, d1, d2 = dil[0], dil[1], dil[2]
+def prepare(dil, coef, delta, hi_ref, lo_ref, eye_ref):
+    spacing = dil[0]
+    for half in range(2):
+        cols = slice(half * 128, (half + 1) * 128)
+        table = delta[:, cols]
+        m = jnp.zeros((256, 128), F32)
+        for t in range(TAPS):
+            m = m + jnp.where(table == (((t - 4) * spacing) & (L - 1)), coef[t:t + 1, :], 0.0)
+        hi = m.astype(BF16)
+        hi_ref[:, cols] = hi
+        lo_ref[:, cols] = (m - hi.astype(F32)).astype(BF16)
+        eye_ref[:, cols] = jnp.where(table == 0, 1.0, 0.0).astype(BF16)
+
+
+def conv_fwd(dil, a_ref, coef, hi_ref, lo_ref, eye_ref, mixed_ref, first_ref, second_ref,
+             field_ref, stage, fir, sec, mix):
+    d1, d2 = dil[1], dil[2]
     stage[...] = a_ref[...].astype(F32)
-    m = jnp.zeros((256, 256), F32)
-    for t in range(TAPS):
-        m = m + jnp.where(delta[...] == (((t - 4) * d0) & (L - 1)), wide[t:t + 1, :], 0.0)
-    hi = m.astype(BF16)
-    lo = (m - hi.astype(F32)).astype(BF16)
-    hi_ref[...] = hi
-    lo_ref[...] = lo
-    eye = jnp.where(delta[...] == 0, 1.0, 0.0).astype(BF16)
+    hi, lo, eye = hi_ref[...], lo_ref[...], eye_ref[...]
     for j in range(8):
         f = load_field(stage, j)
         field_ref[:, j * 128:(j + 1) * 128] = f
@@ -126,15 +126,15 @@
     mixed_ref[...] = stage[...].astype(BF16)
 
 
-def conv_bwd(dil, d_ref, coef, delta, table, first_ref, second_ref, field_ref, hi_ref, lo_ref,
-             out_ref, sums_ref, stage, dmh, dse, dfi, acc_ref):
-    d0, d1, d2 = dil[0], dil[1], dil[2]
+def conv_bwd(dil, d_ref, coef, which, eye_ref, first_ref, second_ref, field_ref,
+             dfi, sums_ref, stage, dmh, dse, acc_ref):
+    d1, d2 = dil[1], dil[2]
     weights = jnp.zeros((EXTRA_W, 128), F32)
     for g in range(GROUPS):
         stage[g * PIECE:(g + 1) * PIECE, :] = d_ref[g, 0:PIECE, :].astype(F32)
         weights = weights + d_ref[g, PIECE:PIECE + EXTRA_W, :].astype(F32)
     sums_ref[0:EXTRA_W, :] = weights
-    eye = jnp.where(delta[...] == 0, 1.0, 0.0).astype(BF16)
+    eye = eye_ref[...]
     for j in range(8):
         out = contract(load_field(stage, j), eye, 0, 0)
         for p in range(2):
@@ -184,22 +184,35 @@
     for t in range(27, 32):
         acc_ref[t] = jnp.zeros((8, 128), F32)
 
+    cross = contract(field_ref[...], dfi[...], 1, 0)
+    for t in range(TAPS):
+        keep = jnp.where(which[...] == t, cross, 0.0)
+        keep = jnp.sum(keep.reshape(32, 8, 256), axis=0)
+        acc_ref[t] = keep[:, :128] + keep[:, 128:]
+    lane = lax.broadcasted_iota(jnp.int32, (8, 128), 1)
+    channel = lax.broadcasted_iota(jnp.int32, (8, 128), 0)
+    table = jnp.where((lax.rem(lane, CH) == channel) & (lane < C), 1.0, 0.0)
+    kern = lax.dot_general(
+        table, jnp.sum(acc_ref[...], axis=1), (((1,), (1,)), ((), ())),
+        precision=lax.Precision.HIGHEST, preferred_element_type=F32)
+    kern = jnp.concatenate([kern] * 4, axis=1)
+    sums_ref[EXTRA_W:EXTRA_W + 8, :] = jnp.where(lane // 32 == dil[3], kern, 0.0)
+
+
+def pack_out(dfi, hi_ref, lo_ref, mine, other, out_ref, weight_ref, stage):
     hi, lo = hi_ref[...], lo_ref[...]
     for j in range(8):
         block = dfi[j * 128:(j + 1) * 128, :]
         out = contract(hi, block, 1, 1) + contract(lo, block, 1, 1)
         for p in range(2):
             stage[pl.ds(2 * j + p, C, stride=STRIDE), :] = out[p * 128:p * 128 + C, :]
-    cross = contract(field_ref[...], dfi[...], 1, 0)
-    for t in range(TAPS):
-        keep = jnp.where(delta[...] == (((t - 4) * d0) & (L - 1)), cross, 0.0)
-        keep = jnp.sum(keep.reshape(32, 8, 256), axis=0)
-        acc_ref[t] = keep[:, :128] + keep[:, 128:]
-    sums_ref[EXTRA_W:EXTRA_W + 8, :] = jnp.zeros((8, 128), F32)
-    sums_ref[EXTRA_W:EXTRA_W + 8, 0:32] = lax.dot_general(
-        table[...], jnp.sum(acc_ref[...], axis=1), (((1,), (1,)), ((), ())),
-        precision=lax.Precision.HIGHEST, preferred_element_type=F32)
-    out_ref[...] = stage[...].astype(BF16)
+    weight_ref[...] = mine[0:EXTRA_W, :] + other[0:EXTRA_W, :]
+    kern = mine[EXTRA_W:, :] + other[EXTRA_W:, :]
+    high = kern.astype(BF16).astype(F32)
+    extra = jnp.concatenate([high, kern - high], axis=0).astype(BF16)
+    for g in range(GROUPS):
+        out_ref[g, 0:PIECE, :] = stage[g * PIECE:(g + 1) * PIECE, :].astype(BF16)
+        out_ref[g, PIECE:PIECE + EXTRA_K, :] = extra
 
 
 BLOCK = 256
@@ -251,35 +264,62 @@
     return jax.ShapeDtypeStruct(dims, dtype)
 
 
-def run_conv_fwd(dilations, rows, coef, delta, wide):
+def estimate(flops):
+    return pl.CostEstimate(flops=flops, bytes_accessed=4 * 10**6, transcendentals=0)
+
+
+def run_prepare(scalars, coef, delta):
+    return pl.pallas_call(
+        prepare,
+        out_shape=(shape(256, 256),) * 3,
+        in_specs=[SMEM] + [VMEM] * 2,
+        out_specs=(VMEM,) * 3,
+        compiler_params=PARAMS,
+        cost_estimate=estimate(10**8),
+        name="prepare",
+    )(scalars, coef, delta)
+
+
+def run_conv_fwd(scalars, rows, coef, hi, lo, eye):
     return pl.pallas_call(
         conv_fwd,
-        out_shape=(shape(ROWS, 128), shape(2, 1024, 128), shape(2, 1024, 128), shape(256, 1024),
-                   shape(256, 256), shape(256, 256)),
-        in_specs=[SMEM] + [VMEM] * 4,
-        out_specs=(VMEM,) * 6,
+        out_shape=(shape(ROWS, 128), shape(2, 1024, 128), shape(2, 1024, 128), shape(256, 1024)),
+        in_specs=[SMEM] + [VMEM] * 5,
+        out_specs=(VMEM,) * 4,
         scratch_shapes=[pltpu.VMEM((ROWS, 128), F32), pltpu.VMEM((2, L, L, 128), F32),
                         pltpu.VMEM((2, L, L + 2 * HALO, 128), F32), pltpu.VMEM((1024, 256), BF16)],
         compiler_params=PARAMS,
-        cost_estimate=pl.CostEstimate(flops=10**9, bytes_accessed=4 * 10**6, transcendentals=0),
+        cost_estimate=estimate(10**9),
         name="conv_fwd",
-    )(dilations, rows, coef, delta, wide)
-
-
-def run_conv_bwd(dilations, rows, coef, delta, table, first, second, field, hi, lo):
+    )(scalars, rows, coef, hi, lo, eye)
+
+
+def run_conv_bwd(scalars, rows, coef, which, eye, first, second, field):
     return pl.pallas_call(
         conv_bwd,
-        out_shape=(shape(ROWS, 128), shape(EXTRA_W + 8, 128, dtype=F32)),
-        in_specs=[SMEM] + [VMEM] * 9,
+        out_shape=(shape(1024, 256), shape(EXTRA_W + 8, 128, dtype=F32)),
+        in_specs=[SMEM] + [VMEM] * 7,
         out_specs=(VMEM,) * 2,
         scratch_shapes=[pltpu.VMEM((ROWS, 128), F32),
                         pltpu.VMEM((2, L, L + 2 * HALO, 128), F32),
-                        pltpu.VMEM((2, L, L, 128), F32), pltpu.VMEM((1024, 256), BF16),
-                        pltpu.VMEM((32, 8, 128), F32)],
+                        pltpu.VMEM((2, L, L, 128), F32), pltpu.VMEM((32, 8, 128), F32)],
         compiler_params=PARAMS,
-        cost_estimate=pl.CostEstimate(flops=10**9, bytes_accessed=4 * 10**6, transcendentals=0),
+        cost_estimate=estimate(10**9),
         name="conv_bwd",
-    )(dilations, rows, coef, delta, table, first, second, field, hi, lo)
+    )(scalars, rows, coef, which, eye, first, second, field)
+
+
+def run_pack_out(d_first, hi, lo, mine, other):
+    return pl.pallas_call(
+        pack_out,
+        out_shape=(shape(GROUPS, PIECE + EXTRA_K, 128), shape(EXTRA_W, 128, dtype=F32)),
+        in_specs=[VMEM] * 5,
+        out_specs=(VMEM,) * 2,
+        scratch_shapes=[pltpu.VMEM((ROWS, 128), F32)],
+        compiler_params=PARAMS,
+        cost_estimate=estimate(10**9),
+        name="pack_out",
+    )(d_first, hi, lo, mine, other)
 
 
 def run_middle(rows, cot_rows, expand_weight, reduce_weight):
@@ -309,49 +349,53 @@
     return lax.all_to_all(parts, "pen", 0, 0, tiled=True)
 
 
-def sum_over_partners(terms):
-    total = terms
-    if lax.axis_size("zh") == 2:
-        flips = [[(0, 2), (1, 3), (2, 0), (3, 1)], [(0, 3), (1, 2), (2, 1), (3, 0)],
-                 [(0, 1), (1, 0), (2, 3), (3, 2)]]
-        for flip in flips:
-            total = total + lax.ppermute(terms, ("zh", "core"), flip)
-    return total
-
-
-def sum_over_y(terms):
-    size = lax.axis_size("y")
+def from_other_core(terms):
+    if lax.axis_size("core") == 1:
+        return jnp.zeros_like(terms)
+    return lax.ppermute(terms, "core", [(0, 1), (1, 0)])
+
+
+def sum_over_chips(terms):
+    size = lax.axis_size("zh") * lax.axis_size("y")
     parts = jnp.broadcast_to(terms.astype(BF16)[None], (size,) + terms.shape)
-    return jnp.sum(lax.all_to_all(parts, "y", 0, 0, tiled=True).astype(F32), axis=0)
+    return jnp.sum(lax.all_to_all(parts, ("zh", "y"), 0, 0, tiled=True).astype(F32), axis=0)
 
 
 def per_device(activations, cotangent, depth_kernels, dilations, expand_weight, reduce_weight):
     delta = jnp.asarray(delta_table())
-    table = jnp.asarray(channel_table())
     own = lax.dynamic_slice_in_dim(depth_kernels, lax.axis_index("pen") * CH, CH, 1)
     coef = jnp.tile(own.transpose(0, 2, 1), (1, 1, GROUPS))
     coef = jnp.pad(coef, ((0, 0), (0, 16 - TAPS), (0, 128 - C))).reshape(48, 128)
-    wide = jnp.concatenate([coef[0:16], coef[0:16]], axis=1)
-
-    lines = swap(to_rows(activations).reshape(GROUPS, PIECE, 128)).reshape(ROWS, 128)
-    mixed, first, second, field, hi, lo = run_conv_fwd(dilations, lines, coef, delta, wide)
+    group = lax.axis_index("pen").astype(jnp.int32)
+    scalars = jnp.concatenate([dilations, jnp.mod(group, 4)[None]])
+    steps = ((jnp.arange(TAPS, dtype=jnp.int32) - 4) * dilations[0]) % L
+    which = jnp.full((256, 256), -1, jnp.int32)
+    for t in range(TAPS):
+        which = jnp.where(delta == steps[t], t, which)
+
+    start = activations.reshape(GROUPS, CH, 2, 8, 128).transpose(0, 1, 3, 2, 4)
+    lines = swap(start).reshape(ROWS, 128)
+    hi, lo, eye = run_prepare(scalars, coef, delta)
+    mixed, first, second, field = run_conv_fwd(scalars, lines, coef, hi, lo, eye)
     cot_rows = to_rows(cotangent)
     mixed = swap(mixed.reshape(GROUPS, PIECE, 128)).reshape(ROWS, 128)
     d_lines = swap(run_middle(mixed, cot_rows, expand_weight, reduce_weight))
-    d_conv, sums = run_conv_bwd(
-        dilations, d_lines, coef, delta, table, first, second, field, hi, lo)
-    d_input = swap(d_conv.reshape(GROUPS, PIECE, 128)).reshape(ROWS, 128)
-    sums = sum_over_partners(sums)
-    sums, d_input = lax.optimization_barrier((sums, d_input))
-    sums = sum_over_y(sums)
+    d_first, mine = run_conv_bwd(scalars, d_lines, coef, which, eye, first, second, field)
+    d_conv, weights = run_pack_out(d_first, hi, lo, mine, from_other_core(mine))
+    arrived = swap(d_conv)
+
+    kern = arrived[:, PIECE:, :].astype(F32).reshape(4, 4, 2, 8, 128)
+    kern = jnp.sum(kern, axis=(1, 2)).reshape(32, 128)
+    sums = sum_over_chips(jnp.concatenate([weights, kern], axis=0))
+    d_input = arrived[:, :PIECE, :].reshape(ROWS, 128)
     grad_input = from_rows((cot_rows.astype(F32) + d_input.astype(F32)).astype(BF16))
 
     samples = lax.axis_size("zh") * lax.axis_size("y") * lax.axis_size("core")
     sums = sums * (1.0 / math.sqrt(samples * L * L * L))
-    kern = jnp.broadcast_to(sums[None, EXTRA_W:, :], (GROUPS, 8, 128))
-    kern = swap(kern)[:, :CH, :3 * TAPS].reshape(C, 3, TAPS).transpose(1, 0, 2)
     own_expand = sums[0:BH, 0:C].T
     own_reduce = sums[BH:EXTRA_W, 0:C]
+    kern = sums[EXTRA_W:].reshape(4, 8, 4, 32)[:, :CH, :, :3 * TAPS]
+    kern = kern.transpose(0, 2, 1, 3).reshape(C, 3, TAPS).transpose(1, 0, 2)
     return grad_input, own_expand, own_reduce, kern
 
 

time: 137 us -> 131 us (0.956)
  the two profiles are of different devices: /device:TPU:1 before, /device:TPU:8 now
where the time goes in v4:
time: 131 us; the launch traced here: 130 us
  waiting for transfers between devices  64.7 us (49%)
  starting transfers between devices  35.9 us (27%)
  Pallas kernels  16.8 us (13%)
  other arithmetic  7.21 us (6%)
  local copies, waits for them, and re-layouts  4.31 us (3%)
    all_to_all x4, waiting for transfers between devices, swap(): return lax.all_to_all(parts, 'pen', 0, 0, tiled=True)  50.2 us
    all_to_all x4, starting transfers between devices, swap(): return lax.all_to_all(parts, 'pen', 0, 0, tiled=True)  20.7 us
    all_to_all x1, starting transfers between devices, sum_over_chips(): lax.all_to_all(parts, ('zh', 'y'), 0, 0, tiled=True).astype(F32)  13.3 us
    all_to_all x1, waiting for transfers between devices, sum_over_chips(): lax.all_to_all(parts, ('zh', 'y'), 0, 0, tiled=True).astype(F32)  13.3 us
    select_n x1, other arithmetic, per_device(): which = jnp.where(delta == steps[t], t, which)  5.86 us
    pallas_call x1, Pallas kernels, run_conv_bwd(): pl.pallas_call(conv_bwd, out_shape=(shape(1024, 256), shape(EXTRA_W + 8,...  4.92 us
    pallas_call x1, Pallas kernels, run_middle(): pl.pallas_call(middle, out_shape=shape(GROUPS, PIECE + EXTRA_W, 128), in_...  4.85 us
    pallas_call x1, Pallas kernels, run_conv_fwd(): pl.pallas_call(conv_fwd, out_shape=(shape(ROWS, 128), shape(2, 1024, 128)...  4.64 us
  transfers between devices with their start and end apart: 6, of which 6 were waited for; matrix products, arithmetic and copies ran while one was open for 6% of the time, Pallas kernels for 1%

profile of v4, /device:TPU:8, one launch (start us, length us, event | category | flops | bytes accessed | tf_op | source)
XLA Modules:
  0.0 129.7 jit_solution(4683230398867235506)
XLA Ops:
  0.6 9.8 %all-to-all-start = ((bf16[16,6,8,2,128]{4,3,2,1,0:T(2,128)(2,1)}), bf16[16,6,8,2,128]{4,3,2,1,0:T(2,128)(2,1)S(1)}, u32[]{:S(2)}, u32[]{:S(2)}) async-start(bf16[16,6,8,2,128]{4,3,2,1,0:T(2,128)(2,1)} %bitcast.53), calls=%async_computation | async-start | bytes 786432 | tf_op jit(solution)/shard_map/all_to_all | solution.py:349
  10.8 0.6 copy-done.5
  11.5 0.8 prepare.1
  12.4 11.8 %all-to-all-done = bf16[16,6,8,2,128]{4,3,2,1,0:T(2,128)(2,1)S(1)} async-done(((bf16[16,6,8,2,128]{4,3,2,1,0:T(2,128)(2,1)}), bf16[16,6,8,2,128]{4,3,2,1,0:T(2,128)(2,1)S(1)}, u32[]{:S(2)}, u32[]{:S(2)}) %all-to-all-start) | async-done | bytes 393248 | tf_op jit(solution)/shard_map/all_to_all | solution.py:349
  24.2 4.6 %conv_fwd.1 = (bf16[1536,128]{1,0:T(8,128)(2,1)}, bf16[2,1024,128]{2,1,0:T(8,128)(2,1)S(1)}, bf16[2,1024,128]{2,1,0:T(8,128)(2,1)S(1)}, bf16[256,1024]{1,0:T(8,128)(2,1)S(1)}) custom-call(s32[4]{0:T(128)S(1)} %pad_add_fusion.dil, bf16[1536,128]{1,0:T(8,128)(2,1)S(1)} %bitcast.45, f32[48,128]{1,0:T(8,128)S(1)} %bitcast.49, ...), custom_call_target="tpu_custom_call" | custom-call | flops 1000000000 | bytes 4000000 | tf_op jit(solution)/shard_map/conv_fwd/pallas_call | solution.py:284
  28.8 3.7 %all-to-all-start.1 = ((bf16[16,96,128]{2,1,0:T(8,128)(2,1)}), bf16[16,96,128]{2,1,0:T(8,128)(2,1)S(1)}, u32[]{:S(2)}, u32[]{:S(2)}) async-start(bf16[16,96,128]{2,1,0:T(8,128)(2,1)} %bitcast.8), calls=%async_computation.1 | async-start | bytes 786432 | tf_op jit(solution)/shard_map/all_to_all | solution.py:349
  32.7 12.7 %all-to-all-done.1 = bf16[16,96,128]{2,1,0:T(8,128)(2,1)S(1)} async-done(((bf16[16,96,128]{2,1,0:T(8,128)(2,1)}), bf16[16,96,128]{2,1,0:T(8,128)(2,1)S(1)}, u32[]{:S(2)}, u32[]{:S(2)}) %all-to-all-start.1) | async-done | bytes 393248 | tf_op jit(solution)/shard_map/all_to_all | solution.py:349
  45.4 4.8 %middle.1 = bf16[16,144,128]{2,1,0:T(8,128)(2,1)} custom-call(bf16[1536,128]{1,0:T(8,128)(2,1)S(1)} %bitcast.46, bf16[1536,128]{1,0:T(8,128)(2,1)S(1)} %bitcast.47, bf16[96,384]{1,0:T(8,128)(2,1)S(1)} %copy-done.3, bf16[384,96]{1,0:T(8,128)(2,1)S(1)} %copy.26.wr), custom_call_target="tpu_custom_call" | custom-call | flops 1000000000 | bytes 4000000 | tf_op jit(solution)/shard_map/middle/pallas_call | solution.py:326
  50.3 3.6 %all-to-all-start.2 = ((bf16[16,144,128]{2,1,0:T(8,128)(2,1)}), bf16[16,144,128]{2,1,0:T(8,128)(2,1)S(1)}, u32[]{:S(2)}, u32[]{:S(2)}) async-start(bf16[16,144,128]{2,1,0:T(8,128)(2,1)} %middle.1), calls=%async_computation.2 | async-start | bytes 1179648 | tf_op jit(solution)/shard_map/all_to_all | solution.py:349
  53.9 0.7 fusion.4
  54.6 5.9 %select_select_fusion.which = s32[256,256]{1,0:T(8,128)S(1)} fusion(s32[256,256]{1,0:T(8,128)S(1)} %copy-done.2, s32[]{:T(128)} %bitcast.21, s32[]{:T(128)} %bitcast.20, s32[]{:T(128)} %bitcast.19, s32[]{:T(128)} %bitcast.18, s32[]{:T(128)} %bitcast.17, s32[]{:T(128)} %bitcast.16, s32[]{:T(128)} %bitcast.15, s32[]{:T(128)} %bitcast.14, s32[]{:T(128)} %bitcast.13), kind=kLoop, calls=%fused_computation.4 | loop fusion | flops 1179648 | bytes 524324 | tf_op jit(solution)/shard_map/jit(_where)/select_n | solution.py:374
  60.4 10.1 %all-to-all-done.2.d_ref = bf16[16,144,128]{2,1,0:T(8,128)(2,1)S(1)} async-done(((bf16[16,144,128]{2,1,0:T(8,128)(2,1)}), bf16[16,144,128]{2,1,0:T(8,128)(2,1)S(1)}, u32[]{:S(2)}, u32[]{:S(2)}) %all-to-all-start.2) | async-done | bytes 589856 | tf_op jit(solution)/shard_map/all_to_all | solution.py:349
  70.5 4.9 %conv_bwd.1 = (bf16[1024,256]{1,0:T(8,128)(2,1)S(1)}, f32[56,128]{1,0:T(8,128)S(1)}) custom-call(s32[4]{0:T(128)S(1)} %pad_add_fusion.dil, bf16[16,144,128]{2,1,0:T(8,128)(2,1)S(1)} %all-to-all-done.2.d_ref, f32[48,128]{1,0:T(8,128)S(1)} %bitcast.50, s32[256,256]{1,0:T(8,128)S(1)} %select_select_fusion.which, ...), custom_call_target="tpu_custom_call" | custom-call | flops 1000000000 | bytes 4000000 | tf_op jit(solution)/shard_map/conv_bwd/pallas_call | solution.py:298
  75.4 1.9 %collective-permute-start = (f32[56,128]{1,0:T(8,128)S(1)}, f32[56,128]{1,0:T(8,128)S(1)}, u32[]{:S(2)}, u32[]{:S(2)}) collective-permute-start(f32[56,128]{1,0:T(8,128)S(1)} %get-tuple-element.23.mine), channel_id=1, source_target_pairs={{0,16},{16,0},{1,17},{17,1},{2,18},{18,2},{3,19},{19,3},{4,20},{20... | collective-permute-start | bytes 86024 | tf_op jit(solution)/shard_map/ppermute | solution.py:355
  77.4 1.2 collective-permute-done.other
  78.5 1.5 %pack_out.1 = (bf16[16,112,128]{2,1,0:T(8,128)(2,1)}, f32[48,128]{1,0:T(8,128)S(1)}) custom-call(bf16[1024,256]{1,0:T(8,128)(2,1)S(1)} %get-tuple-element.22.dfi, bf16[256,256]{1,0:T(8,128)(2,1)S(1)} %get-tuple-element.15.hi_ref, bf16[256,256]{1,0:T(8,128)(2,1)S(1)} %get-tuple-element.16.lo_ref, f32[56,128]{1,0:T(8,128)S(1)} %get-tuple-element.23.mine, ...), custom_call_target="tpu_custom_call" | custom-call | flops 1000000000 | bytes 4000000 | tf_op jit(solution)/shard_map/pack_out/pallas_call | solution.py:313
  80.1 3.6 %all-to-all-start.3 = ((bf16[16,112,128]{2,1,0:T(8,128)(2,1)}), bf16[16,112,128]{2,1,0:T(8,128)(2,1)S(1)}, u32[]{:S(2)}, u32[]{:S(2)}) async-start(bf16[16,112,128]{2,1,0:T(8,128)(2,1)} %get-tuple-element.24), calls=%async_computation.3 | async-start | bytes 917504 | tf_op jit(solution)/shard_map/all_to_all | solution.py:349
  83.6 15.7 %all-to-all-done.3 = bf16[16,112,128]{2,1,0:T(8,128)(2,1)S(1)} async-done(((bf16[16,112,128]{2,1,0:T(8,128)(2,1)}), bf16[16,112,128]{2,1,0:T(8,128)(2,1)S(1)}, u32[]{:S(2)}, u32[]{:S(2)}) %all-to-all-start.3) | async-done | bytes 458784 | tf_op jit(solution)/shard_map/all_to_all | solution.py:349
  99.3 0.8 broadcast_in_dim.51
  100.1 13.3 %all-to-all-start.4 = ((bf16[16,80,128]{2,1,0:T(8,128)(2,1)}), bf16[16,80,128]{2,1,0:T(8,128)(2,1)S(1)}, u32[]{:S(2)}, u32[]{:S(2)}) async-start(bf16[16,80,128]{2,1,0:T(8,128)(2,1)} %broadcast_in_dim.51), calls=%async_computation.4 | async-start | bytes 655360 | tf_op jit(solution)/shard_map/all_to_all | solution.py:361
  113.4 1.2 fusion.1
  114.6 13.3 %all-to-all-done.4 = bf16[16,80,128]{2,1,0:T(8,128)(2,1)S(1)} async-done(((bf16[16,80,128]{2,1,0:T(8,128)(2,1)}), bf16[16,80,128]{2,1,0:T(8,128)(2,1)S(1)}, u32[]{:S(2)}, u32[]{:S(2)}) %all-to-all-start.4) | async-done | bytes 327712 | tf_op jit(solution)/shard_map/all_to_all | solution.py:361
  128.0 0.6 fusion.3
  129.1 0.6 copy.29
  (31 shorter events, 1.2 us)
Async XLA Ops:
  0.6 9.9 %copy-start = (f32[3,96,9]{1,0,2:T(4,128)S(1)}, f32[3,96,9]{1,0,2:T(4,128)}, u32[]{:S(2)}) copy-start(f32[3,96,9]{1,0,2:T(4,128)} %param.9) | copy-start | bytes 31108
  0.6 23.5 %all-to-all-start = ((bf16[16,6,8,2,128]{4,3,2,1,0:T(2,128)(2,1)}), bf16[16,6,8,2,128]{4,3,2,1,0:T(2,128)(2,1)S(1)}, u32[]{:S(2)}, u32[]{:S(2)}) async-start(bf16[16,6,8,2,128]{4,3,2,1,0:T(2,128)(2,1)} %bitcast.53), calls=%async_computation | async-start | bytes 786432 | tf_op jit(solution)/shard_map/all_to_all | solution.py:349
  10.6 1.0 copy-start.2
  10.8 0.7 copy-start.5
  28.8 3.7 %copy-start.4 = (bf16[384,96]{0,1:T(8,128)(2,1)S(1)}, bf16[384,96]{0,1:T(8,128)(2,1)}, u32[]{:S(2)}) copy-start(bf16[384,96]{0,1:T(8,128)(2,1)} %param.12) | copy-start | bytes 221188
  28.8 16.6 %copy-start.1 = (bf16[1,96,2,1024]{3,2,1,0:T(2,128)(2,1)S(1)}, bf16[1,96,2,1024]{3,2,1,0:T(2,128)(2,1)}, u32[]{:S(2)}) copy-start(bf16[1,96,2,1024]{3,2,1,0:T(2,128)(2,1)} %param.8) | copy-start | bytes 1179652
  28.8 16.6 %all-to-all-start.1 = ((bf16[16,96,128]{2,1,0:T(8,128)(2,1)}), bf16[16,96,128]{2,1,0:T(8,128)(2,1)S(1)}, u32[]{:S(2)}, u32[]{:S(2)}) async-start(bf16[16,96,128]{2,1,0:T(8,128)(2,1)} %bitcast.8), calls=%async_computation.1 | async-start | bytes 786432 | tf_op jit(solution)/shard_map/all_to_all | solution.py:349
  32.5 12.9 %copy-start.3 = (bf16[96,384]{1,0:T(8,128)(2,1)S(1)}, bf16[96,384]{1,0:T(8,128)(2,1)}, u32[]{:S(2)}) copy-start(bf16[96,384]{1,0:T(8,128)(2,1)} %we.1) | copy-start | bytes 221188
  50.3 20.2 %all-to-all-start.2 = ((bf16[16,144,128]{2,1,0:T(8,128)(2,1)}), bf16[16,144,128]{2,1,0:T(8,128)(2,1)S(1)}, u32[]{:S(2)}, u32[]{:S(2)}) async-start(bf16[16,144,128]{2,1,0:T(8,128)(2,1)} %middle.1), calls=%async_computation.2 | async-start | bytes 1179648 | tf_op jit(solution)/shard_map/all_to_all | solution.py:349
  75.4 3.1 %collective-permute-start = (f32[56,128]{1,0:T(8,128)S(1)}, f32[56,128]{1,0:T(8,128)S(1)}, u32[]{:S(2)}, u32[]{:S(2)}) collective-permute-start(f32[56,128]{1,0:T(8,128)S(1)} %get-tuple-element.23.mine), channel_id=1, source_target_pairs={{0,16},{16,0},{1,17},{17,1},{2,18},{18,2},{3,19},{19,3},{4,20},{20... | collective-permute-start | bytes 86024 | tf_op jit(solution)/shard_map/ppermute | solution.py:355
  80.1 19.2 %all-to-all-start.3 = ((bf16[16,112,128]{2,1,0:T(8,128)(2,1)}), bf16[16,112,128]{2,1,0:T(8,128)(2,1)S(1)}, u32[]{:S(2)}, u32[]{:S(2)}) async-start(bf16[16,112,128]{2,1,0:T(8,128)(2,1)} %get-tuple-element.24), calls=%async_computation.3 | async-start | bytes 917504 | tf_op jit(solution)/shard_map/all_to_all | solution.py:349
  100.1 27.8 %all-to-all-start.4 = ((bf16[16,80,128]{2,1,0:T(8,128)(2,1)}), bf16[16,80,128]{2,1,0:T(8,128)(2,1)S(1)}, u32[]{:S(2)}, u32[]{:S(2)}) async-start(bf16[16,80,128]{2,1,0:T(8,128)(2,1)} %broadcast_in_dim.51), calls=%async_computation.4 | async-start | bytes 655360 | tf_op jit(solution)/shard_map/all_to_all | solution.py:361

commit v5 on v4

--- a/solution.py
+++ b/solution.py
@@ -20,7 +20,6 @@
 PIECE = ROWS // GROUPS
 BH = H // GROUPS
 EXTRA_W = 2 * BH
-EXTRA_K = 16
 HALO = 16
 F32 = jnp.float32
 BF16 = jnp.bfloat16
@@ -97,7 +96,7 @@
 
     taps = spread(coef, 16)
 
-    @pl.loop(0, L)
+    @pl.loop(0, L, unroll=2)
     def _(y):
         row = pl.ds(pl.multiple_of(y * L, L), L)
         for p in range(2):
@@ -110,7 +109,7 @@
 
     taps_z = spread(coef, 32)
 
-    @pl.loop(0, L)
+    @pl.loop(0, L, unroll=2)
     def _(y):
         row = pl.ds(pl.multiple_of(y * L, L), L)
         for p in range(2):
@@ -160,7 +159,7 @@
             dse[p, y] = acc.reshape(L, 128).astype(BF16).astype(F32)
         return tuple(sums)
 
-    sums = lax.fori_loop(0, L, along_z, empty)
+    sums = lax.fori_loop(0, L, along_z, empty, unroll=2)
     for t in range(TAPS):
         acc_ref[18 + t] = sums[t]
     taps = spread(coef, 16)
@@ -178,7 +177,7 @@
             dfi[row, p * 128:(p + 1) * 128] = acc.reshape(L, 128).astype(BF16)
         return tuple(sums)
 
-    sums = lax.fori_loop(0, L, along_y, empty)
+    sums = lax.fori_loop(0, L, along_y, empty, unroll=2)
     for t in range(TAPS):
         acc_ref[9 + t] = sums[t]
     for t in range(27, 32):
@@ -195,24 +194,18 @@
     kern = lax.dot_general(
         table, jnp.sum(acc_ref[...], axis=1), (((1,), (1,)), ((), ())),
         precision=lax.Precision.HIGHEST, preferred_element_type=F32)
-    kern = jnp.concatenate([kern] * 4, axis=1)
-    sums_ref[EXTRA_W:EXTRA_W + 8, :] = jnp.where(lane // 32 == dil[3], kern, 0.0)
-
-
-def pack_out(dfi, hi_ref, lo_ref, mine, other, out_ref, weight_ref, stage):
+    sums_ref[EXTRA_W:, :] = jnp.zeros((8, 128), F32)
+    sums_ref[EXTRA_W:, 0:32] = kern
+
+
+def pack_out(dfi, hi_ref, lo_ref, out_ref, stage):
     hi, lo = hi_ref[...], lo_ref[...]
     for j in range(8):
         block = dfi[j * 128:(j + 1) * 128, :]
         out = contract(hi, block, 1, 1) + contract(lo, block, 1, 1)
         for p in range(2):
             stage[pl.ds(2 * j + p, C, stride=STRIDE), :] = out[p * 128:p * 128 + C, :]
-    weight_ref[...] = mine[0:EXTRA_W, :] + other[0:EXTRA_W, :]
-    kern = mine[EXTRA_W:, :] + other[EXTRA_W:, :]
-    high = kern.astype(BF16).astype(F32)
-    extra = jnp.concatenate([high, kern - high], axis=0).astype(BF16)
-    for g in range(GROUPS):
-        out_ref[g, 0:PIECE, :] = stage[g * PIECE:(g + 1) * PIECE, :].astype(BF16)
-        out_ref[g, PIECE:PIECE + EXTRA_K, :] = extra
+    out_ref[...] = stage[...].astype(BF16)
 
 
 BLOCK = 256
@@ -309,17 +302,17 @@
     )(scalars, rows, coef, which, eye, first, second, field)
 
 
-def run_pack_out(d_first, hi, lo, mine, other):
+def run_pack_out(d_first, hi, lo):
     return pl.pallas_call(
         pack_out,
-        out_shape=(shape(GROUPS, PIECE + EXTRA_K, 128), shape(EXTRA_W, 128, dtype=F32)),
-        in_specs=[VMEM] * 5,
-        out_specs=(VMEM,) * 2,
+        out_shape=shape(ROWS, 128),
+        in_specs=[VMEM] * 3,
+        out_specs=VMEM,
         scratch_shapes=[pltpu.VMEM((ROWS, 128), F32)],
         compiler_params=PARAMS,
         cost_estimate=estimate(10**9),
         name="pack_out",
-    )(d_first, hi, lo, mine, other)
+    )(d_first, hi, lo)
 
 
 def run_middle(rows, cot_rows, expand_weight, reduce_weight):
@@ -349,16 +342,21 @@
     return lax.all_to_all(parts, "pen", 0, 0, tiled=True)
 
 
-def from_other_core(terms):
-    if lax.axis_size("core") == 1:
-        return jnp.zeros_like(terms)
-    return lax.ppermute(terms, "core", [(0, 1), (1, 0)])
-
-
-def sum_over_chips(terms):
-    size = lax.axis_size("zh") * lax.axis_size("y")
-    parts = jnp.broadcast_to(terms.astype(BF16)[None], (size,) + terms.shape)
-    return jnp.sum(lax.all_to_all(parts, ("zh", "y"), 0, 0, tiled=True).astype(F32), axis=0)
+def shifted(terms, axis, by):
+    size = lax.axis_size(axis)
+    return lax.ppermute(terms, axis, [(i, (i + by) % size) for i in range(size)])
+
+
+def sum_over_core_and_y(terms):
+    if lax.axis_size("core") == 2:
+        terms = terms + shifted(terms, "core", 1)
+    if lax.axis_size("y") == 8:
+        terms = terms + shifted(terms, "y", 4)
+        return terms + shifted(terms, "y", 1) + shifted(terms, "y", -1) + shifted(terms, "y", 2)
+    total = terms
+    for by in range(1, lax.axis_size("y")):
+        total = total + shifted(terms, "y", by)
+    return total
 
 
 def per_device(activations, cotangent, depth_kernels, dilations, expand_weight, reduce_weight):
@@ -366,8 +364,7 @@
     own = lax.dynamic_slice_in_dim(depth_kernels, lax.axis_index("pen") * CH, CH, 1)
     coef = jnp.tile(own.transpose(0, 2, 1), (1, 1, GROUPS))
     coef = jnp.pad(coef, ((0, 0), (0, 16 - TAPS), (0, 128 - C))).reshape(48, 128)
-    group = lax.axis_index("pen").astype(jnp.int32)
-    scalars = jnp.concatenate([dilations, jnp.mod(group, 4)[None]])
+    scalars = jnp.concatenate([dilations, jnp.zeros((1,), jnp.int32)])
     steps = ((jnp.arange(TAPS, dtype=jnp.int32) - 4) * dilations[0]) % L
     which = jnp.full((256, 256), -1, jnp.int32)
     for t in range(TAPS):
@@ -381,21 +378,25 @@
     mixed = swap(mixed.reshape(GROUPS, PIECE, 128)).reshape(ROWS, 128)
     d_lines = swap(run_middle(mixed, cot_rows, expand_weight, reduce_weight))
     d_first, mine = run_conv_bwd(scalars, d_lines, coef, which, eye, first, second, field)
-    d_conv, weights = run_pack_out(d_first, hi, lo, mine, from_other_core(mine))
-    arrived = swap(d_conv)
-
-    kern = arrived[:, PIECE:, :].astype(F32).reshape(4, 4, 2, 8, 128)
-    kern = jnp.sum(kern, axis=(1, 2)).reshape(32, 128)
-    sums = sum_over_chips(jnp.concatenate([weights, kern], axis=0))
-    d_input = arrived[:, :PIECE, :].reshape(ROWS, 128)
+    d_conv = run_pack_out(d_first, hi, lo)
+    d_input = swap(d_conv.reshape(GROUPS, PIECE, 128)).reshape(ROWS, 128)
+    sums = sum_over_core_and_y(mine)
+    sums, d_input = lax.optimization_barrier((sums, d_input))
+
+    halves = lax.axis_size("zh")
+    kern = jnp.broadcast_to(sums[None, EXTRA_W:], (halves * GROUPS, 8, 128))
+    kern = lax.all_to_all(kern, ("zh", "pen"), 0, 0, tiled=True)
+    weights = sums[:EXTRA_W]
+    if halves == 2:
+        weights = weights + shifted(weights, "zh", 1)
     grad_input = from_rows((cot_rows.astype(F32) + d_input.astype(F32)).astype(BF16))
 
-    samples = lax.axis_size("zh") * lax.axis_size("y") * lax.axis_size("core")
-    sums = sums * (1.0 / math.sqrt(samples * L * L * L))
-    own_expand = sums[0:BH, 0:C].T
-    own_reduce = sums[BH:EXTRA_W, 0:C]
-    kern = sums[EXTRA_W:].reshape(4, 8, 4, 32)[:, :CH, :, :3 * TAPS]
-    kern = kern.transpose(0, 2, 1, 3).reshape(C, 3, TAPS).transpose(1, 0, 2)
+    samples = halves * lax.axis_size("y") * lax.axis_size("core")
+    scale = 1.0 / math.sqrt(samples * L * L * L)
+    own_expand = weights[0:BH, 0:C].T * scale
+    own_reduce = weights[BH:EXTRA_W, 0:C] * scale
+    kern = jnp.sum(kern.reshape(halves, GROUPS, 8, 128), axis=0) * scale
+    kern = kern[:, :CH, :3 * TAPS].reshape(C, 3, TAPS).transpose(1, 0, 2)
     return grad_input, own_expand, own_reduce, kern
 
 

time: 131 us -> 137 us (1.046)
  the two profiles are of different devices: /device:TPU:8 before, /device:TPU:32 now
where the time goes in v5:
time: 137 us
  waiting for transfers between devices  59 us (43%)
  starting transfers between devices  49.7 us (36%)
  Pallas kernels  16.3 us (12%)
  other arithmetic  7.41 us (5%)
  local copies, waits for them, and re-layouts  3.28 us (2%)
    all_to_all x4, waiting for transfers between devices, swap(): return lax.all_to_all(parts, 'pen', 0, 0, tiled=True)  34.6 us
    ppermute x6, starting transfers between devices, shifted(): lax.ppermute(terms, axis, [(i, (i + by) % size) for i in range(size)])  21.3 us
    all_to_all x4, starting transfers between devices, swap(): return lax.all_to_all(parts, 'pen', 0, 0, tiled=True)  20.7 us
    ppermute x6, waiting for transfers between devices, shifted(): lax.ppermute(terms, axis, [(i, (i + by) % size) for i in range(size)])  14 us
    all_to_all x1, waiting for transfers between devices, per_device(): kern = lax.all_to_all(kern, ('zh', 'pen'), 0, 0, tiled=True)  10.3 us
    all_to_all x1, starting transfers between devices, per_device(): kern = lax.all_to_all(kern, ('zh', 'pen'), 0, 0, tiled=True)  7.73 us
    select_n x1, other arithmetic, per_device(): which = jnp.where(delta == steps[t], t, which)  5.78 us
    pallas_call x1, Pallas kernels, run_middle(): pl.pallas_call(middle, out_shape=shape(GROUPS, PIECE + EXTRA_W, 128), in_...  4.86 us
  transfers between devices with their start and end apart: 11, of which 7 were waited for; matrix products, arithmetic and copies ran while one was open for 7% of the time, Pallas kernels for 1%

profile of v5, /device:TPU:32, one launch (start us, length us, event | category | flops | bytes accessed | tf_op | source)
XLA Modules:
  0.0 136.5 jit_solution(14695718210287106253)
XLA Ops:
  0.6 9.8 %all-to-all-start = ((bf16[16,6,8,2,128]{4,3,2,1,0:T(2,128)(2,1)}), bf16[16,6,8,2,128]{4,3,2,1,0:T(2,128)(2,1)S(1)}, u32[]{:S(2)}, u32[]{:S(2)}) async-start(bf16[16,6,8,2,128]{4,3,2,1,0:T(2,128)(2,1)} %bitcast.49), calls=%async_computation | async-start | bytes 786432 | tf_op jit(solution)/shard_map/all_to_all | solution.py:342
  12.4 11.8 %all-to-all-done = bf16[16,6,8,2,128]{4,3,2,1,0:T(2,128)(2,1)S(1)} async-done(((bf16[16,6,8,2,128]{4,3,2,1,0:T(2,128)(2,1)}), bf16[16,6,8,2,128]{4,3,2,1,0:T(2,128)(2,1)S(1)}, u32[]{:S(2)}, u32[]{:S(2)}) %all-to-all-start) | async-done | bytes 393248 | tf_op jit(solution)/shard_map/all_to_all | solution.py:342
  24.2 4.5 %conv_fwd.1 = (bf16[1536,128]{1,0:T(8,128)(2,1)}, bf16[2,1024,128]{2,1,0:T(8,128)(2,1)S(1)}, bf16[2,1024,128]{2,1,0:T(8,128)(2,1)S(1)}, bf16[256,1024]{1,0:T(8,128)(2,1)S(1)}) custom-call(s32[4]{0:T(128)S(1)} %pad_add_fusion.dil, bf16[1536,128]{1,0:T(8,128)(2,1)S(1)} %bitcast.40, f32[48,128]{1,0:T(8,128)S(1)} %bitcast.45, ...), custom_call_target="tpu_custom_call" | custom-call | flops 1000000000 | bytes 4000000 | tf_op jit(solution)/shard_map/conv_fwd/pallas_call | solution.py:277
  28.7 3.7 %all-to-all-start.1 = ((bf16[16,96,128]{2,1,0:T(8,128)(2,1)}), bf16[16,96,128]{2,1,0:T(8,128)(2,1)S(1)}, u32[]{:S(2)}, u32[]{:S(2)}) async-start(bf16[16,96,128]{2,1,0:T(8,128)(2,1)} %bitcast.8), calls=%async_computation.1 | async-start | bytes 786432 | tf_op jit(solution)/shard_map/all_to_all | solution.py:342
  32.5 12.7 %all-to-all-done.1 = bf16[16,96,128]{2,1,0:T(8,128)(2,1)S(1)} async-done(((bf16[16,96,128]{2,1,0:T(8,128)(2,1)}), bf16[16,96,128]{2,1,0:T(8,128)(2,1)S(1)}, u32[]{:S(2)}, u32[]{:S(2)}) %all-to-all-start.1) | async-done | bytes 393248 | tf_op jit(solution)/shard_map/all_to_all | solution.py:342
  45.2 4.9 %middle.1 = bf16[16,144,128]{2,1,0:T(8,128)(2,1)} custom-call(bf16[1536,128]{1,0:T(8,128)(2,1)S(1)} %bitcast.41, bf16[1536,128]{1,0:T(8,128)(2,1)S(1)} %bitcast.42, bf16[96,384]{1,0:T(8,128)(2,1)S(1)} %copy-done.3, bf16[384,96]{1,0:T(8,128)(2,1)S(1)} %copy.25.wr), custom_call_target="tpu_custom_call" | custom-call | flops 1000000000 | bytes 4000000 | tf_op jit(solution)/shard_map/middle/pallas_call | solution.py:319
  50.1 3.6 %all-to-all-start.2 = ((bf16[16,144,128]{2,1,0:T(8,128)(2,1)}), bf16[16,144,128]{2,1,0:T(8,128)(2,1)S(1)}, u32[]{:S(2)}, u32[]{:S(2)}) async-start(bf16[16,144,128]{2,1,0:T(8,128)(2,1)} %middle.1), calls=%async_computation.2 | async-start | bytes 1179648 | tf_op jit(solution)/shard_map/all_to_all | solution.py:342
  54.4 5.8 %select_select_fusion.which = s32[256,256]{1,0:T(8,128)S(1)} fusion(s32[256,256]{1,0:T(8,128)S(1)} %copy-done.2, s32[]{:T(128)} %bitcast.21, s32[]{:T(128)} %bitcast.20, s32[]{:T(128)} %bitcast.19, s32[]{:T(128)} %bitcast.18, s32[]{:T(128)} %bitcast.17, s32[]{:T(128)} %bitcast.16, s32[]{:T(128)} %bitcast.15, s32[]{:T(128)} %bitcast.14, s32[]{:T(128)} %bitcast.13), kind=kLoop, calls=%fused_computation.1 | loop fusion | flops 1179648 | bytes 524324 | tf_op jit(solution)/shard_map/jit(_where)/select_n | solution.py:371
  60.2 10.1 %all-to-all-done.2.d_ref = bf16[16,144,128]{2,1,0:T(8,128)(2,1)S(1)} async-done(((bf16[16,144,128]{2,1,0:T(8,128)(2,1)}), bf16[16,144,128]{2,1,0:T(8,128)(2,1)S(1)}, u32[]{:S(2)}, u32[]{:S(2)}) %all-to-all-start.2) | async-done | bytes 589856 | tf_op jit(solution)/shard_map/all_to_all | solution.py:342
  70.3 4.6 %conv_bwd.1 = (bf16[1024,256]{1,0:T(8,128)(2,1)S(1)}, f32[56,128]{1,0:T(8,128)S(1)}) custom-call(s32[4]{0:T(128)S(1)} %pad_add_fusion.dil, bf16[16,144,128]{2,1,0:T(8,128)(2,1)S(1)} %all-to-all-done.2.d_ref, f32[48,128]{1,0:T(8,128)S(1)} %bitcast.46, s32[256,256]{1,0:T(8,128)S(1)} %select_select_fusion.which, ...), custom_call_target="tpu_custom_call" | custom-call | flops 1000000000 | bytes 4000000 | tf_op jit(solution)/shard_map/conv_bwd/pallas_call | solution.py:291
  74.9 1.5 %pack_out.1 = bf16[1536,128]{1,0:T(8,128)(2,1)} custom-call(bf16[1024,256]{1,0:T(8,128)(2,1)S(1)} %get-tuple-element.23.dfi, bf16[256,256]{1,0:T(8,128)(2,1)S(1)} %get-tuple-element.15.hi_ref, bf16[256,256]{1,0:T(8,128)(2,1)S(1)} %get-tuple-element.16.lo_ref), custom_call_target="tpu_custom_call" | custom-call | flops 1000000000 | bytes 4000000 | tf_op jit(solution)/shard_map/pack_out/pallas_call | solution.py:306
  76.5 3.6 %all-to-all-start.3 = ((bf16[16,96,128]{2,1,0:T(8,128)(2,1)}), bf16[16,96,128]{2,1,0:T(8,128)(2,1)S(1)}, u32[]{:S(2)}, u32[]{:S(2)}) async-start(bf16[16,96,128]{2,1,0:T(8,128)(2,1)} %bitcast.22), calls=%async_computation.3 | async-start | bytes 786432 | tf_op jit(solution)/shard_map/all_to_all | solution.py:342
  80.0 1.9 %collective-permute-start = (f32[56,128]{1,0:T(8,128)S(1)}, f32[56,128]{1,0:T(8,128)S(1)}, u32[]{:S(2)}, u32[]{:S(2)}) collective-permute-start(f32[56,128]{1,0:T(8,128)S(1)} %get-tuple-element.22), channel_id=1, source_target_pairs={{0,16},{16,0},{1,17},{17,1},{2,18},{18,2},{3,19},{19,3},{4,20},{20... | collective-permute-start | bytes 86024 | tf_op jit(solution)/shard_map/ppermute | solution.py:347
  82.0 1.2 collective-permute-done
  83.1 2.0 %collective-permute-start.1 = (f32[56,128]{1,0:T(8,128)S(1)}, f32[56,128]{1,0:T(8,128)S(1)}, u32[]{:S(2)}, u32[]{:S(2)}) collective-permute-start(f32[56,128]{1,0:T(8,128)S(1)} %add.35), channel_id=1, source_target_pairs={{0,128},{32,160},{64,192},{96,224},{128,0},{160,32},{192,64},{224,... | collective-permute-start | bytes 86024 | tf_op jit(solution)/shard_map/ppermute | solution.py:347
  85.1 7.8 %collective-permute-done.1 = f32[56,128]{1,0:T(8,128)S(1)} collective-permute-done((f32[56,128]{1,0:T(8,128)S(1)}, f32[56,128]{1,0:T(8,128)S(1)}, u32[]{:S(2)}, u32[]{:S(2)}) %collective-permute-start.1) | collective-permute-done | bytes 28704 | tf_op jit(solution)/shard_map/ppermute | solution.py:347
  93.0 2.5 %collective-permute-start.4 = (f32[56,128]{1,0:T(8,128)S(1)}, f32[56,128]{1,0:T(8,128)S(1)}, u32[]{:S(2)}, u32[]{:S(2)}) collective-permute-start(f32[56,128]{1,0:T(8,128)S(1)} %add.36), channel_id=1, source_target_pairs={{0,64},{32,96},{64,128},{96,160},{128,192},{160,224},{192,0},{224,... | collective-permute-start | bytes 86024 | tf_op jit(solution)/shard_map/ppermute | solution.py:347
  95.5 4.7 %collective-permute-start.3 = (f32[56,128]{1,0:T(8,128)S(1)}, f32[56,128]{1,0:T(8,128)S(1)}, u32[]{:S(2)}, u32[]{:S(2)}) collective-permute-start(f32[56,128]{1,0:T(8,128)S(1)} %add.36), channel_id=1, source_target_pairs={{0,224},{32,0},{64,32},{96,64},{128,96},{160,128},{192,160},{224,1... | collective-permute-start | bytes 86024 | tf_op jit(solution)/shard_map/ppermute | solution.py:347
  100.2 1.9 %collective-permute-start.2 = (f32[56,128]{1,0:T(8,128)S(1)}, f32[56,128]{1,0:T(8,128)S(1)}, u32[]{:S(2)}, u32[]{:S(2)}) collective-permute-start(f32[56,128]{1,0:T(8,128)S(1)} %add.36), channel_id=1, source_target_pairs={{0,32},{32,64},{64,96},{96,128},{128,160},{160,192},{192,224},{224... | collective-permute-start | bytes 86024 | tf_op jit(solution)/shard_map/ppermute | solution.py:347
  102.1 5.0 %collective-permute-done.2 = f32[56,128]{1,0:T(8,128)S(1)} collective-permute-done((f32[56,128]{1,0:T(8,128)S(1)}, f32[56,128]{1,0:T(8,128)S(1)}, u32[]{:S(2)}, u32[]{:S(2)}) %collective-permute-start.2) | collective-permute-done | bytes 28704 | tf_op jit(solution)/shard_map/ppermute | solution.py:347
  107.2 8.2 %collective-permute-start.5 = (f32[48,128]{1,0:T(8,128)S(1)}, f32[48,128]{1,0:T(8,128)S(1)}, u32[]{:S(2)}, u32[]{:S(2)}) collective-permute-start(f32[48,128]{1,0:T(8,128)S(1)} %slice.55), channel_id=1, source_target_pairs={{0,256},{256,0},{1,257},{257,1},{2,258},{258,2},{3,259},{259,3},{4... | collective-permute-start | bytes 73736 | tf_op jit(solution)/shard_map/ppermute | solution.py:347
  115.4 0.9 add_convert_fusion
  116.9 7.7 %all-to-all-start.4 = ((f32[32,8,128]{2,1,0:T(8,128)}), f32[32,8,128]{2,1,0:T(8,128)S(1)}, u32[]{:S(2)}, u32[]{:S(2)}) async-start(f32[32,8,128]{2,1,0:T(8,128)} %broadcast_in_dim.47), calls=%async_computation.4 | async-start | bytes 262144 | tf_op jit(solution)/shard_map/all_to_all | solution.py:388
  125.3 10.3 %all-to-all-done.4 = f32[32,8,128]{2,1,0:T(8,128)S(1)} async-done(((f32[32,8,128]{2,1,0:T(8,128)}), f32[32,8,128]{2,1,0:T(8,128)S(1)}, u32[]{:S(2)}, u32[]{:S(2)}) %all-to-all-start.4) | async-done | bytes 131104 | tf_op jit(solution)/shard_map/all_to_all | solution.py:388
  (39 shorter events, 4.9 us)
Async XLA Ops:
  0.6 9.9 %copy-start = (f32[3,96,9]{1,0,2:T(4,128)S(1)}, f32[3,96,9]{1,0,2:T(4,128)}, u32[]{:S(2)}) copy-start(f32[3,96,9]{1,0,2:T(4,128)} %param.9) | copy-start | bytes 31108
  0.6 23.5 %all-to-all-start = ((bf16[16,6,8,2,128]{4,3,2,1,0:T(2,128)(2,1)}), bf16[16,6,8,2,128]{4,3,2,1,0:T(2,128)(2,1)S(1)}, u32[]{:S(2)}, u32[]{:S(2)}) async-start(bf16[16,6,8,2,128]{4,3,2,1,0:T(2,128)(2,1)} %bitcast.49), calls=%async_computation | async-start | bytes 786432 | tf_op jit(solution)/shard_map/all_to_all | solution.py:342
  10.6 1.0 copy-start.2
  10.8 0.7 copy-start.5
  28.7 3.7 %copy-start.4 = (bf16[384,96]{0,1:T(8,128)(2,1)S(1)}, bf16[384,96]{0,1:T(8,128)(2,1)}, u32[]{:S(2)}) copy-start(bf16[384,96]{0,1:T(8,128)(2,1)} %param.12) | copy-start | bytes 221188
  28.7 16.6 %copy-start.1 = (bf16[1,96,2,1024]{3,2,1,0:T(2,128)(2,1)S(1)}, bf16[1,96,2,1024]{3,2,1,0:T(2,128)(2,1)}, u32[]{:S(2)}) copy-start(bf16[1,96,2,1024]{3,2,1,0:T(2,128)(2,1)} %param.8) | copy-start | bytes 1179652
  28.7 16.6 %all-to-all-start.1 = ((bf16[16,96,128]{2,1,0:T(8,128)(2,1)}), bf16[16,96,128]{2,1,0:T(8,128)(2,1)S(1)}, u32[]{:S(2)}, u32[]{:S(2)}) async-start(bf16[16,96,128]{2,1,0:T(8,128)(2,1)} %bitcast.8), calls=%async_computation.1 | async-start | bytes 786432 | tf_op jit(solution)/shard_map/all_to_all | solution.py:342
  32.4 12.9 %copy-start.3 = (bf16[96,384]{1,0:T(8,128)(2,1)S(1)}, bf16[96,384]{1,0:T(8,128)(2,1)}, u32[]{:S(2)}) copy-start(bf16[96,384]{1,0:T(8,128)(2,1)} %we.1) | copy-start | bytes 221188
  50.1 20.2 %all-to-all-start.2 = ((bf16[16,144,128]{2,1,0:T(8,128)(2,1)}), bf16[16,144,128]{2,1,0:T(8,128)(2,1)S(1)}, u32[]{:S(2)}, u32[]{:S(2)}) async-start(bf16[16,144,128]{2,1,0:T(8,128)(2,1)} %middle.1), calls=%async_computation.2 | async-start | bytes 1179648 | tf_op jit(solution)/shard_map/all_to_all | solution.py:342
  76.5 30.7 %all-to-all-start.3 = ((bf16[16,96,128]{2,1,0:T(8,128)(2,1)}), bf16[16,96,128]{2,1,0:T(8,128)(2,1)S(1)}, u32[]{:S(2)}, u32[]{:S(2)}) async-start(bf16[16,96,128]{2,1,0:T(8,128)(2,1)} %bitcast.22), calls=%async_computation.3 | async-start | bytes 786432 | tf_op jit(solution)/shard_map/all_to_all | solution.py:342
  80.0 3.1 %collective-permute-start = (f32[56,128]{1,0:T(8,128)S(1)}, f32[56,128]{1,0:T(8,128)S(1)}, u32[]{:S(2)}, u32[]{:S(2)}) collective-permute-start(f32[56,128]{1,0:T(8,128)S(1)} %get-tuple-element.22), channel_id=1, source_target_pairs={{0,16},{16,0},{1,17},{17,1},{2,18},{18,2},{3,19},{19,3},{4,20},{20... | collective-permute-start | bytes 86024 | tf_op jit(solution)/shard_map/ppermute | solution.py:347
  83.1 9.8 %collective-permute-start.1 = (f32[56,128]{1,0:T(8,128)S(1)}, f32[56,128]{1,0:T(8,128)S(1)}, u32[]{:S(2)}, u32[]{:S(2)}) collective-permute-start(f32[56,128]{1,0:T(8,128)S(1)} %add.35), channel_id=1, source_target_pairs={{0,128},{32,160},{64,192},{96,224},{128,0},{160,32},{192,64},{224,... | collective-permute-start | bytes 86024 | tf_op jit(solution)/shard_map/ppermute | solution.py:347
  93.0 9.2 %collective-permute-start.4 = (f32[56,128]{1,0:T(8,128)S(1)}, f32[56,128]{1,0:T(8,128)S(1)}, u32[]{:S(2)}, u32[]{:S(2)}) collective-permute-start(f32[56,128]{1,0:T(8,128)S(1)} %add.36), channel_id=1, source_target_pairs={{0,64},{32,96},{64,128},{96,160},{128,192},{160,224},{192,0},{224,... | collective-permute-start | bytes 86024 | tf_op jit(solution)/shard_map/ppermute | solution.py:347
  95.5 6.6 %collective-permute-start.3 = (f32[56,128]{1,0:T(8,128)S(1)}, f32[56,128]{1,0:T(8,128)S(1)}, u32[]{:S(2)}, u32[]{:S(2)}) collective-permute-start(f32[56,128]{1,0:T(8,128)S(1)} %add.36), channel_id=1, source_target_pairs={{0,224},{32,0},{64,32},{96,64},{128,96},{160,128},{192,160},{224,1... | collective-permute-start | bytes 86024 | tf_op jit(solution)/shard_map/ppermute | solution.py:347
  100.2 7.0 %collective-permute-start.2 = (f32[56,128]{1,0:T(8,128)S(1)}, f32[56,128]{1,0:T(8,128)S(1)}, u32[]{:S(2)}, u32[]{:S(2)}) collective-permute-start(f32[56,128]{1,0:T(8,128)S(1)} %add.36), channel_id=1, source_target_pairs={{0,32},{32,64},{64,96},{96,128},{128,160},{160,192},{192,224},{224... | collective-permute-start | bytes 86024 | tf_op jit(solution)/shard_map/ppermute | solution.py:347
  107.2 17.5 %collective-permute-start.5 = (f32[48,128]{1,0:T(8,128)S(1)}, f32[48,128]{1,0:T(8,128)S(1)}, u32[]{:S(2)}, u32[]{:S(2)}) collective-permute-start(f32[48,128]{1,0:T(8,128)S(1)} %slice.55), channel_id=1, source_target_pairs={{0,256},{256,0},{1,257},{257,1},{2,258},{258,2},{3,259},{259,3},{4... | collective-permute-start | bytes 73736 | tf_op jit(solution)/shard_map/ppermute | solution.py:347
  116.9 18.7 %all-to-all-start.4 = ((f32[32,8,128]{2,1,0:T(8,128)}), f32[32,8,128]{2,1,0:T(8,128)S(1)}, u32[]{:S(2)}, u32[]{:S(2)}) async-start(f32[32,8,128]{2,1,0:T(8,128)} %broadcast_in_dim.47), calls=%async_computation.4 | async-start | bytes 262144 | tf_op jit(solution)/shard_map/all_to_all | solution.py:388

commit v6 on v4

--- a/solution.py
+++ b/solution.py
@@ -19,8 +19,6 @@
 STRIDE = 16
 PIECE = ROWS // GROUPS
 BH = H // GROUPS
-EXTRA_W = 2 * BH
-EXTRA_K = 16
 HALO = 16
 F32 = jnp.float32
 BF16 = jnp.bfloat16
@@ -67,14 +65,18 @@
     ref[p, y, HALO + L:, :] = v[:HALO, :]
 
 
-def prepare(dil, coef, delta, hi_ref, lo_ref, eye_ref):
+def prepare(dil, coef, delta, hi_ref, lo_ref, eye_ref, which_ref):
     spacing = dil[0]
     for half in range(2):
         cols = slice(half * 128, (half + 1) * 128)
         table = delta[:, cols]
         m = jnp.zeros((256, 128), F32)
+        which = jnp.full((256, 128), -1, jnp.int32)
         for t in range(TAPS):
-            m = m + jnp.where(table == (((t - 4) * spacing) & (L - 1)), coef[t:t + 1, :], 0.0)
+            here = table == (((t - 4) * spacing) & (L - 1))
+            m = m + jnp.where(here, coef[t:t + 1, :], 0.0)
+            which = jnp.where(here, t, which)
+        which_ref[:, cols] = which
         hi = m.astype(BF16)
         hi_ref[:, cols] = hi
         lo_ref[:, cols] = (m - hi.astype(F32)).astype(BF16)
@@ -97,7 +99,7 @@
 
     taps = spread(coef, 16)
 
-    @pl.loop(0, L)
+    @pl.loop(0, L, unroll=2)
     def _(y):
         row = pl.ds(pl.multiple_of(y * L, L), L)
         for p in range(2):
@@ -110,7 +112,7 @@
 
     taps_z = spread(coef, 32)
 
-    @pl.loop(0, L)
+    @pl.loop(0, L, unroll=2)
     def _(y):
         row = pl.ds(pl.multiple_of(y * L, L), L)
         for p in range(2):
@@ -126,14 +128,10 @@
     mixed_ref[...] = stage[...].astype(BF16)
 
 
-def conv_bwd(dil, d_ref, coef, which, eye_ref, first_ref, second_ref, field_ref,
-             dfi, sums_ref, stage, dmh, dse, acc_ref):
+def conv_bwd(dil, d_ref, coef, hi_ref, lo_ref, which, eye_ref, first_ref, second_ref, field_ref,
+             kept, other, out_ref, stage, dmh, dse, dfi, acc_ref):
     d1, d2 = dil[1], dil[2]
-    weights = jnp.zeros((EXTRA_W, 128), F32)
-    for g in range(GROUPS):
-        stage[g * PIECE:(g + 1) * PIECE, :] = d_ref[g, 0:PIECE, :].astype(F32)
-        weights = weights + d_ref[g, PIECE:PIECE + EXTRA_W, :].astype(F32)
-    sums_ref[0:EXTRA_W, :] = weights
+    stage[...] = d_ref[...].astype(F32)
     eye = eye_ref[...]
     for j in range(8):
         out = contract(load_field(stage, j), eye, 0, 0)
@@ -160,7 +158,7 @@
             dse[p, y] = acc.reshape(L, 128).astype(BF16).astype(F32)
         return tuple(sums)
 
-    sums = lax.fori_loop(0, L, along_z, empty)
+    sums = lax.fori_loop(0, L, along_z, empty, unroll=2)
     for t in range(TAPS):
         acc_ref[18 + t] = sums[t]
     taps = spread(coef, 16)
@@ -178,7 +176,7 @@
             dfi[row, p * 128:(p + 1) * 128] = acc.reshape(L, 128).astype(BF16)
         return tuple(sums)
 
-    sums = lax.fori_loop(0, L, along_y, empty)
+    sums = lax.fori_loop(0, L, along_y, empty, unroll=2)
     for t in range(TAPS):
         acc_ref[9 + t] = sums[t]
     for t in range(27, 32):
@@ -196,63 +194,72 @@
         table, jnp.sum(acc_ref[...], axis=1), (((1,), (1,)), ((), ())),
         precision=lax.Precision.HIGHEST, preferred_element_type=F32)
     kern = jnp.concatenate([kern] * 4, axis=1)
-    sums_ref[EXTRA_W:EXTRA_W + 8, :] = jnp.where(lane // 32 == dil[3], kern, 0.0)
-
-
-def pack_out(dfi, hi_ref, lo_ref, mine, other, out_ref, weight_ref, stage):
+    kern = jnp.where(lane // 32 == dil[3], kern, 0.0)
     hi, lo = hi_ref[...], lo_ref[...]
     for j in range(8):
         block = dfi[j * 128:(j + 1) * 128, :]
         out = contract(hi, block, 1, 1) + contract(lo, block, 1, 1)
         for p in range(2):
             stage[pl.ds(2 * j + p, C, stride=STRIDE), :] = out[p * 128:p * 128 + C, :]
-    weight_ref[...] = mine[0:EXTRA_W, :] + other[0:EXTRA_W, :]
-    kern = mine[EXTRA_W:, :] + other[EXTRA_W:, :]
-    high = kern.astype(BF16).astype(F32)
-    extra = jnp.concatenate([high, kern - high], axis=0).astype(BF16)
+    gap = jnp.zeros((BH, 128 - C), F32)
     for g in range(GROUPS):
         out_ref[g, 0:PIECE, :] = stage[g * PIECE:(g + 1) * PIECE, :].astype(BF16)
-        out_ref[g, PIECE:PIECE + EXTRA_K, :] = extra
+        own = slice(g * BH, (g + 1) * BH)
+        weights = jnp.concatenate([kept[own, :] + other[own, :], gap], axis=1)
+        out_ref[g, PIECE:, :] = jnp.concatenate([weights, kern], axis=0).astype(BF16)
 
 
 BLOCK = 256
 
 
-def middle(m_ref, c_ref, we, wr, out_ref, stage, stage_c, mix, cot, expand_ref, reduce_ref):
+def load_sites(m_ref, c_ref, stage, stage_c, mix, cot):
     stage[...] = m_ref[...].astype(F32)
     stage_c[...] = c_ref[...].astype(F32)
     for j in range(8):
         for p in range(2):
-            k = 2 * j + p
-            mix[:, k * 128:(k + 1) * 128] = pieces(stage, j, p).astype(BF16)
-            cot[:, k * 128:(k + 1) * 128] = pieces(stage_c, j, p).astype(BF16)
-    expand_ref[...] = jnp.zeros_like(expand_ref)
-    reduce_ref[...] = jnp.zeros_like(reduce_ref)
+            cols = slice((2 * j + p) * 128, (2 * j + p + 1) * 128)
+            mix[:, cols] = pieces(stage, j, p).astype(BF16)
+            cot[:, cols] = pieces(stage_c, j, p).astype(BF16)
+
+
+def activation(mb, cb, we, wr):
     root = math.sqrt(2.0 / math.pi)
-
+    pre = contract(we[...], mb, 0, 0)
+    d_hidden = contract(wr[...], cb, 1, 0)
+    square = pre * pre
+    inner = pre * (root + (root * 0.044715) * square)
+    half = 0.5 + 0.5 * jnp.tanh(inner)
+    hidden = pre * half
+    slope = half + hidden * (1.0 - half) * (2.0 * root + (6.0 * root * 0.044715) * square)
+    return hidden, (d_hidden * slope).astype(BF16)
+
+
+def middle(m_ref, c_ref, we, wr, out_ref, stage, stage_c, mix, cot):
+    load_sites(m_ref, c_ref, stage, stage_c, mix, cot)
     for b in range(2 * L * L // BLOCK):
         cols = slice(b * BLOCK, (b + 1) * BLOCK)
-        mb, cb = mix[:, cols], cot[:, cols]
-        pre = contract(we[...], mb, 0, 0)
-        d_hidden = contract(wr[...], cb, 1, 0)
-        square = pre * pre
-        inner = root * pre * (1.0 + 0.044715 * square)
-        half = 0.5 + 0.5 * jnp.tanh(inner)
-        hidden = (pre * half).astype(BF16)
-        slope = half + pre * (2.0 * half * (1.0 - half)) * (root * (1.0 + 3.0 * 0.044715 * square))
-        d_pre = (d_hidden * slope).astype(BF16)
-        reduce_ref[...] += contract(hidden, cb, 1, 1)
-        expand_ref[...] += contract(d_pre, mb, 1, 1)
+        _, d_pre = activation(mix[:, cols], cot[:, cols], we, wr)
         out = contract(we[...], d_pre, 1, 0)
         for i in range(BLOCK // 128):
             k = b * (BLOCK // 128) + i
             stage[pl.ds(k, C, stride=STRIDE), :] = out[:, i * 128:(i + 1) * 128]
-    gap = jnp.zeros((EXTRA_W, 128 - C), F32)
-    for g in range(GROUPS):
-        own = slice(g * BH, (g + 1) * BH)
-        terms = jnp.concatenate([expand_ref[own, :], reduce_ref[own, :]], axis=0)
-        out_ref[g, 0:PIECE, :] = stage[g * PIECE:(g + 1) * PIECE, :].astype(BF16)
-        out_ref[g, PIECE:PIECE + EXTRA_W, :] = jnp.concatenate([terms, gap], axis=1).astype(BF16)
+    out_ref[...] = stage[...].astype(BF16)
+
+
+def weight_terms(core, m_ref, c_ref, we, wr, keep_ref, send_ref, stage, stage_c, mix, cot,
+                 expand_ref, reduce_ref):
+    load_sites(m_ref, c_ref, stage, stage_c, mix, cot)
+    expand_ref[...] = jnp.zeros_like(expand_ref)
+    reduce_ref[...] = jnp.zeros_like(reduce_ref)
+    for b in range(2 * L * L // BLOCK):
+        cols = slice(b * BLOCK, (b + 1) * BLOCK)
+        mb, cb = mix[:, cols], cot[:, cols]
+        hidden, d_pre = activation(mb, cb, we, wr)
+        reduce_ref[...] += contract(hidden.astype(BF16), cb, 1, 1)
+        expand_ref[...] += contract(d_pre, mb, 1, 1)
+    expand, reduce = expand_ref[...], reduce_ref[...]
+    keep_ref[...] = jnp.where(core[0] == 0, expand, reduce)
+    send_ref[...] = jnp.where(core[0] == 0, reduce, expand)
 
 
 VMEM = pl.BlockSpec(memory_space=pltpu.VMEM)
@@ -271,9 +278,9 @@
 def run_prepare(scalars, coef, delta):
     return pl.pallas_call(
         prepare,
-        out_shape=(shape(256, 256),) * 3,
+        out_shape=(shape(256, 256),) * 3 + (shape(256, 256, dtype=jnp.int32),),
         in_specs=[SMEM] + [VMEM] * 2,
-        out_specs=(VMEM,) * 3,
+        out_specs=(VMEM,) * 4,
         compiler_params=PARAMS,
         cost_estimate=estimate(10**8),
         name="prepare",
@@ -294,47 +301,51 @@
     )(scalars, rows, coef, hi, lo, eye)
 
 
-def run_conv_bwd(scalars, rows, coef, which, eye, first, second, field):
+def run_conv_bwd(scalars, *arrays):
     return pl.pallas_call(
         conv_bwd,
-        out_shape=(shape(1024, 256), shape(EXTRA_W + 8, 128, dtype=F32)),
-        in_specs=[SMEM] + [VMEM] * 7,
-        out_specs=(VMEM,) * 2,
+        out_shape=shape(GROUPS, PIECE + BH + 8, 128),
+        in_specs=[SMEM] + [VMEM] * len(arrays),
+        out_specs=VMEM,
         scratch_shapes=[pltpu.VMEM((ROWS, 128), F32),
                         pltpu.VMEM((2, L, L + 2 * HALO, 128), F32),
-                        pltpu.VMEM((2, L, L, 128), F32), pltpu.VMEM((32, 8, 128), F32)],
+                        pltpu.VMEM((2, L, L, 128), F32), pltpu.VMEM((1024, 256), BF16),
+                        pltpu.VMEM((32, 8, 128), F32)],
         compiler_params=PARAMS,
         cost_estimate=estimate(10**9),
         name="conv_bwd",
-    )(scalars, rows, coef, which, eye, first, second, field)
-
-
-def run_pack_out(d_first, hi, lo, mine, other):
+    )(scalars, *arrays)
+
+
+def site_scratch():
+    return [pltpu.VMEM((ROWS, 128), F32), pltpu.VMEM((ROWS, 128), F32),
+            pltpu.VMEM((C, 2048), BF16), pltpu.VMEM((C, 2048), BF16)]
+
+
+def run_middle(*arrays):
     return pl.pallas_call(
-        pack_out,
-        out_shape=(shape(GROUPS, PIECE + EXTRA_K, 128), shape(EXTRA_W, 128, dtype=F32)),
-        in_specs=[VMEM] * 5,
-        out_specs=(VMEM,) * 2,
-        scratch_shapes=[pltpu.VMEM((ROWS, 128), F32)],
+        middle,
+        out_shape=shape(ROWS, 128),
+        in_specs=[VMEM] * 4,
+        out_specs=VMEM,
+        scratch_shapes=site_scratch(),
         compiler_params=PARAMS,
         cost_estimate=estimate(10**9),
-        name="pack_out",
-    )(d_first, hi, lo, mine, other)
-
-
-def run_middle(rows, cot_rows, expand_weight, reduce_weight):
+        name="middle",
+    )(*arrays)
+
+
+def run_weight_terms(core, *arrays):
     return pl.pallas_call(
-        middle,
-        out_shape=shape(GROUPS, PIECE + EXTRA_W, 128),
-        in_specs=[VMEM] * 4,
-        out_specs=VMEM,
-        scratch_shapes=[pltpu.VMEM((ROWS, 128), F32), pltpu.VMEM((ROWS, 128), F32),
-                        pltpu.VMEM((C, 2048), BF16), pltpu.VMEM((C, 2048), BF16),
-                        pltpu.VMEM((H, C), F32), pltpu.VMEM((H, C), F32)],
+        weight_terms,
+        out_shape=(shape(H, C, dtype=F32),) * 2,
+        in_specs=[SMEM] + [VMEM] * 4,
+        out_specs=(VMEM,) * 2,
+        scratch_shapes=site_scratch() + [pltpu.VMEM((H, C), F32)] * 2,
         compiler_params=PARAMS,
-        cost_estimate=pl.CostEstimate(flops=10**9, bytes_accessed=4 * 10**6, transcendentals=10**6),
-        name="middle",
-    )(rows, cot_rows, expand_weight, reduce_weight)
+        cost_estimate=estimate(10**9),
+        name="weight_terms",
+    )(core, *arrays)
 
 
 def to_rows(field):
@@ -350,8 +361,6 @@
 
 
 def from_other_core(terms):
-    if lax.axis_size("core") == 1:
-        return jnp.zeros_like(terms)
     return lax.ppermute(terms, "core", [(0, 1), (1, 0)])
 
 
@@ -367,41 +376,42 @@
     coef = jnp.tile(own.transpose(0, 2, 1), (1, 1, GROUPS))
     coef = jnp.pad(coef, ((0, 0), (0, 16 - TAPS), (0, 128 - C))).reshape(48, 128)
     group = lax.axis_index("pen").astype(jnp.int32)
+    core = lax.axis_index("core").astype(jnp.int32)
     scalars = jnp.concatenate([dilations, jnp.mod(group, 4)[None]])
-    steps = ((jnp.arange(TAPS, dtype=jnp.int32) - 4) * dilations[0]) % L
-    which = jnp.full((256, 256), -1, jnp.int32)
-    for t in range(TAPS):
-        which = jnp.where(delta == steps[t], t, which)
 
     start = activations.reshape(GROUPS, CH, 2, 8, 128).transpose(0, 1, 3, 2, 4)
     lines = swap(start).reshape(ROWS, 128)
-    hi, lo, eye = run_prepare(scalars, coef, delta)
+    hi, lo, eye, which = run_prepare(scalars, coef, delta)
     mixed, first, second, field = run_conv_fwd(scalars, lines, coef, hi, lo, eye)
     cot_rows = to_rows(cotangent)
     mixed = swap(mixed.reshape(GROUPS, PIECE, 128)).reshape(ROWS, 128)
-    d_lines = swap(run_middle(mixed, cot_rows, expand_weight, reduce_weight))
-    d_first, mine = run_conv_bwd(scalars, d_lines, coef, which, eye, first, second, field)
-    d_conv, weights = run_pack_out(d_first, hi, lo, mine, from_other_core(mine))
+    d_mixed = run_middle(mixed, cot_rows, expand_weight, reduce_weight)
+    d_lines = swap(d_mixed.reshape(GROUPS, PIECE, 128)).reshape(ROWS, 128)
+    keep, send = run_weight_terms(core[None], mixed, cot_rows, expand_weight, reduce_weight)
+    d_conv = run_conv_bwd(scalars, d_lines, coef, hi, lo, which, eye, first, second, field,
+                          keep, from_other_core(send))
     arrived = swap(d_conv)
 
-    kern = arrived[:, PIECE:, :].astype(F32).reshape(4, 4, 2, 8, 128)
-    kern = jnp.sum(kern, axis=(1, 2)).reshape(32, 128)
-    sums = sum_over_chips(jnp.concatenate([weights, kern], axis=0))
+    weights = jnp.sum(arrived[:, PIECE:PIECE + BH, :].astype(F32), axis=0)
+    kern = arrived[:, PIECE + BH:, :].astype(F32).reshape(4, 4, 8, 128)
+    kern = jnp.sum(kern, axis=1)[:, :CH, :].reshape(4 * CH, 128)
+    mine = sum_over_chips(jnp.concatenate([weights, kern], axis=0))
     d_input = arrived[:, :PIECE, :].reshape(ROWS, 128)
     grad_input = from_rows((cot_rows.astype(F32) + d_input.astype(F32)).astype(BF16))
 
     samples = lax.axis_size("zh") * lax.axis_size("y") * lax.axis_size("core")
-    sums = sums * (1.0 / math.sqrt(samples * L * L * L))
-    own_expand = sums[0:BH, 0:C].T
-    own_reduce = sums[BH:EXTRA_W, 0:C]
-    kern = sums[EXTRA_W:].reshape(4, 8, 4, 32)[:, :CH, :, :3 * TAPS]
+    mine = mine * (1.0 / math.sqrt(samples * L * L * L))
+    other = from_other_core(mine)
+    own_expand = jnp.where(core == 0, mine, other)[0:BH, 0:C].T
+    own_reduce = jnp.where(core == 0, other, mine)[0:BH, 0:C]
+    kern = (mine + other)[BH:].reshape(4, CH, 4, 32)[:, :, :, :3 * TAPS]
     kern = kern.transpose(0, 2, 1, 3).reshape(C, 3, TAPS).transpose(1, 0, 2)
     return grad_input, own_expand, own_reduce, kern
 
 
 def solution(mesh):
     samp = mesh.devices.shape[0]
-    split = (2, samp // 4, 2) if samp % 4 == 0 else (1, samp, 1)
+    split = (2, samp // 4, 2)
     fine = Mesh(mesh.devices.reshape(*split, GROUPS), (*SAMP, "pen"))
     field = P(SAMP, None, "pen", None)
     return jax.shard_map(

time: 131 us -> 125 us (0.954)
  the two profiles are of different devices: /device:TPU:8 before, /device:TPU:1 now
where the time goes in v6:
time: 125 us
  starting transfers between devices  39.4 us (32%)
  waiting for transfers between devices  38.9 us (31%)
  blocking collectives  19.6 us (16%)
  Pallas kernels  18.4 us (15%)
  local copies, waits for them, and re-layouts  5.47 us (4%)
  other arithmetic  1.92 us (2%)
    all_to_all x3, waiting for transfers between devices, swap(): return lax.all_to_all(parts, 'pen', 0, 0, tiled=True)  26.3 us
    all_to_all x1, blocking collectives, swap(): return lax.all_to_all(parts, 'pen', 0, 0, tiled=True)  19.6 us
    all_to_all x3, starting transfers between devices, swap(): return lax.all_to_all(parts, 'pen', 0, 0, tiled=True)  17.6 us
    all_to_all x1, starting transfers between devices, sum_over_chips(): lax.all_to_all(parts, ('zh', 'y'), 0, 0, tiled=True).astype(F32)  12.7 us
    all_to_all x1, waiting for transfers between devices, sum_over_chips(): lax.all_to_all(parts, ('zh', 'y'), 0, 0, tiled=True).astype(F32)  11.6 us
    ppermute x2, starting transfers between devices, from_other_core(): return lax.ppermute(terms, 'core', [(0, 1), (1, 0)])  9.06 us
    pallas_call x1, Pallas kernels, run_conv_bwd(): pl.pallas_call(conv_bwd, out_shape=shape(GROUPS, PIECE + BH + 8, 128), in...  5.39 us
    pallas_call x1, Pallas kernels, run_conv_fwd(): pl.pallas_call(conv_fwd, out_shape=(shape(ROWS, 128), shape(2, 1024, 128)...  4.51 us
  transfers between devices with their start and end apart: 6, of which 5 were waited for; matrix products, arithmetic and copies ran while one was open for 1% of the time, Pallas kernels for 3%

profile of v6, /device:TPU:1, one launch (start us, length us, event | category | flops | bytes accessed | tf_op | source)
XLA Modules:
  0.0 124.6 jit_solution(11630608081801942568)
XLA Ops:
  0.6 10.4 %all-to-all-start = ((bf16[16,6,8,2,128]{4,3,2,1,0:T(2,128)(2,1)}), bf16[16,6,8,2,128]{4,3,2,1,0:T(2,128)(2,1)S(1)}, u32[]{:S(2)}, u32[]{:S(2)}) async-start(bf16[16,6,8,2,128]{4,3,2,1,0:T(2,128)(2,1)} %bitcast.50), calls=%async_computation | async-start | bytes 786432 | tf_op jit(solution)/shard_map/all_to_all | solution.py:360
  11.4 0.6 copy-done.9
  12.1 0.9 prepare.1
  13.0 10.9 %all-to-all-done = bf16[16,6,8,2,128]{4,3,2,1,0:T(2,128)(2,1)S(1)} async-done(((bf16[16,6,8,2,128]{4,3,2,1,0:T(2,128)(2,1)}), bf16[16,6,8,2,128]{4,3,2,1,0:T(2,128)(2,1)S(1)}, u32[]{:S(2)}, u32[]{:S(2)}) %all-to-all-start) | async-done | bytes 393248 | tf_op jit(solution)/shard_map/all_to_all | solution.py:360
  24.0 4.5 %conv_fwd.1 = (bf16[1536,128]{1,0:T(8,128)(2,1)}, bf16[2,1024,128]{2,1,0:T(8,128)(2,1)S(1)}, bf16[2,1024,128]{2,1,0:T(8,128)(2,1)S(1)}, bf16[256,1024]{1,0:T(8,128)(2,1)S(1)}) custom-call(s32[4]{0:T(128)S(1)} %pad_add_fusion.dil, bf16[1536,128]{1,0:T(8,128)(2,1)S(1)} %bitcast.39, f32[48,128]{1,0:T(8,128)S(1)} %bitcast.46, ...), custom_call_target="tpu_custom_call" | custom-call | flops 1000000000 | bytes 4000000 | tf_op jit(solution)/shard_map/conv_fwd/pallas_call | solution.py:291
  28.5 3.7 %all-to-all-start.1 = ((bf16[16,96,128]{2,1,0:T(8,128)(2,1)}), bf16[16,96,128]{2,1,0:T(8,128)(2,1)S(1)}, u32[]{:S(2)}, u32[]{:S(2)}) async-start(bf16[16,96,128]{2,1,0:T(8,128)(2,1)} %bitcast.8), calls=%async_computation.1 | async-start | bytes 786432 | tf_op jit(solution)/shard_map/all_to_all | solution.py:360
  32.3 12.3 %all-to-all-done.1 = bf16[16,96,128]{2,1,0:T(8,128)(2,1)S(1)} async-done(((bf16[16,96,128]{2,1,0:T(8,128)(2,1)}), bf16[16,96,128]{2,1,0:T(8,128)(2,1)S(1)}, u32[]{:S(2)}, u32[]{:S(2)}) %all-to-all-start.1) | async-done | bytes 393248 | tf_op jit(solution)/shard_map/all_to_all | solution.py:360
  44.6 4.2 %middle.1 = bf16[1536,128]{1,0:T(8,128)(2,1)} custom-call(bf16[1536,128]{1,0:T(8,128)(2,1)S(1)} %bitcast.41, bf16[1536,128]{1,0:T(8,128)(2,1)S(1)} %bitcast.43, bf16[96,384]{1,0:T(8,128)(2,1)S(1)} %copy-done.2, bf16[384,96]{1,0:T(8,128)(2,1)S(1)} %copy.28.wr), custom_call_target="tpu_custom_call" | custom-call | flops 1000000000 | bytes 4000000 | tf_op jit(solution)/shard_map/middle/pallas_call | solution.py:326
  48.8 3.6 %all-to-all-start.2 = ((bf16[16,96,128]{2,1,0:T(8,128)(2,1)}), bf16[16,96,128]{2,1,0:T(8,128)(2,1)S(1)}, u32[]{:S(2)}, u32[]{:S(2)}) async-start(bf16[16,96,128]{2,1,0:T(8,128)(2,1)} %bitcast.12), calls=%async_computation.2 | async-start | bytes 786432 | tf_op jit(solution)/shard_map/all_to_all | solution.py:360
  52.4 3.4 %weight_terms.1 = (f32[384,96]{1,0:T(8,128)S(1)}, f32[384,96]{1,0:T(8,128)S(1)}) custom-call(s32[1]{0:T(128)} %bitcast.14.core, bf16[1536,128]{1,0:T(8,128)(2,1)S(1)} %bitcast.42, bf16[1536,128]{1,0:T(8,128)(2,1)S(1)} %bitcast.44, bf16[96,384]{1,0:T(8,128)(2,1)S(1)} %copy-done.2, bf16[384,96]{1,0:T(8,128)(2,1)S(1)} %copy.28.wr), custom_call_target="tpu_custom_call" | custom-call | flops 1000000000 | bytes 4000000 | tf_op jit(solution)/shard_map/weight_terms/pallas_call | solution.py:339
  55.8 0.7 copy-done.6
  56.5 4.1 %collective-permute-start = (f32[384,96]{1,0:T(8,128)S(1)}, f32[384,96]{1,0:T(8,128)S(1)}, u32[]{:S(2)}, u32[]{:S(2)}) collective-permute-start(f32[384,96]{1,0:T(8,128)S(1)} %get-tuple-element.23), channel_id=1, source_target_pairs={{0,16},{16,0},{1,17},{17,1},{2,18},{18,2},{3,19},{19,3},{4,20},{20... | collective-permute-start | bytes 442376 | tf_op jit(solution)/shard_map/ppermute | solution.py:364
  60.6 1.0 collective-permute-done.other
  61.6 3.0 %all-to-all-done.2 = bf16[16,96,128]{2,1,0:T(8,128)(2,1)S(1)} async-done(((bf16[16,96,128]{2,1,0:T(8,128)(2,1)}), bf16[16,96,128]{2,1,0:T(8,128)(2,1)S(1)}, u32[]{:S(2)}, u32[]{:S(2)}) %all-to-all-start.2) | async-done | bytes 393248 | tf_op jit(solution)/shard_map/all_to_all | solution.py:360
  64.7 0.9 copy-done.5
  65.6 0.9 copy-done.7
  66.5 5.4 %conv_bwd.1 = bf16[16,128,128]{2,1,0:T(8,128)(2,1)S(1)} custom-call(s32[4]{0:T(128)S(1)} %pad_add_fusion.dil, bf16[1536,128]{1,0:T(8,128)(2,1)S(1)} %bitcast.40, f32[48,128]{1,0:T(8,128)S(1)} %bitcast.47, bf16[256,256]{1,0:T(8,128)(2,1)S(1)} %get-tuple-element.14.hi_ref, bf16[256,256]{1,0:T(8,128)(2,1)S(1)} %get-tuple-element.15.lo_ref, ...), custom_call_target="tpu_custom_call" | custom-call | flops 1000000000 | bytes 4000000 | tf_op jit(solution)/shard_map/conv_bwd/pallas_call | solution.py:305
  71.9 19.6 %all_to_all.25 = bf16[16,128,128]{2,1,0:T(8,128)(2,1)S(1)} all-to-all(bf16[16,128,128]{2,1,0:T(8,128)(2,1)S(1)} %conv_bwd.1), channel_id=1, replica_groups=mesh['zh'=2,'y'=8,'core'=2,'pen'=16] {'pen'}, dimensions={0} | all-to-all | bytes 1048576 | tf_op jit(solution)/shard_map/all_to_all | solution.py:360
  91.6 0.7 broadcast_in_dim.14
  92.3 12.7 %all-to-all-start.4 = ((bf16[16,48,128]{2,1,0:T(8,128)(2,1)}), bf16[16,48,128]{2,1,0:T(8,128)(2,1)S(1)}, u32[]{:S(2)}, u32[]{:S(2)}) async-start(bf16[16,48,128]{2,1,0:T(8,128)(2,1)} %broadcast_in_dim.14), calls=%async_computation.4 | async-start | bytes 393216 | tf_op jit(solution)/shard_map/all_to_all | solution.py:370
  105.0 11.6 %all-to-all-done.4 = bf16[16,48,128]{2,1,0:T(8,128)(2,1)S(1)} async-done(((bf16[16,48,128]{2,1,0:T(8,128)(2,1)}), bf16[16,48,128]{2,1,0:T(8,128)(2,1)S(1)}, u32[]{:S(2)}, u32[]{:S(2)}) %all-to-all-start.4) | async-done | bytes 196640 | tf_op jit(solution)/shard_map/all_to_all | solution.py:370
  116.6 5.0 %collective-permute-start.1 = (f32[48,128]{1,0:T(8,128)S(1)}, f32[48,128]{1,0:T(8,128)S(1)}, u32[]{:S(2)}, u32[]{:S(2)}) collective-permute-start(f32[48,128]{1,0:T(8,128)S(1)} %broadcast_multiply_fusion), channel_id=1, source_target_pairs={{0,16},{16,0},{1,17},{17,1},{2,18},{18,2},{3,19},{19,3},{4,20},{20... | collective-permute-start | bytes 73736 | tf_op jit(solution)/shard_map/ppermute | solution.py:364
  121.6 1.2 fusion.1
  123.3 0.6 copy.32
  (36 shorter events, 1.8 us)
Async XLA Ops:
  0.6 10.4 %copy-start = (f32[3,96,9]{1,0,2:T(4,128)S(1)}, f32[3,96,9]{1,0,2:T(4,128)}, u32[]{:S(2)}) copy-start(f32[3,96,9]{1,0,2:T(4,128)} %param.9) | copy-start | bytes 31108
  0.6 23.3 %all-to-all-start = ((bf16[16,6,8,2,128]{4,3,2,1,0:T(2,128)(2,1)}), bf16[16,6,8,2,128]{4,3,2,1,0:T(2,128)(2,1)S(1)}, u32[]{:S(2)}, u32[]{:S(2)}) async-start(bf16[16,6,8,2,128]{4,3,2,1,0:T(2,128)(2,1)} %bitcast.50), calls=%async_computation | async-start | bytes 786432 | tf_op jit(solution)/shard_map/all_to_all | solution.py:360
  11.1 1.0 copy-start.3
  11.3 0.7 copy-start.9
  13.0 15.5 %copy-start.4 = (bf16[256,256]{1,0:T(8,128)(2,1)}, bf16[256,256]{1,0:T(8,128)(2,1)S(1)}, u32[]{:S(2)}) copy-start(bf16[256,256]{1,0:T(8,128)(2,1)S(1)} %get-tuple-element.16.eye_ref) | copy-start | bytes 393220
  28.5 3.7 %copy-start.8 = (bf16[384,96]{0,1:T(8,128)(2,1)S(1)}, bf16[384,96]{0,1:T(8,128)(2,1)}, u32[]{:S(2)}) copy-start(bf16[384,96]{0,1:T(8,128)(2,1)} %param.12) | copy-start | bytes 221188
  28.5 16.1 %copy-start.1 = (bf16[1,96,2,1024]{3,2,1,0:T(2,128)(2,1)S(1)}, bf16[1,96,2,1024]{3,2,1,0:T(2,128)(2,1)}, u32[]{:S(2)}) copy-start(bf16[1,96,2,1024]{3,2,1,0:T(2,128)(2,1)} %param.8) | copy-start | bytes 1179652
  28.5 16.1 %all-to-all-start.1 = ((bf16[16,96,128]{2,1,0:T(8,128)(2,1)}), bf16[16,96,128]{2,1,0:T(8,128)(2,1)S(1)}, u32[]{:S(2)}, u32[]{:S(2)}) async-start(bf16[16,96,128]{2,1,0:T(8,128)(2,1)} %bitcast.8), calls=%async_computation.1 | async-start | bytes 786432 | tf_op jit(solution)/shard_map/all_to_all | solution.py:360
  32.2 12.4 %copy-start.2 = (bf16[96,384]{1,0:T(8,128)(2,1)S(1)}, bf16[96,384]{1,0:T(8,128)(2,1)}, u32[]{:S(2)}) copy-start(bf16[96,384]{1,0:T(8,128)(2,1)} %we.3) | copy-start | bytes 221188
  48.8 15.9 %all-to-all-start.2 = ((bf16[16,96,128]{2,1,0:T(8,128)(2,1)}), bf16[16,96,128]{2,1,0:T(8,128)(2,1)S(1)}, u32[]{:S(2)}, u32[]{:S(2)}) async-start(bf16[16,96,128]{2,1,0:T(8,128)(2,1)} %bitcast.12), calls=%async_computation.2 | async-start | bytes 786432 | tf_op jit(solution)/shard_map/all_to_all | solution.py:360
  55.8 0.7 copy-start.6
  56.5 5.1 %collective-permute-start = (f32[384,96]{1,0:T(8,128)S(1)}, f32[384,96]{1,0:T(8,128)S(1)}, u32[]{:S(2)}, u32[]{:S(2)}) collective-permute-start(f32[384,96]{1,0:T(8,128)S(1)} %get-tuple-element.23), channel_id=1, source_target_pairs={{0,16},{16,0},{1,17},{17,1},{2,18},{18,2},{3,19},{19,3},{4,20},{20... | collective-permute-start | bytes 442376 | tf_op jit(solution)/shard_map/ppermute | solution.py:364
  64.7 0.9 copy-start.5
  65.6 0.9 copy-start.7
  92.3 24.3 %all-to-all-start.4 = ((bf16[16,48,128]{2,1,0:T(8,128)(2,1)}), bf16[16,48,128]{2,1,0:T(8,128)(2,1)S(1)}, u32[]{:S(2)}, u32[]{:S(2)}) async-start(bf16[16,48,128]{2,1,0:T(8,128)(2,1)} %broadcast_in_dim.14), calls=%async_computation.4 | async-start | bytes 393216 | tf_op jit(solution)/shard_map/all_to_all | solution.py:370
  116.6 6.2 %collective-permute-start.1 = (f32[48,128]{1,0:T(8,128)S(1)}, f32[48,128]{1,0:T(8,128)S(1)}, u32[]{:S(2)}, u32[]{:S(2)}) collective-permute-start(f32[48,128]{1,0:T(8,128)S(1)} %broadcast_multiply_fusion), channel_id=1, source_target_pairs={{0,16},{16,0},{1,17},{17,1},{2,18},{18,2},{3,19},{19,3},{4,20},{20... | collective-permute-start | bytes 73736 | tf_op jit(solution)/shard_map/ppermute | solution.py:364

commit v7 on v6

--- a/solution.py
+++ b/solution.py
@@ -71,12 +71,12 @@
         cols = slice(half * 128, (half + 1) * 128)
         table = delta[:, cols]
         m = jnp.zeros((256, 128), F32)
-        which = jnp.full((256, 128), -1, jnp.int32)
+        which = jnp.full((256, 128), -1.0, F32)
         for t in range(TAPS):
             here = table == (((t - 4) * spacing) & (L - 1))
             m = m + jnp.where(here, coef[t:t + 1, :], 0.0)
-            which = jnp.where(here, t, which)
-        which_ref[:, cols] = which
+            which = jnp.where(here, float(t), which)
+        which_ref[:, cols] = which.astype(BF16)
         hi = m.astype(BF16)
         hi_ref[:, cols] = hi
         lo_ref[:, cols] = (m - hi.astype(F32)).astype(BF16)
@@ -99,7 +99,7 @@
 
     taps = spread(coef, 16)
 
-    @pl.loop(0, L, unroll=2)
+    @pl.loop(0, L, unroll=4)
     def _(y):
         row = pl.ds(pl.multiple_of(y * L, L), L)
         for p in range(2):
@@ -112,7 +112,7 @@
 
     taps_z = spread(coef, 32)
 
-    @pl.loop(0, L, unroll=2)
+    @pl.loop(0, L, unroll=4)
     def _(y):
         row = pl.ds(pl.multiple_of(y * L, L), L)
         for p in range(2):
@@ -128,11 +128,11 @@
     mixed_ref[...] = stage[...].astype(BF16)
 
 
-def conv_bwd(dil, d_ref, coef, hi_ref, lo_ref, which, eye_ref, first_ref, second_ref, field_ref,
-             kept, other, out_ref, stage, dmh, dse, dfi, acc_ref):
+def conv_bwd(dil, d_ref, coef, hi_ref, lo_ref, which, first_ref, second_ref, field_ref,
+             terms, out_ref, stage, dmh, dse, dfi, acc_ref):
     d1, d2 = dil[1], dil[2]
     stage[...] = d_ref[...].astype(F32)
-    eye = eye_ref[...]
+    eye = jnp.where(which[...].astype(F32) == 4.0, 1.0, 0.0).astype(BF16)
     for j in range(8):
         out = contract(load_field(stage, j), eye, 0, 0)
         for p in range(2):
@@ -158,7 +158,7 @@
             dse[p, y] = acc.reshape(L, 128).astype(BF16).astype(F32)
         return tuple(sums)
 
-    sums = lax.fori_loop(0, L, along_z, empty, unroll=2)
+    sums = lax.fori_loop(0, L, along_z, empty, unroll=4)
     for t in range(TAPS):
         acc_ref[18 + t] = sums[t]
     taps = spread(coef, 16)
@@ -176,15 +176,16 @@
             dfi[row, p * 128:(p + 1) * 128] = acc.reshape(L, 128).astype(BF16)
         return tuple(sums)
 
-    sums = lax.fori_loop(0, L, along_y, empty, unroll=2)
+    sums = lax.fori_loop(0, L, along_y, empty, unroll=4)
     for t in range(TAPS):
         acc_ref[9 + t] = sums[t]
     for t in range(27, 32):
         acc_ref[t] = jnp.zeros((8, 128), F32)
 
     cross = contract(field_ref[...], dfi[...], 1, 0)
+    tap_of = which[...].astype(F32)
     for t in range(TAPS):
-        keep = jnp.where(which[...] == t, cross, 0.0)
+        keep = jnp.where(tap_of == float(t), cross, 0.0)
         keep = jnp.sum(keep.reshape(32, 8, 256), axis=0)
         acc_ref[t] = keep[:, :128] + keep[:, 128:]
     lane = lax.broadcasted_iota(jnp.int32, (8, 128), 1)
@@ -205,21 +206,19 @@
     for g in range(GROUPS):
         out_ref[g, 0:PIECE, :] = stage[g * PIECE:(g + 1) * PIECE, :].astype(BF16)
         own = slice(g * BH, (g + 1) * BH)
-        weights = jnp.concatenate([kept[own, :] + other[own, :], gap], axis=1)
+        weights = jnp.concatenate([terms[own, :], gap], axis=1)
         out_ref[g, PIECE:, :] = jnp.concatenate([weights, kern], axis=0).astype(BF16)
 
 
-BLOCK = 256
-
-
-def load_sites(m_ref, c_ref, stage, stage_c, mix, cot):
-    stage[...] = m_ref[...].astype(F32)
-    stage_c[...] = c_ref[...].astype(F32)
+BLOCK = 512
+
+
+def by_site(rows_ref, stage, out):
+    stage[...] = rows_ref[...].astype(F32)
     for j in range(8):
         for p in range(2):
             cols = slice((2 * j + p) * 128, (2 * j + p + 1) * 128)
-            mix[:, cols] = pieces(stage, j, p).astype(BF16)
-            cot[:, cols] = pieces(stage_c, j, p).astype(BF16)
+            out[:, cols] = pieces(stage, j, p).astype(BF16)
 
 
 def activation(mb, cb, we, wr):
@@ -235,7 +234,8 @@
 
 
 def middle(m_ref, c_ref, we, wr, out_ref, stage, stage_c, mix, cot):
-    load_sites(m_ref, c_ref, stage, stage_c, mix, cot)
+    by_site(m_ref, stage, mix)
+    by_site(c_ref, stage_c, cot)
     for b in range(2 * L * L // BLOCK):
         cols = slice(b * BLOCK, (b + 1) * BLOCK)
         _, d_pre = activation(mix[:, cols], cot[:, cols], we, wr)
@@ -248,7 +248,8 @@
 
 def weight_terms(core, m_ref, c_ref, we, wr, keep_ref, send_ref, stage, stage_c, mix, cot,
                  expand_ref, reduce_ref):
-    load_sites(m_ref, c_ref, stage, stage_c, mix, cot)
+    by_site(m_ref, stage, mix)
+    by_site(c_ref, stage_c, cot)
     expand_ref[...] = jnp.zeros_like(expand_ref)
     reduce_ref[...] = jnp.zeros_like(reduce_ref)
     for b in range(2 * L * L // BLOCK):
@@ -278,7 +279,7 @@
 def run_prepare(scalars, coef, delta):
     return pl.pallas_call(
         prepare,
-        out_shape=(shape(256, 256),) * 3 + (shape(256, 256, dtype=jnp.int32),),
+        out_shape=(shape(256, 256),) * 4,
         in_specs=[SMEM] + [VMEM] * 2,
         out_specs=(VMEM,) * 4,
         compiler_params=PARAMS,
@@ -388,8 +389,8 @@
     d_mixed = run_middle(mixed, cot_rows, expand_weight, reduce_weight)
     d_lines = swap(d_mixed.reshape(GROUPS, PIECE, 128)).reshape(ROWS, 128)
     keep, send = run_weight_terms(core[None], mixed, cot_rows, expand_weight, reduce_weight)
-    d_conv = run_conv_bwd(scalars, d_lines, coef, hi, lo, which, eye, first, second, field,
-                          keep, from_other_core(send))
+    terms = keep + from_other_core(send)
+    d_conv = run_conv_bwd(scalars, d_lines, coef, hi, lo, which, first, second, field, terms)
     arrived = swap(d_conv)
 
     weights = jnp.sum(arrived[:, PIECE:PIECE + BH, :].astype(F32), axis=0)

time: 125 us -> 122 us (0.976)
  local copies, waits for them, and re-layouts: 5.47 us -> 2.96 us
    unnamed x24 -> x16, local copies, waits for them, and re-layouts: 4.18 us -> 1.67 us
where the time goes in v7:
time: 122 us
  waiting for transfers between devices  39.8 us (33%)
  starting transfers between devices  39.3 us (32%)
  blocking collectives  19.3 us (16%)
  Pallas kernels  17.6 us (14%)
  local copies, waits for them, and re-layouts  2.96 us (2%)
  other arithmetic  1.95 us (2%)
    all_to_all x3, waiting for transfers between devices, swap(): return lax.all_to_all(parts, 'pen', 0, 0, tiled=True)  27.1 us
    all_to_all x1, blocking collectives, swap(): return lax.all_to_all(parts, 'pen', 0, 0, tiled=True)  19.3 us
    all_to_all x3, starting transfers between devices, swap(): return lax.all_to_all(parts, 'pen', 0, 0, tiled=True)  17.6 us
    all_to_all x1, starting transfers between devices, sum_over_chips(): lax.all_to_all(parts, ('zh', 'y'), 0, 0, tiled=True).astype(F32)  12.7 us
    all_to_all x1, waiting for transfers between devices, sum_over_chips(): lax.all_to_all(parts, ('zh', 'y'), 0, 0, tiled=True).astype(F32)  11.6 us
    ppermute x2, starting transfers between devices, from_other_core(): return lax.ppermute(terms, 'core', [(0, 1), (1, 0)])  8.98 us
    pallas_call x1, Pallas kernels, run_conv_bwd(): pl.pallas_call(conv_bwd, out_shape=shape(GROUPS, PIECE + BH + 8, 128), in...  5.29 us
    pallas_call x1, Pallas kernels, run_conv_fwd(): pl.pallas_call(conv_fwd, out_shape=(shape(ROWS, 128), shape(2, 1024, 128)...  4.44 us
  transfers between devices with their start and end apart: 6, of which 5 were waited for; matrix products, arithmetic and copies ran while one was open for 1% of the time, Pallas kernels for 3%

profile of v7, /device:TPU:1, one launch (start us, length us, event | category | flops | bytes accessed | tf_op | source)
XLA Modules:
  0.0 121.8 jit_solution(16159155281555172208)
XLA Ops:
  0.6 10.4 %all-to-all-start = ((bf16[16,6,8,2,128]{4,3,2,1,0:T(2,128)(2,1)}), bf16[16,6,8,2,128]{4,3,2,1,0:T(2,128)(2,1)S(1)}, u32[]{:S(2)}, u32[]{:S(2)}) async-start(bf16[16,6,8,2,128]{4,3,2,1,0:T(2,128)(2,1)} %bitcast.50), calls=%async_computation | async-start | bytes 786432 | tf_op jit(solution)/shard_map/all_to_all | solution.py:361
  11.4 0.6 copy-done.5
  12.1 0.9 prepare.1
  13.0 10.9 %all-to-all-done = bf16[16,6,8,2,128]{4,3,2,1,0:T(2,128)(2,1)S(1)} async-done(((bf16[16,6,8,2,128]{4,3,2,1,0:T(2,128)(2,1)}), bf16[16,6,8,2,128]{4,3,2,1,0:T(2,128)(2,1)S(1)}, u32[]{:S(2)}, u32[]{:S(2)}) %all-to-all-start) | async-done | bytes 393248 | tf_op jit(solution)/shard_map/all_to_all | solution.py:361
  24.0 4.4 %conv_fwd.1 = (bf16[1536,128]{1,0:T(8,128)(2,1)}, bf16[2,1024,128]{2,1,0:T(8,128)(2,1)S(1)}, bf16[2,1024,128]{2,1,0:T(8,128)(2,1)S(1)}, bf16[256,1024]{1,0:T(8,128)(2,1)S(1)}) custom-call(s32[4]{0:T(128)S(1)} %pad_add_fusion.dil, bf16[1536,128]{1,0:T(8,128)(2,1)S(1)} %bitcast.39, f32[48,128]{1,0:T(8,128)S(1)} %bitcast.46, ...), custom_call_target="tpu_custom_call" | custom-call | flops 1000000000 | bytes 4000000 | tf_op jit(solution)/shard_map/conv_fwd/pallas_call | solution.py:292
  28.4 3.7 %all-to-all-start.1 = ((bf16[16,96,128]{2,1,0:T(8,128)(2,1)}), bf16[16,96,128]{2,1,0:T(8,128)(2,1)S(1)}, u32[]{:S(2)}, u32[]{:S(2)}) async-start(bf16[16,96,128]{2,1,0:T(8,128)(2,1)} %bitcast.8), calls=%async_computation.1 | async-start | bytes 786432 | tf_op jit(solution)/shard_map/all_to_all | solution.py:361
  32.2 12.3 %all-to-all-done.1 = bf16[16,96,128]{2,1,0:T(8,128)(2,1)S(1)} async-done(((bf16[16,96,128]{2,1,0:T(8,128)(2,1)}), bf16[16,96,128]{2,1,0:T(8,128)(2,1)S(1)}, u32[]{:S(2)}, u32[]{:S(2)}) %all-to-all-start.1) | async-done | bytes 393248 | tf_op jit(solution)/shard_map/all_to_all | solution.py:361
  44.5 3.7 %middle.1 = bf16[1536,128]{1,0:T(8,128)(2,1)} custom-call(bf16[1536,128]{1,0:T(8,128)(2,1)S(1)} %bitcast.41, bf16[1536,128]{1,0:T(8,128)(2,1)S(1)} %bitcast.43, bf16[96,384]{1,0:T(8,128)(2,1)S(1)} %copy-done.2, bf16[384,96]{1,0:T(8,128)(2,1)S(1)} %copy.28.wr), custom_call_target="tpu_custom_call" | custom-call | flops 1000000000 | bytes 4000000 | tf_op jit(solution)/shard_map/middle/pallas_call | solution.py:327
  48.3 3.6 %all-to-all-start.2 = ((bf16[16,96,128]{2,1,0:T(8,128)(2,1)}), bf16[16,96,128]{2,1,0:T(8,128)(2,1)S(1)}, u32[]{:S(2)}, u32[]{:S(2)}) async-start(bf16[16,96,128]{2,1,0:T(8,128)(2,1)} %bitcast.12), calls=%async_computation.2 | async-start | bytes 786432 | tf_op jit(solution)/shard_map/all_to_all | solution.py:361
  51.8 3.2 %weight_terms.1 = (f32[384,96]{1,0:T(8,128)S(1)}, f32[384,96]{1,0:T(8,128)S(1)}) custom-call(s32[1]{0:T(128)} %bitcast.14.core, bf16[1536,128]{1,0:T(8,128)(2,1)S(1)} %bitcast.42, bf16[1536,128]{1,0:T(8,128)(2,1)S(1)} %bitcast.44, bf16[96,384]{1,0:T(8,128)(2,1)S(1)} %copy-done.2, bf16[384,96]{1,0:T(8,128)(2,1)S(1)} %copy.28.wr), custom_call_target="tpu_custom_call" | custom-call | flops 1000000000 | bytes 4000000 | tf_op jit(solution)/shard_map/weight_terms/pallas_call | solution.py:340
  55.0 4.1 %collective-permute-start = (f32[384,96]{1,0:T(8,128)S(1)}, f32[384,96]{1,0:T(8,128)S(1)}, u32[]{:S(2)}, u32[]{:S(2)}) collective-permute-start(f32[384,96]{1,0:T(8,128)S(1)} %get-tuple-element.23), channel_id=1, source_target_pairs={{0,16},{16,0},{1,17},{17,1},{2,18},{18,2},{3,19},{19,3},{4,20},{20... | collective-permute-start | bytes 442376 | tf_op jit(solution)/shard_map/ppermute | solution.py:365
  59.1 1.0 collective-permute-done
  60.2 3.9 %all-to-all-done.2 = bf16[16,96,128]{2,1,0:T(8,128)(2,1)S(1)} async-done(((bf16[16,96,128]{2,1,0:T(8,128)(2,1)}), bf16[16,96,128]{2,1,0:T(8,128)(2,1)S(1)}, u32[]{:S(2)}, u32[]{:S(2)}) %all-to-all-start.2) | async-done | bytes 393248 | tf_op jit(solution)/shard_map/all_to_all | solution.py:361
  64.1 5.3 %conv_bwd.1 = bf16[16,128,128]{2,1,0:T(8,128)(2,1)S(1)} custom-call(s32[4]{0:T(128)S(1)} %pad_add_fusion.dil, bf16[1536,128]{1,0:T(8,128)(2,1)S(1)} %bitcast.40, f32[48,128]{1,0:T(8,128)S(1)} %bitcast.47, bf16[256,256]{1,0:T(8,128)(2,1)S(1)} %get-tuple-element.14.hi_ref, bf16[256,256]{1,0:T(8,128)(2,1)S(1)} %get-tuple-element.15.lo_ref, ...), custom_call_target="tpu_custom_call" | custom-call | flops 1000000000 | bytes 4000000 | tf_op jit(solution)/shard_map/conv_bwd/pallas_call | solution.py:306
  69.4 19.3 %all_to_all.25 = bf16[16,128,128]{2,1,0:T(8,128)(2,1)S(1)} all-to-all(bf16[16,128,128]{2,1,0:T(8,128)(2,1)S(1)} %conv_bwd.1), channel_id=1, replica_groups=mesh['zh'=2,'y'=8,'core'=2,'pen'=16] {'pen'}, dimensions={0} | all-to-all | bytes 1048576 | tf_op jit(solution)/shard_map/all_to_all | solution.py:361
  88.8 0.7 broadcast_in_dim.14
  89.5 12.7 %all-to-all-start.4 = ((bf16[16,48,128]{2,1,0:T(8,128)(2,1)}), bf16[16,48,128]{2,1,0:T(8,128)(2,1)S(1)}, u32[]{:S(2)}, u32[]{:S(2)}) async-start(bf16[16,48,128]{2,1,0:T(8,128)(2,1)} %broadcast_in_dim.14), calls=%async_computation.4 | async-start | bytes 393216 | tf_op jit(solution)/shard_map/all_to_all | solution.py:371
  102.2 11.6 %all-to-all-done.4 = bf16[16,48,128]{2,1,0:T(8,128)(2,1)S(1)} async-done(((bf16[16,48,128]{2,1,0:T(8,128)(2,1)}), bf16[16,48,128]{2,1,0:T(8,128)(2,1)S(1)}, u32[]{:S(2)}, u32[]{:S(2)}) %all-to-all-start.4) | async-done | bytes 196640 | tf_op jit(solution)/shard_map/all_to_all | solution.py:371
  113.9 4.9 %collective-permute-start.1 = (f32[48,128]{1,0:T(8,128)S(1)}, f32[48,128]{1,0:T(8,128)S(1)}, u32[]{:S(2)}, u32[]{:S(2)}) collective-permute-start(f32[48,128]{1,0:T(8,128)S(1)} %broadcast_multiply_fusion), channel_id=1, source_target_pairs={{0,16},{16,0},{1,17},{17,1},{2,18},{18,2},{3,19},{19,3},{4,20},{20... | collective-permute-start | bytes 73736 | tf_op jit(solution)/shard_map/ppermute | solution.py:365
  118.8 1.2 fusion.1
  120.1 0.2 copy.33
  120.3 0.2 reshape.90
  120.6 0.6 copy.32
  121.2 0.6 slice_select_fusion
  (29 shorter events, 0.7 us)
Async XLA Ops:
  0.6 10.4 %copy-start = (f32[3,96,9]{1,0,2:T(4,128)S(1)}, f32[3,96,9]{1,0,2:T(4,128)}, u32[]{:S(2)}) copy-start(f32[3,96,9]{1,0,2:T(4,128)} %param.9) | copy-start | bytes 31108
  0.6 23.3 %all-to-all-start = ((bf16[16,6,8,2,128]{4,3,2,1,0:T(2,128)(2,1)}), bf16[16,6,8,2,128]{4,3,2,1,0:T(2,128)(2,1)S(1)}, u32[]{:S(2)}, u32[]{:S(2)}) async-start(bf16[16,6,8,2,128]{4,3,2,1,0:T(2,128)(2,1)} %bitcast.50), calls=%async_computation | async-start | bytes 786432 | tf_op jit(solution)/shard_map/all_to_all | solution.py:361
  11.1 1.0 copy-start.3
  11.3 0.7 copy-start.5
  28.4 3.7 %copy-start.4 = (bf16[384,96]{0,1:T(8,128)(2,1)S(1)}, bf16[384,96]{0,1:T(8,128)(2,1)}, u32[]{:S(2)}) copy-start(bf16[384,96]{0,1:T(8,128)(2,1)} %param.12) | copy-start | bytes 221188
  28.4 16.1 %copy-start.1 = (bf16[1,96,2,1024]{3,2,1,0:T(2,128)(2,1)S(1)}, bf16[1,96,2,1024]{3,2,1,0:T(2,128)(2,1)}, u32[]{:S(2)}) copy-start(bf16[1,96,2,1024]{3,2,1,0:T(2,128)(2,1)} %param.8) | copy-start | bytes 1179652
  28.4 16.1 %all-to-all-start.1 = ((bf16[16,96,128]{2,1,0:T(8,128)(2,1)}), bf16[16,96,128]{2,1,0:T(8,128)(2,1)S(1)}, u32[]{:S(2)}, u32[]{:S(2)}) async-start(bf16[16,96,128]{2,1,0:T(8,128)(2,1)} %bitcast.8), calls=%async_computation.1 | async-start | bytes 786432 | tf_op jit(solution)/shard_map/all_to_all | solution.py:361
  32.1 12.4 %copy-start.2 = (bf16[96,384]{1,0:T(8,128)(2,1)S(1)}, bf16[96,384]{1,0:T(8,128)(2,1)}, u32[]{:S(2)}) copy-start(bf16[96,384]{1,0:T(8,128)(2,1)} %we.3) | copy-start | bytes 221188
  48.3 15.9 %all-to-all-start.2 = ((bf16[16,96,128]{2,1,0:T(8,128)(2,1)}), bf16[16,96,128]{2,1,0:T(8,128)(2,1)S(1)}, u32[]{:S(2)}, u32[]{:S(2)}) async-start(bf16[16,96,128]{2,1,0:T(8,128)(2,1)} %bitcast.12), calls=%async_computation.2 | async-start | bytes 786432 | tf_op jit(solution)/shard_map/all_to_all | solution.py:361
  55.0 5.1 %collective-permute-start = (f32[384,96]{1,0:T(8,128)S(1)}, f32[384,96]{1,0:T(8,128)S(1)}, u32[]{:S(2)}, u32[]{:S(2)}) collective-permute-start(f32[384,96]{1,0:T(8,128)S(1)} %get-tuple-element.23), channel_id=1, source_target_pairs={{0,16},{16,0},{1,17},{17,1},{2,18},{18,2},{3,19},{19,3},{4,20},{20... | collective-permute-start | bytes 442376 | tf_op jit(solution)/shard_map/ppermute | solution.py:365
  89.5 24.4 %all-to-all-start.4 = ((bf16[16,48,128]{2,1,0:T(8,128)(2,1)}), bf16[16,48,128]{2,1,0:T(8,128)(2,1)S(1)}, u32[]{:S(2)}, u32[]{:S(2)}) async-start(bf16[16,48,128]{2,1,0:T(8,128)(2,1)} %broadcast_in_dim.14), calls=%async_computation.4 | async-start | bytes 393216 | tf_op jit(solution)/shard_map/all_to_all | solution.py:371
  113.9 6.1 %collective-permute-start.1 = (f32[48,128]{1,0:T(8,128)S(1)}, f32[48,128]{1,0:T(8,128)S(1)}, u32[]{:S(2)}, u32[]{:S(2)}) collective-permute-start(f32[48,128]{1,0:T(8,128)S(1)} %broadcast_multiply_fusion), channel_id=1, source_target_pairs={{0,16},{16,0},{1,17},{17,1},{2,18},{18,2},{3,19},{19,3},{4,20},{20... | collective-permute-start | bytes 73736 | tf_op jit(solution)/shard_map/ppermute | solution.py:365

commit v8 on v7

--- a/solution.py
+++ b/solution.py
@@ -224,7 +224,7 @@
 def activation(mb, cb, we, wr):
     root = math.sqrt(2.0 / math.pi)
     pre = contract(we[...], mb, 0, 0)
-    d_hidden = contract(wr[...], cb, 1, 0)
+    d_hidden = contract(wr[...], cb, 0, 0)
     square = pre * pre
     inner = pre * (root + (root * 0.044715) * square)
     half = 0.5 + 0.5 * jnp.tanh(inner)
@@ -378,6 +378,7 @@
     coef = jnp.pad(coef, ((0, 0), (0, 16 - TAPS), (0, 128 - C))).reshape(48, 128)
     group = lax.axis_index("pen").astype(jnp.int32)
     core = lax.axis_index("core").astype(jnp.int32)
+    reduce_columns = reduce_weight.T
     scalars = jnp.concatenate([dilations, jnp.mod(group, 4)[None]])
 
     start = activations.reshape(GROUPS, CH, 2, 8, 128).transpose(0, 1, 3, 2, 4)
@@ -386,9 +387,9 @@
     mixed, first, second, field = run_conv_fwd(scalars, lines, coef, hi, lo, eye)
     cot_rows = to_rows(cotangent)
     mixed = swap(mixed.reshape(GROUPS, PIECE, 128)).reshape(ROWS, 128)
-    d_mixed = run_middle(mixed, cot_rows, expand_weight, reduce_weight)
+    d_mixed = run_middle(mixed, cot_rows, expand_weight, reduce_columns)
     d_lines = swap(d_mixed.reshape(GROUPS, PIECE, 128)).reshape(ROWS, 128)
-    keep, send = run_weight_terms(core[None], mixed, cot_rows, expand_weight, reduce_weight)
+    keep, send = run_weight_terms(core[None], mixed, cot_rows, expand_weight, reduce_columns)
     terms = keep + from_other_core(send)
     d_conv = run_conv_bwd(scalars, d_lines, coef, hi, lo, which, first, second, field, terms)
     arrived = swap(d_conv)

time: 122 us -> 122 us (level)
  blocking collectives: 19.3 us -> 35.4 us
  waiting for transfers between devices: 39.8 us -> 28.1 us
  starting transfers between devices: 39.3 us -> 35.2 us
    all_to_all x1 -> x2, blocking collectives: 19.3 us -> 35.4 us  [swap(): return lax.all_to_all(parts, 'pen', 0, 0, tiled=True)]
    all_to_all x3 -> x2, waiting for transfers between devices: 27.1 us -> 15.4 us  [swap(): return lax.all_to_all(parts, 'pen', 0, 0, tiled=True)]
    all_to_all x3 -> x2, starting transfers between devices: 17.6 us -> 13.9 us  [swap(): return lax.all_to_all(parts, 'pen', 0, 0, tiled=True)]
  transfers between devices with their start and end apart: 6 -> 5, of which waited for: 5 -> 4; matrix products, arithmetic and copies ran while one was open for 1% -> 1% of each run, Pallas kernels for 3% -> 3%
where the time goes in v8:
time: 122 us; the launch traced here: 121 us
  blocking collectives  35.4 us (29%)
  starting transfers between devices  35.2 us (29%)
  waiting for transfers between devices  28.1 us (23%)
  Pallas kernels  16.7 us (14%)
  local copies, waits for them, and re-layouts  2.84 us (2%)
  other arithmetic  1.95 us (2%)
    all_to_all x2, blocking collectives, swap(): return lax.all_to_all(parts, 'pen', 0, 0, tiled=True)  35.4 us
    all_to_all x2, waiting for transfers between devices, swap(): return lax.all_to_all(parts, 'pen', 0, 0, tiled=True)  15.4 us
    all_to_all x2, starting transfers between devices, swap(): return lax.all_to_all(parts, 'pen', 0, 0, tiled=True)  13.9 us
    all_to_all x1, starting transfers between devices, sum_over_chips(): lax.all_to_all(parts, ('zh', 'y'), 0, 0, tiled=True).astype(F32)  12.7 us
    all_to_all x1, waiting for transfers between devices, sum_over_chips(): lax.all_to_all(parts, ('zh', 'y'), 0, 0, tiled=True).astype(F32)  11.6 us
    ppermute x2, starting transfers between devices, from_other_core(): return lax.ppermute(terms, 'core', [(0, 1), (1, 0)])  8.57 us
    pallas_call x1, Pallas kernels, run_conv_bwd(): pl.pallas_call(conv_bwd, out_shape=shape(GROUPS, PIECE + BH + 8, 128), in...  5.29 us
    pallas_call x1, Pallas kernels, run_middle(): pl.pallas_call(middle, out_shape=shape(ROWS, 128), in_specs=[VMEM] * 4, o...  3.73 us
  transfers between devices with their start and end apart: 5, of which 4 were waited for; matrix products, arithmetic and copies ran while one was open for 1% of the time, Pallas kernels for 3%

profile of v8, /device:TPU:1, one launch (start us, length us, event | category | flops | bytes accessed | tf_op | source)
XLA Modules:
  0.0 120.9 jit_solution(17562969803354044371)
XLA Ops:
  0.6 10.4 %all-to-all-start = ((bf16[16,6,8,2,128]{4,3,2,1,0:T(2,128)(2,1)}), bf16[16,6,8,2,128]{4,3,2,1,0:T(2,128)(2,1)S(1)}, u32[]{:S(2)}, u32[]{:S(2)}) async-start(bf16[16,6,8,2,128]{4,3,2,1,0:T(2,128)(2,1)} %bitcast.54), calls=%async_computation | async-start | bytes 786432 | tf_op jit(solution)/shard_map/all_to_all | solution.py:361
  11.2 0.1 tile.10
  11.4 0.6 copy-done.5
  12.1 0.9 prepare.1
  13.0 10.9 %all-to-all-done = bf16[16,6,8,2,128]{4,3,2,1,0:T(2,128)(2,1)S(1)} async-done(((bf16[16,6,8,2,128]{4,3,2,1,0:T(2,128)(2,1)}), bf16[16,6,8,2,128]{4,3,2,1,0:T(2,128)(2,1)S(1)}, u32[]{:S(2)}, u32[]{:S(2)}) %all-to-all-start) | async-done | bytes 393248 | tf_op jit(solution)/shard_map/all_to_all | solution.py:361
  24.0 3.5 %conv_fwd.1 = (bf16[1536,128]{1,0:T(8,128)(2,1)S(1)}, bf16[2,1024,128]{2,1,0:T(8,128)(2,1)S(1)}, bf16[2,1024,128]{2,1,0:T(8,128)(2,1)S(1)}, bf16[256,1024]{1,0:T(8,128)(2,1)S(1)}) custom-call(s32[4]{0:T(128)S(1)} %pad_add_fusion.dil, bf16[1536,128]{1,0:T(8,128)(2,1)S(1)} %bitcast.40, f32[48,128]{1,0:T(8,128)S(1)} %bitcast.48, ...), custom_call_target="tpu_custom_call" | custom-call | flops 1000000000 | bytes 4000000 | tf_op jit(solution)/shard_map/conv_fwd/pallas_call | solution.py:292
  27.5 16.3 %all_to_all.25 = bf16[16,96,128]{2,1,0:T(8,128)(2,1)S(1)} all-to-all(bf16[16,96,128]{2,1,0:T(8,128)(2,1)S(1)} %bitcast.44), channel_id=1, replica_groups=mesh['zh'=2,'y'=8,'core'=2,'pen'=16] {'pen'}, dimensions={0} | all-to-all | bytes 786432 | tf_op jit(solution)/shard_map/all_to_all | solution.py:361
  43.8 3.7 %middle.1 = bf16[1536,128]{1,0:T(8,128)(2,1)} custom-call(bf16[1536,128]{1,0:T(8,128)(2,1)S(1)} %bitcast.42, bf16[1536,128]{1,0:T(8,128)(2,1)S(1)} %bitcast.45, bf16[96,384]{1,0:T(8,128)(2,1)S(1)} %copy-done.2, bf16[96,384]{1,0:T(8,128)(2,1)S(1)} %bitcast.50), custom_call_target="tpu_custom_call" | custom-call | flops 1000000000 | bytes 4000000 | tf_op jit(solution)/shard_map/middle/pallas_call | solution.py:327
  47.6 3.6 %all-to-all-start.2 = ((bf16[16,96,128]{2,1,0:T(8,128)(2,1)}), bf16[16,96,128]{2,1,0:T(8,128)(2,1)S(1)}, u32[]{:S(2)}, u32[]{:S(2)}) async-start(bf16[16,96,128]{2,1,0:T(8,128)(2,1)} %bitcast.13), calls=%async_computation.2 | async-start | bytes 786432 | tf_op jit(solution)/shard_map/all_to_all | solution.py:361
  51.1 3.2 %weight_terms.1 = (f32[384,96]{1,0:T(8,128)S(1)}, f32[384,96]{1,0:T(8,128)S(1)}) custom-call(s32[1]{0:T(128)} %bitcast.15.core, bf16[1536,128]{1,0:T(8,128)(2,1)S(1)} %bitcast.43, bf16[1536,128]{1,0:T(8,128)(2,1)S(1)} %bitcast.46, bf16[96,384]{1,0:T(8,128)(2,1)S(1)} %copy-done.2, bf16[96,384]{1,0:T(8,128)(2,1)S(1)} %bitcast.51), custom_call_target="tpu_custom_call" | custom-call | flops 1000000000 | bytes 4000000 | tf_op jit(solution)/shard_map/weight_terms/pallas_call | solution.py:340
  54.3 3.7 %collective-permute-start = (f32[384,96]{1,0:T(8,128)S(1)}, f32[384,96]{1,0:T(8,128)S(1)}, u32[]{:S(2)}, u32[]{:S(2)}) collective-permute-start(f32[384,96]{1,0:T(8,128)S(1)} %get-tuple-element.23), channel_id=1, source_target_pairs={{0,16},{16,0},{1,17},{17,1},{2,18},{18,2},{3,19},{19,3},{4,20},{20... | collective-permute-start | bytes 442376 | tf_op jit(solution)/shard_map/ppermute | solution.py:365
  58.0 1.0 collective-permute-done
  59.1 4.5 %all-to-all-done.2 = bf16[16,96,128]{2,1,0:T(8,128)(2,1)S(1)} async-done(((bf16[16,96,128]{2,1,0:T(8,128)(2,1)}), bf16[16,96,128]{2,1,0:T(8,128)(2,1)S(1)}, u32[]{:S(2)}, u32[]{:S(2)}) %all-to-all-start.2) | async-done | bytes 393248 | tf_op jit(solution)/shard_map/all_to_all | solution.py:361
  63.6 5.3 %conv_bwd.1 = bf16[16,128,128]{2,1,0:T(8,128)(2,1)S(1)} custom-call(s32[4]{0:T(128)S(1)} %pad_add_fusion.dil, bf16[1536,128]{1,0:T(8,128)(2,1)S(1)} %bitcast.41, f32[48,128]{1,0:T(8,128)S(1)} %bitcast.49, bf16[256,256]{1,0:T(8,128)(2,1)S(1)} %get-tuple-element.14.hi_ref, bf16[256,256]{1,0:T(8,128)(2,1)S(1)} %get-tuple-element.15.lo_ref, ...), custom_call_target="tpu_custom_call" | custom-call | flops 1000000000 | bytes 4000000 | tf_op jit(solution)/shard_map/conv_bwd/pallas_call | solution.py:306
  68.8 19.0 %all_to_all.26 = bf16[16,128,128]{2,1,0:T(8,128)(2,1)S(1)} all-to-all(bf16[16,128,128]{2,1,0:T(8,128)(2,1)S(1)} %conv_bwd.1), channel_id=1, replica_groups=mesh['zh'=2,'y'=8,'core'=2,'pen'=16] {'pen'}, dimensions={0} | all-to-all | bytes 1048576 | tf_op jit(solution)/shard_map/all_to_all | solution.py:361
  88.0 0.7 broadcast_in_dim.14
  88.7 12.7 %all-to-all-start.4 = ((bf16[16,48,128]{2,1,0:T(8,128)(2,1)}), bf16[16,48,128]{2,1,0:T(8,128)(2,1)S(1)}, u32[]{:S(2)}, u32[]{:S(2)}) async-start(bf16[16,48,128]{2,1,0:T(8,128)(2,1)} %broadcast_in_dim.14), calls=%async_computation.4 | async-start | bytes 393216 | tf_op jit(solution)/shard_map/all_to_all | solution.py:371
  101.4 11.6 %all-to-all-done.4 = bf16[16,48,128]{2,1,0:T(8,128)(2,1)S(1)} async-done(((bf16[16,48,128]{2,1,0:T(8,128)(2,1)}), bf16[16,48,128]{2,1,0:T(8,128)(2,1)S(1)}, u32[]{:S(2)}, u32[]{:S(2)}) %all-to-all-start.4) | async-done | bytes 196640 | tf_op jit(solution)/shard_map/all_to_all | solution.py:371
  113.1 4.9 %collective-permute-start.1 = (f32[48,128]{1,0:T(8,128)S(1)}, f32[48,128]{1,0:T(8,128)S(1)}, u32[]{:S(2)}, u32[]{:S(2)}) collective-permute-start(f32[48,128]{1,0:T(8,128)S(1)} %broadcast_multiply_fusion), channel_id=1, source_target_pairs={{0,16},{16,0},{1,17},{17,1},{2,18},{18,2},{3,19},{19,3},{4,20},{20... | collective-permute-start | bytes 73736 | tf_op jit(solution)/shard_map/ppermute | solution.py:365
  118.0 1.2 fusion.1
  119.3 0.2 copy.27
  119.5 0.2 reshape.90
  119.7 0.6 copy.26
  120.3 0.6 slice_select_fusion
  (27 shorter events, 0.5 us)
Async XLA Ops:
  0.6 10.4 %copy-start = (f32[3,96,9]{1,0,2:T(4,128)S(1)}, f32[3,96,9]{1,0,2:T(4,128)}, u32[]{:S(2)}) copy-start(f32[3,96,9]{1,0,2:T(4,128)} %param.9) | copy-start | bytes 31108
  0.6 23.3 %all-to-all-start = ((bf16[16,6,8,2,128]{4,3,2,1,0:T(2,128)(2,1)}), bf16[16,6,8,2,128]{4,3,2,1,0:T(2,128)(2,1)S(1)}, u32[]{:S(2)}, u32[]{:S(2)}) async-start(bf16[16,6,8,2,128]{4,3,2,1,0:T(2,128)(2,1)} %bitcast.54), calls=%async_computation | async-start | bytes 786432 | tf_op jit(solution)/shard_map/all_to_all | solution.py:361
  11.1 1.0 copy-start.4
  11.3 0.7 copy-start.5
  27.5 16.3 %copy-start.1 = (bf16[1,96,2,1024]{3,2,1,0:T(2,128)(2,1)S(1)}, bf16[1,96,2,1024]{3,2,1,0:T(2,128)(2,1)}, u32[]{:S(2)}) copy-start(bf16[1,96,2,1024]{3,2,1,0:T(2,128)(2,1)} %param.8) | copy-start | bytes 1179652
  27.5 16.3 %copy-start.2 = (bf16[96,384]{1,0:T(8,128)(2,1)S(1)}, bf16[96,384]{1,0:T(8,128)(2,1)}, u32[]{:S(2)}) copy-start(bf16[96,384]{1,0:T(8,128)(2,1)} %we.3) | copy-start | bytes 221188
  27.5 16.3 %copy-start.3 = (bf16[384,96]{0,1:T(8,128)(2,1)S(1)}, bf16[384,96]{0,1:T(8,128)(2,1)}, u32[]{:S(2)}) copy-start(bf16[384,96]{0,1:T(8,128)(2,1)} %param.12) | copy-start | bytes 221188
  47.6 16.0 %all-to-all-start.2 = ((bf16[16,96,128]{2,1,0:T(8,128)(2,1)}), bf16[16,96,128]{2,1,0:T(8,128)(2,1)S(1)}, u32[]{:S(2)}, u32[]{:S(2)}) async-start(bf16[16,96,128]{2,1,0:T(8,128)(2,1)} %bitcast.13), calls=%async_computation.2 | async-start | bytes 786432 | tf_op jit(solution)/shard_map/all_to_all | solution.py:361
  54.3 4.7 %collective-permute-start = (f32[384,96]{1,0:T(8,128)S(1)}, f32[384,96]{1,0:T(8,128)S(1)}, u32[]{:S(2)}, u32[]{:S(2)}) collective-permute-start(f32[384,96]{1,0:T(8,128)S(1)} %get-tuple-element.23), channel_id=1, source_target_pairs={{0,16},{16,0},{1,17},{17,1},{2,18},{18,2},{3,19},{19,3},{4,20},{20... | collective-permute-start | bytes 442376 | tf_op jit(solution)/shard_map/ppermute | solution.py:365
  88.7 24.4 %all-to-all-start.4 = ((bf16[16,48,128]{2,1,0:T(8,128)(2,1)}), bf16[16,48,128]{2,1,0:T(8,128)(2,1)S(1)}, u32[]{:S(2)}, u32[]{:S(2)}) async-start(bf16[16,48,128]{2,1,0:T(8,128)(2,1)} %broadcast_in_dim.14), calls=%async_computation.4 | async-start | bytes 393216 | tf_op jit(solution)/shard_map/all_to_all | solution.py:371
  113.1 6.1 %collective-permute-start.1 = (f32[48,128]{1,0:T(8,128)S(1)}, f32[48,128]{1,0:T(8,128)S(1)}, u32[]{:S(2)}, u32[]{:S(2)}) collective-permute-start(f32[48,128]{1,0:T(8,128)S(1)} %broadcast_multiply_fusion), channel_id=1, source_target_pairs={{0,16},{16,0},{1,17},{17,1},{2,18},{18,2},{3,19},{19,3},{4,20},{20... | collective-permute-start | bytes 73736 | tf_op jit(solution)/shard_map/ppermute | solution.py:365

commit v9 on v8

--- a/solution.py
+++ b/solution.py
@@ -160,7 +160,7 @@
 
     sums = lax.fori_loop(0, L, along_z, empty, unroll=4)
     for t in range(TAPS):
-        acc_ref[18 + t] = sums[t]
+        acc_ref[3 * t + 2] = sums[t]
     taps = spread(coef, 16)
 
     def along_y(y, sums):
@@ -178,7 +178,7 @@
 
     sums = lax.fori_loop(0, L, along_y, empty, unroll=4)
     for t in range(TAPS):
-        acc_ref[9 + t] = sums[t]
+        acc_ref[3 * t + 1] = sums[t]
     for t in range(27, 32):
         acc_ref[t] = jnp.zeros((8, 128), F32)
 
@@ -187,7 +187,7 @@
     for t in range(TAPS):
         keep = jnp.where(tap_of == float(t), cross, 0.0)
         keep = jnp.sum(keep.reshape(32, 8, 256), axis=0)
-        acc_ref[t] = keep[:, :128] + keep[:, 128:]
+        acc_ref[3 * t] = keep[:, :128] + keep[:, 128:]
     lane = lax.broadcasted_iota(jnp.int32, (8, 128), 1)
     channel = lax.broadcasted_iota(jnp.int32, (8, 128), 0)
     table = jnp.where((lax.rem(lane, CH) == channel) & (lane < C), 1.0, 0.0)
@@ -263,6 +263,25 @@
     send_ref[...] = jnp.where(core[0] == 0, reduce, expand)
 
 
+def finish(core, mine_ref, other_ref, expand_ref, reduce_ref, kern_ref):
+    mine, other = mine_ref[...], other_ref[...]
+    is_first = core[0] == 0
+    expand_ref[...] = jnp.where(is_first, mine, other)[0:BH, 0:C]
+    reduce_ref[...] = jnp.where(is_first, other, mine)[0:BH, 0:C]
+    kern = (mine + other)[BH:, :]
+    row = lax.broadcasted_iota(jnp.int32, (4 * CH, C), 0)
+    lane = lax.broadcasted_iota(jnp.int32, (4 * CH, C), 1)
+    total = jnp.zeros((32, C), F32)
+    for i in range(4):
+        target = lax.div(row, CH) * (4 * CH) + i * CH + lax.rem(row, CH)
+        place = jnp.where(lane == target, 1.0, 0.0)
+        total = total + lax.dot_general(
+            kern[:, 32 * i:32 * i + 32], place, (((0,), (0,)), ((), ())),
+            precision=lax.Precision.HIGHEST, preferred_element_type=F32)
+    for t in range(TAPS):
+        kern_ref[t] = total[3 * t:3 * t + 3, :]
+
+
 VMEM = pl.BlockSpec(memory_space=pltpu.VMEM)
 SMEM = pl.BlockSpec(memory_space=pltpu.SMEM)
 PARAMS = pltpu.CompilerParams(vmem_limit_bytes=28 * 1024 * 1024)
@@ -347,6 +366,18 @@
         cost_estimate=estimate(10**9),
         name="weight_terms",
     )(core, *arrays)
+
+
+def run_finish(core, mine, other):
+    return pl.pallas_call(
+        finish,
+        out_shape=(shape(BH, C, dtype=F32), shape(BH, C, dtype=F32), shape(TAPS, 3, C, dtype=F32)),
+        in_specs=[SMEM] + [VMEM] * 2,
+        out_specs=(VMEM,) * 3,
+        compiler_params=PARAMS,
+        cost_estimate=estimate(10**7),
+        name="finish",
+    )(core, mine, other)
 
 
 def to_rows(field):
@@ -403,12 +434,8 @@
 
     samples = lax.axis_size("zh") * lax.axis_size("y") * lax.axis_size("core")
     mine = mine * (1.0 / math.sqrt(samples * L * L * L))
-    other = from_other_core(mine)
-    own_expand = jnp.where(core == 0, mine, other)[0:BH, 0:C].T
-    own_reduce = jnp.where(core == 0, other, mine)[0:BH, 0:C]
-    kern = (mine + other)[BH:].reshape(4, CH, 4, 32)[:, :, :, :3 * TAPS]
-    kern = kern.transpose(0, 2, 1, 3).reshape(C, 3, TAPS).transpose(1, 0, 2)
-    return grad_input, own_expand, own_reduce, kern
+    expand, reduce, kern = run_finish(core[None], mine, from_other_core(mine))
+    return grad_input, expand.T, reduce, kern.transpose(1, 2, 0)
 
 
 def solution(mesh):

time: 122 us -> 121 us (level)
  no operation moved by 1% of the time
where the time goes in v9:
time: 121 us; the launch traced here: 120 us
  blocking collectives  35.4 us (29%)
  starting transfers between devices  35.2 us (29%)
  waiting for transfers between devices  28.1 us (23%)
  Pallas kernels  17.8 us (15%)
  local copies, waits for them, and re-layouts  1.69 us (1%)
  other arithmetic  1.34 us (1%)
    all_to_all x2, blocking collectives, swap(): return lax.all_to_all(parts, 'pen', 0, 0, tiled=True)  35.4 us
    all_to_all x2, waiting for transfers between devices, swap(): return lax.all_to_all(parts, 'pen', 0, 0, tiled=True)  15.4 us
    all_to_all x2, starting transfers between devices, swap(): return lax.all_to_all(parts, 'pen', 0, 0, tiled=True)  13.9 us
    all_to_all x1, starting transfers between devices, sum_over_chips(): lax.all_to_all(parts, ('zh', 'y'), 0, 0, tiled=True).astype(F32)  12.7 us
    all_to_all x1, waiting for transfers between devices, sum_over_chips(): lax.all_to_all(parts, ('zh', 'y'), 0, 0, tiled=True).astype(F32)  11.6 us
    ppermute x2, starting transfers between devices, from_other_core(): return lax.ppermute(terms, 'core', [(0, 1), (1, 0)])  8.56 us
    pallas_call x1, Pallas kernels, run_conv_bwd(): pl.pallas_call(conv_bwd, out_shape=shape(GROUPS, PIECE + BH + 8, 128), in...  5.29 us
    pallas_call x1, Pallas kernels, run_middle(): pl.pallas_call(middle, out_shape=shape(ROWS, 128), in_specs=[VMEM] * 4, o...  3.74 us
  transfers between devices with their start and end apart: 5, of which 4 were waited for; matrix products, arithmetic and copies ran while one was open for 1% of the time, Pallas kernels for 3%

profile of v9, /device:TPU:1, one launch (start us, length us, event | category | flops | bytes accessed | tf_op | source)
XLA Modules:
  0.0 120.3 jit_solution(6660969897217102849)
XLA Ops:
  0.6 10.4 %all-to-all-start = ((bf16[16,6,8,2,128]{4,3,2,1,0:T(2,128)(2,1)}), bf16[16,6,8,2,128]{4,3,2,1,0:T(2,128)(2,1)S(1)}, u32[]{:S(2)}, u32[]{:S(2)}) async-start(bf16[16,6,8,2,128]{4,3,2,1,0:T(2,128)(2,1)} %bitcast.48), calls=%async_computation | async-start | bytes 786432 | tf_op jit(solution)/shard_map/all_to_all | solution.py:392
  11.1 0.1 dynamic-slice_bitcast_fusion
  11.2 0.1 tile.10
  11.4 0.6 copy-done.5
  12.0 0.1 pad_add_fusion.dil
  12.1 0.0 copy-done.4
  12.1 0.9 prepare.1
  13.0 10.9 %all-to-all-done = bf16[16,6,8,2,128]{4,3,2,1,0:T(2,128)(2,1)S(1)} async-done(((bf16[16,6,8,2,128]{4,3,2,1,0:T(2,128)(2,1)}), bf16[16,6,8,2,128]{4,3,2,1,0:T(2,128)(2,1)S(1)}, u32[]{:S(2)}, u32[]{:S(2)}) %all-to-all-start) | async-done | bytes 393248 | tf_op jit(solution)/shard_map/all_to_all | solution.py:392
  24.0 3.7 %conv_fwd.1 = (bf16[1536,128]{1,0:T(8,128)(2,1)S(1)}, bf16[2,1024,128]{2,1,0:T(8,128)(2,1)S(1)}, bf16[2,1024,128]{2,1,0:T(8,128)(2,1)S(1)}, bf16[256,1024]{1,0:T(8,128)(2,1)S(1)}) custom-call(s32[4]{0:T(128)S(1)} %pad_add_fusion.dil, bf16[1536,128]{1,0:T(8,128)(2,1)S(1)} %bitcast.35, f32[48,128]{1,0:T(8,128)S(1)} %bitcast.43, ...), custom_call_target="tpu_custom_call" | custom-call | flops 1000000000 | bytes 4000000 | tf_op jit(solution)/shard_map/conv_fwd/pallas_call | solution.py:311
  27.7 16.3 %all_to_all.25 = bf16[16,96,128]{2,1,0:T(8,128)(2,1)S(1)} all-to-all(bf16[16,96,128]{2,1,0:T(8,128)(2,1)S(1)} %bitcast.39), channel_id=1, replica_groups=mesh['zh'=2,'y'=8,'core'=2,'pen'=16] {'pen'}, dimensions={0} | all-to-all | bytes 786432 | tf_op jit(solution)/shard_map/all_to_all | solution.py:392
  44.0 3.7 %middle.1 = bf16[1536,128]{1,0:T(8,128)(2,1)} custom-call(bf16[1536,128]{1,0:T(8,128)(2,1)S(1)} %bitcast.37, bf16[1536,128]{1,0:T(8,128)(2,1)S(1)} %bitcast.40, bf16[96,384]{1,0:T(8,128)(2,1)S(1)} %copy-done.2, bf16[96,384]{1,0:T(8,128)(2,1)S(1)} %bitcast.45), custom_call_target="tpu_custom_call" | custom-call | flops 1000000000 | bytes 4000000 | tf_op jit(solution)/shard_map/middle/pallas_call | solution.py:346
  47.7 3.6 %all-to-all-start.2 = ((bf16[16,96,128]{2,1,0:T(8,128)(2,1)}), bf16[16,96,128]{2,1,0:T(8,128)(2,1)S(1)}, u32[]{:S(2)}, u32[]{:S(2)}) async-start(bf16[16,96,128]{2,1,0:T(8,128)(2,1)} %bitcast.13), calls=%async_computation.2 | async-start | bytes 786432 | tf_op jit(solution)/shard_map/all_to_all | solution.py:392
  51.3 3.2 %weight_terms.1 = (f32[384,96]{1,0:T(8,128)S(1)}, f32[384,96]{1,0:T(8,128)S(1)}) custom-call(s32[1]{0:T(128)} %bitcast.15.core, bf16[1536,128]{1,0:T(8,128)(2,1)S(1)} %bitcast.38, bf16[1536,128]{1,0:T(8,128)(2,1)S(1)} %bitcast.41, bf16[96,384]{1,0:T(8,128)(2,1)S(1)} %copy-done.2, bf16[96,384]{1,0:T(8,128)(2,1)S(1)} %bitcast.46), custom_call_target="tpu_custom_call" | custom-call | flops 1000000000 | bytes 4000000 | tf_op jit(solution)/shard_map/weight_terms/pallas_call | solution.py:359
  54.5 3.7 %collective-permute-start = (f32[384,96]{1,0:T(8,128)S(1)}, f32[384,96]{1,0:T(8,128)S(1)}, u32[]{:S(2)}, u32[]{:S(2)}) collective-permute-start(f32[384,96]{1,0:T(8,128)S(1)} %get-tuple-element.26), channel_id=1, source_target_pairs={{0,16},{16,0},{1,17},{17,1},{2,18},{18,2},{3,19},{19,3},{4,20},{20... | collective-permute-start | bytes 442376 | tf_op jit(solution)/shard_map/ppermute | solution.py:396
  58.2 1.0 collective-permute-done
  59.3 4.5 %all-to-all-done.2 = bf16[16,96,128]{2,1,0:T(8,128)(2,1)S(1)} async-done(((bf16[16,96,128]{2,1,0:T(8,128)(2,1)}), bf16[16,96,128]{2,1,0:T(8,128)(2,1)S(1)}, u32[]{:S(2)}, u32[]{:S(2)}) %all-to-all-start.2) | async-done | bytes 393248 | tf_op jit(solution)/shard_map/all_to_all | solution.py:392
  63.7 5.3 %conv_bwd.1 = bf16[16,128,128]{2,1,0:T(8,128)(2,1)S(1)} custom-call(s32[4]{0:T(128)S(1)} %pad_add_fusion.dil, bf16[1536,128]{1,0:T(8,128)(2,1)S(1)} %bitcast.36, f32[48,128]{1,0:T(8,128)S(1)} %bitcast.44, bf16[256,256]{1,0:T(8,128)(2,1)S(1)} %get-tuple-element.17.hi_ref, bf16[256,256]{1,0:T(8,128)(2,1)S(1)} %get-tuple-element.18.lo_ref, ...), custom_call_target="tpu_custom_call" | custom-call | flops 1000000000 | bytes 4000000 | tf_op jit(solution)/shard_map/conv_bwd/pallas_call | solution.py:325
  69.0 19.0 %all_to_all.26 = bf16[16,128,128]{2,1,0:T(8,128)(2,1)S(1)} all-to-all(bf16[16,128,128]{2,1,0:T(8,128)(2,1)S(1)} %conv_bwd.1), channel_id=1, replica_groups=mesh['zh'=2,'y'=8,'core'=2,'pen'=16] {'pen'}, dimensions={0} | all-to-all | bytes 1048576 | tf_op jit(solution)/shard_map/all_to_all | solution.py:392
  88.1 0.7 broadcast_in_dim.15
  88.8 12.7 %all-to-all-start.4 = ((bf16[16,48,128]{2,1,0:T(8,128)(2,1)}), bf16[16,48,128]{2,1,0:T(8,128)(2,1)S(1)}, u32[]{:S(2)}, u32[]{:S(2)}) async-start(bf16[16,48,128]{2,1,0:T(8,128)(2,1)} %broadcast_in_dim.15), calls=%async_computation.4 | async-start | bytes 393216 | tf_op jit(solution)/shard_map/all_to_all | solution.py:402
  101.6 11.6 %all-to-all-done.4 = bf16[16,48,128]{2,1,0:T(8,128)(2,1)S(1)} async-done(((bf16[16,48,128]{2,1,0:T(8,128)(2,1)}), bf16[16,48,128]{2,1,0:T(8,128)(2,1)S(1)}, u32[]{:S(2)}, u32[]{:S(2)}) %all-to-all-start.4) | async-done | bytes 196640 | tf_op jit(solution)/shard_map/all_to_all | solution.py:402
  113.3 4.9 %collective-permute-start.1 = (f32[48,128]{1,0:T(8,128)S(1)}, f32[48,128]{1,0:T(8,128)S(1)}, u32[]{:S(2)}, u32[]{:S(2)}) collective-permute-start(f32[48,128]{1,0:T(8,128)S(1)} %broadcast_multiply_fusion.mine_ref), channel_id=1, source_target_pairs={{0,16},{16,0},{1,17},{17,1},{2,18},{18,2},{3,19},{19,3},{4,20},{20... | collective-permute-start | bytes 73736 | tf_op jit(solution)/shard_map/ppermute | solution.py:396
  118.2 1.2 fusion.1
  119.3 1.0 finish.1
  (22 shorter events, 0.2 us)
Async XLA Ops:
  0.6 10.4 %copy-start = (f32[3,96,9]{1,0,2:T(4,128)S(1)}, f32[3,96,9]{1,0,2:T(4,128)}, u32[]{:S(2)}) copy-start(f32[3,96,9]{1,0,2:T(4,128)} %param.9) | copy-start | bytes 31108
  0.6 23.3 %all-to-all-start = ((bf16[16,6,8,2,128]{4,3,2,1,0:T(2,128)(2,1)}), bf16[16,6,8,2,128]{4,3,2,1,0:T(2,128)(2,1)S(1)}, u32[]{:S(2)}, u32[]{:S(2)}) async-start(bf16[16,6,8,2,128]{4,3,2,1,0:T(2,128)(2,1)} %bitcast.48), calls=%async_computation | async-start | bytes 786432 | tf_op jit(solution)/shard_map/all_to_all | solution.py:392
  11.1 1.0 copy-start.4
  11.3 0.7 copy-start.5
  27.6 16.3 %copy-start.1 = (bf16[1,96,2,1024]{3,2,1,0:T(2,128)(2,1)S(1)}, bf16[1,96,2,1024]{3,2,1,0:T(2,128)(2,1)}, u32[]{:S(2)}) copy-start(bf16[1,96,2,1024]{3,2,1,0:T(2,128)(2,1)} %param.8) | copy-start | bytes 1179652
  27.7 16.3 %copy-start.2 = (bf16[96,384]{1,0:T(8,128)(2,1)S(1)}, bf16[96,384]{1,0:T(8,128)(2,1)}, u32[]{:S(2)}) copy-start(bf16[96,384]{1,0:T(8,128)(2,1)} %we.3) | copy-start | bytes 221188
  27.7 16.3 %copy-start.3 = (bf16[384,96]{0,1:T(8,128)(2,1)S(1)}, bf16[384,96]{0,1:T(8,128)(2,1)}, u32[]{:S(2)}) copy-start(bf16[384,96]{0,1:T(8,128)(2,1)} %param.12) | copy-start | bytes 221188
  47.7 16.0 %all-to-all-start.2 = ((bf16[16,96,128]{2,1,0:T(8,128)(2,1)}), bf16[16,96,128]{2,1,0:T(8,128)(2,1)S(1)}, u32[]{:S(2)}, u32[]{:S(2)}) async-start(bf16[16,96,128]{2,1,0:T(8,128)(2,1)} %bitcast.13), calls=%async_computation.2 | async-start | bytes 786432 | tf_op jit(solution)/shard_map/all_to_all | solution.py:392
  54.5 4.7 %collective-permute-start = (f32[384,96]{1,0:T(8,128)S(1)}, f32[384,96]{1,0:T(8,128)S(1)}, u32[]{:S(2)}, u32[]{:S(2)}) collective-permute-start(f32[384,96]{1,0:T(8,128)S(1)} %get-tuple-element.26), channel_id=1, source_target_pairs={{0,16},{16,0},{1,17},{17,1},{2,18},{18,2},{3,19},{19,3},{4,20},{20... | collective-permute-start | bytes 442376 | tf_op jit(solution)/shard_map/ppermute | solution.py:396
  88.8 24.4 %all-to-all-start.4 = ((bf16[16,48,128]{2,1,0:T(8,128)(2,1)}), bf16[16,48,128]{2,1,0:T(8,128)(2,1)S(1)}, u32[]{:S(2)}, u32[]{:S(2)}) async-start(bf16[16,48,128]{2,1,0:T(8,128)(2,1)} %broadcast_in_dim.15), calls=%async_computation.4 | async-start | bytes 393216 | tf_op jit(solution)/shard_map/all_to_all | solution.py:402
  113.3 6.1 %collective-permute-start.1 = (f32[48,128]{1,0:T(8,128)S(1)}, f32[48,128]{1,0:T(8,128)S(1)}, u32[]{:S(2)}, u32[]{:S(2)}) collective-permute-start(f32[48,128]{1,0:T(8,128)S(1)} %broadcast_multiply_fusion.mine_ref), channel_id=1, source_target_pairs={{0,16},{16,0},{1,17},{17,1},{2,18},{18,2},{3,19},{19,3},{4,20},{20... | collective-permute-start | bytes 73736 | tf_op jit(solution)/shard_map/ppermute | solution.py:396

commit v10 on v9

--- a/solution.py
+++ b/solution.py
@@ -1,3 +1,4 @@
+import functools
 import math
 
 import jax
@@ -233,9 +234,12 @@
     return hidden, (d_hidden * slope).astype(BF16)
 
 
-def middle(m_ref, c_ref, we, wr, out_ref, stage, stage_c, mix, cot):
+def lay_out(c_ref, cot, stage):
+    by_site(c_ref, stage, cot)
+
+
+def middle(m_ref, cot, we, wr, out_ref, stage, mix):
     by_site(m_ref, stage, mix)
-    by_site(c_ref, stage_c, cot)
     for b in range(2 * L * L // BLOCK):
         cols = slice(b * BLOCK, (b + 1) * BLOCK)
         _, d_pre = activation(mix[:, cols], cot[:, cols], we, wr)
@@ -246,10 +250,8 @@
     out_ref[...] = stage[...].astype(BF16)
 
 
-def weight_terms(core, m_ref, c_ref, we, wr, keep_ref, send_ref, stage, stage_c, mix, cot,
-                 expand_ref, reduce_ref):
+def weight_terms(core, m_ref, cot, we, wr, keep_ref, send_ref, stage, mix, expand_ref, reduce_ref):
     by_site(m_ref, stage, mix)
-    by_site(c_ref, stage_c, cot)
     expand_ref[...] = jnp.zeros_like(expand_ref)
     reduce_ref[...] = jnp.zeros_like(reduce_ref)
     for b in range(2 * L * L // BLOCK):
@@ -263,8 +265,8 @@
     send_ref[...] = jnp.where(core[0] == 0, reduce, expand)
 
 
-def finish(core, mine_ref, other_ref, expand_ref, reduce_ref, kern_ref):
-    mine, other = mine_ref[...], other_ref[...]
+def finish(scale, core, mine_ref, other_ref, expand_ref, reduce_ref, kern_ref):
+    mine, other = mine_ref[...] * scale, other_ref[...] * scale
     is_first = core[0] == 0
     expand_ref[...] = jnp.where(is_first, mine, other)[0:BH, 0:C]
     reduce_ref[...] = jnp.where(is_first, other, mine)[0:BH, 0:C]
@@ -338,8 +340,20 @@
 
 
 def site_scratch():
-    return [pltpu.VMEM((ROWS, 128), F32), pltpu.VMEM((ROWS, 128), F32),
-            pltpu.VMEM((C, 2048), BF16), pltpu.VMEM((C, 2048), BF16)]
+    return [pltpu.VMEM((ROWS, 128), F32), pltpu.VMEM((C, 2048), BF16)]
+
+
+def run_lay_out(rows):
+    return pl.pallas_call(
+        lay_out,
+        out_shape=shape(C, 2048),
+        in_specs=[VMEM],
+        out_specs=VMEM,
+        scratch_shapes=[pltpu.VMEM((ROWS, 128), F32)],
+        compiler_params=PARAMS,
+        cost_estimate=estimate(10**8),
+        name="lay_out",
+    )(rows)
 
 
 def run_middle(*arrays):
@@ -368,9 +382,9 @@
     )(core, *arrays)
 
 
-def run_finish(core, mine, other):
-    return pl.pallas_call(
-        finish,
+def run_finish(scale, core, mine, other):
+    return pl.pallas_call(
+        functools.partial(finish, scale),
         out_shape=(shape(BH, C, dtype=F32), shape(BH, C, dtype=F32), shape(TAPS, 3, C, dtype=F32)),
         in_specs=[SMEM] + [VMEM] * 2,
         out_specs=(VMEM,) * 3,
@@ -399,7 +413,7 @@
 def sum_over_chips(terms):
     size = lax.axis_size("zh") * lax.axis_size("y")
     parts = jnp.broadcast_to(terms.astype(BF16)[None], (size,) + terms.shape)
-    return jnp.sum(lax.all_to_all(parts, ("zh", "y"), 0, 0, tiled=True).astype(F32), axis=0)
+    return jnp.sum(lax.all_to_all(parts, ("y", "zh"), 0, 0, tiled=True).astype(F32), axis=0)
 
 
 def per_device(activations, cotangent, depth_kernels, dilations, expand_weight, reduce_weight):
@@ -414,13 +428,14 @@
 
     start = activations.reshape(GROUPS, CH, 2, 8, 128).transpose(0, 1, 3, 2, 4)
     lines = swap(start).reshape(ROWS, 128)
+    cot_rows = to_rows(cotangent)
+    lines, cot = lax.optimization_barrier((lines, run_lay_out(cot_rows)))
     hi, lo, eye, which = run_prepare(scalars, coef, delta)
     mixed, first, second, field = run_conv_fwd(scalars, lines, coef, hi, lo, eye)
-    cot_rows = to_rows(cotangent)
     mixed = swap(mixed.reshape(GROUPS, PIECE, 128)).reshape(ROWS, 128)
-    d_mixed = run_middle(mixed, cot_rows, expand_weight, reduce_columns)
+    d_mixed = run_middle(mixed, cot, expand_weight, reduce_columns)
     d_lines = swap(d_mixed.reshape(GROUPS, PIECE, 128)).reshape(ROWS, 128)
-    keep, send = run_weight_terms(core[None], mixed, cot_rows, expand_weight, reduce_columns)
+    keep, send = run_weight_terms(core[None], mixed, cot, expand_weight, reduce_columns)
     terms = keep + from_other_core(send)
     d_conv = run_conv_bwd(scalars, d_lines, coef, hi, lo, which, first, second, field, terms)
     arrived = swap(d_conv)
@@ -433,8 +448,8 @@
     grad_input = from_rows((cot_rows.astype(F32) + d_input.astype(F32)).astype(BF16))
 
     samples = lax.axis_size("zh") * lax.axis_size("y") * lax.axis_size("core")
-    mine = mine * (1.0 / math.sqrt(samples * L * L * L))
-    expand, reduce, kern = run_finish(core[None], mine, from_other_core(mine))
+    scale = 1.0 / math.sqrt(samples * L * L * L)
+    expand, reduce, kern = run_finish(scale, core[None], mine, from_other_core(mine))
     return grad_input, expand.T, reduce, kern.transpose(1, 2, 0)
 
 

time: 121 us -> 122 us (level)
    all_to_all x1, waiting for transfers between devices: 11.6 us -> 12.9 us  [sum_over_chips(): lax.all_to_all(parts, ('y', 'zh'), 0, 0, tiled=True).astype(F32)]
  transfers between devices with their start and end apart: 5 -> 5, of which waited for: 4 -> 4; matrix products, arithmetic and copies ran while one was open for 1% -> 1% of each run, Pallas kernels for 3% -> 4%
where the time goes in v10:
time: 122 us
  starting transfers between devices  35.6 us (29%)
  blocking collectives  35.4 us (29%)
  waiting for transfers between devices  28.4 us (23%)
  Pallas kernels  17.9 us (15%)
  local copies, waits for them, and re-layouts  2.37 us (2%)
  other arithmetic  1.33 us (1%)
    all_to_all x2, blocking collectives, swap(): return lax.all_to_all(parts, 'pen', 0, 0, tiled=True)  35.4 us
    all_to_all x2, waiting for transfers between devices, swap(): return lax.all_to_all(parts, 'pen', 0, 0, tiled=True)  14.4 us
    all_to_all x2, starting transfers between devices, swap(): return lax.all_to_all(parts, 'pen', 0, 0, tiled=True)  13.9 us
    all_to_all x1, waiting for transfers between devices, sum_over_chips(): lax.all_to_all(parts, ('y', 'zh'), 0, 0, tiled=True).astype(F32)  12.9 us
    all_to_all x1, starting transfers between devices, sum_over_chips(): lax.all_to_all(parts, ('y', 'zh'), 0, 0, tiled=True).astype(F32)  12.7 us
    ppermute x2, starting transfers between devices, from_other_core(): return lax.ppermute(terms, 'core', [(0, 1), (1, 0)])  9 us
    pallas_call x1, Pallas kernels, run_conv_bwd(): pl.pallas_call(conv_bwd, out_shape=shape(GROUPS, PIECE + BH + 8, 128), in...  5.3 us
    pallas_call x1, Pallas kernels, run_conv_fwd(): pl.pallas_call(conv_fwd, out_shape=(shape(ROWS, 128), shape(2, 1024, 128)...  3.69 us
  transfers between devices with their start and end apart: 5, of which 4 were waited for; matrix products, arithmetic and copies ran while one was open for 1% of the time, Pallas kernels for 4%

profile of v10, /device:TPU:1, one launch (start us, length us, event | category | flops | bytes accessed | tf_op | source)
XLA Modules:
  0.0 121.8 jit_solution(16385646195730979998)
XLA Ops:
  0.6 10.4 %all-to-all-start = ((bf16[16,6,8,2,128]{4,3,2,1,0:T(2,128)(2,1)}), bf16[16,6,8,2,128]{4,3,2,1,0:T(2,128)(2,1)S(1)}, u32[]{:S(2)}, u32[]{:S(2)}) async-start(bf16[16,6,8,2,128]{4,3,2,1,0:T(2,128)(2,1)} %bitcast.47), calls=%async_computation | async-start | bytes 786432 | tf_op jit(solution)/shard_map/all_to_all | solution.py:406
  11.1 0.1 dynamic-slice_bitcast_fusion
  11.2 0.1 tile.10
  11.4 0.7 copy-done.1
  12.0 0.3 lay_out.1.cot
  12.4 0.6 copy-done.7
  13.1 0.9 prepare.1
  14.0 9.9 %all-to-all-done = bf16[16,6,8,2,128]{4,3,2,1,0:T(2,128)(2,1)S(1)} async-done(((bf16[16,6,8,2,128]{4,3,2,1,0:T(2,128)(2,1)}), bf16[16,6,8,2,128]{4,3,2,1,0:T(2,128)(2,1)S(1)}, u32[]{:S(2)}, u32[]{:S(2)}) %all-to-all-start) | async-done | bytes 393248 | tf_op jit(solution)/shard_map/all_to_all | solution.py:406
  24.0 3.7 %conv_fwd.1 = (bf16[1536,128]{1,0:T(8,128)(2,1)S(1)}, bf16[2,1024,128]{2,1,0:T(8,128)(2,1)S(1)}, bf16[2,1024,128]{2,1,0:T(8,128)(2,1)S(1)}, bf16[256,1024]{1,0:T(8,128)(2,1)S(1)}) custom-call(s32[4]{0:T(128)S(1)} %pad_add_fusion.dil, bf16[1536,128]{1,0:T(8,128)(2,1)S(1)} %bitcast.36, f32[48,128]{1,0:T(8,128)S(1)} %bitcast.42, ...), custom_call_target="tpu_custom_call" | custom-call | flops 1000000000 | bytes 4000000 | tf_op jit(solution)/shard_map/conv_fwd/pallas_call | solution.py:313
  27.7 16.3 %all_to_all.25 = bf16[16,96,128]{2,1,0:T(8,128)(2,1)S(1)} all-to-all(bf16[16,96,128]{2,1,0:T(8,128)(2,1)S(1)} %bitcast.40), channel_id=1, replica_groups=mesh['zh'=2,'y'=8,'core'=2,'pen'=16] {'pen'}, dimensions={0} | all-to-all | bytes 786432 | tf_op jit(solution)/shard_map/all_to_all | solution.py:406
  44.0 3.6 %middle.1 = bf16[1536,128]{1,0:T(8,128)(2,1)} custom-call(bf16[1536,128]{1,0:T(8,128)(2,1)S(1)} %bitcast.38, bf16[96,2048]{1,0:T(8,128)(2,1)S(1)} %lay_out.1.cot, bf16[96,384]{1,0:T(8,128)(2,1)S(1)} %copy-done.2, bf16[96,384]{1,0:T(8,128)(2,1)S(1)} %bitcast.44), custom_call_target="tpu_custom_call" | custom-call | flops 1000000000 | bytes 4000000 | tf_op jit(solution)/shard_map/middle/pallas_call | solution.py:360
  47.6 3.6 %all-to-all-start.2 = ((bf16[16,96,128]{2,1,0:T(8,128)(2,1)}), bf16[16,96,128]{2,1,0:T(8,128)(2,1)S(1)}, u32[]{:S(2)}, u32[]{:S(2)}) async-start(bf16[16,96,128]{2,1,0:T(8,128)(2,1)} %bitcast.13), calls=%async_computation.2 | async-start | bytes 786432 | tf_op jit(solution)/shard_map/all_to_all | solution.py:406
  51.2 3.1 %weight_terms.1 = (f32[384,96]{1,0:T(8,128)S(1)}, f32[384,96]{1,0:T(8,128)S(1)}) custom-call(s32[1]{0:T(128)} %bitcast.15.core, bf16[1536,128]{1,0:T(8,128)(2,1)S(1)} %bitcast.39, bf16[96,2048]{1,0:T(8,128)(2,1)S(1)} %lay_out.1.cot, bf16[96,384]{1,0:T(8,128)(2,1)S(1)} %copy-done.2, bf16[96,384]{1,0:T(8,128)(2,1)S(1)} %bitcast.45), custom_call_target="tpu_custom_call" | custom-call | flops 1000000000 | bytes 4000000 | tf_op jit(solution)/shard_map/weight_terms/pallas_call | solution.py:373
  54.3 3.8 %collective-permute-start = (f32[384,96]{1,0:T(8,128)S(1)}, f32[384,96]{1,0:T(8,128)S(1)}, u32[]{:S(2)}, u32[]{:S(2)}) collective-permute-start(f32[384,96]{1,0:T(8,128)S(1)} %get-tuple-element.30), channel_id=1, source_target_pairs={{0,16},{16,0},{1,17},{17,1},{2,18},{18,2},{3,19},{19,3},{4,20},{20... | collective-permute-start | bytes 442376 | tf_op jit(solution)/shard_map/ppermute | solution.py:410
  58.1 1.0 collective-permute-done
  59.2 4.4 %all-to-all-done.2 = bf16[16,96,128]{2,1,0:T(8,128)(2,1)S(1)} async-done(((bf16[16,96,128]{2,1,0:T(8,128)(2,1)}), bf16[16,96,128]{2,1,0:T(8,128)(2,1)S(1)}, u32[]{:S(2)}, u32[]{:S(2)}) %all-to-all-start.2) | async-done | bytes 393248 | tf_op jit(solution)/shard_map/all_to_all | solution.py:406
  63.6 5.3 %conv_bwd.1 = bf16[16,128,128]{2,1,0:T(8,128)(2,1)S(1)} custom-call(s32[4]{0:T(128)S(1)} %pad_add_fusion.dil, bf16[1536,128]{1,0:T(8,128)(2,1)S(1)} %bitcast.37, f32[48,128]{1,0:T(8,128)S(1)} %bitcast.43, bf16[256,256]{1,0:T(8,128)(2,1)S(1)} %get-tuple-element.20.hi_ref, bf16[256,256]{1,0:T(8,128)(2,1)S(1)} %get-tuple-element.21.lo_ref, ...), custom_call_target="tpu_custom_call" | custom-call | flops 1000000000 | bytes 4000000 | tf_op jit(solution)/shard_map/conv_bwd/pallas_call | solution.py:327
  68.9 19.0 %all_to_all.26 = bf16[16,128,128]{2,1,0:T(8,128)(2,1)S(1)} all-to-all(bf16[16,128,128]{2,1,0:T(8,128)(2,1)S(1)} %conv_bwd.1), channel_id=1, replica_groups=mesh['zh'=2,'y'=8,'core'=2,'pen'=16] {'pen'}, dimensions={0} | all-to-all | bytes 1048576 | tf_op jit(solution)/shard_map/all_to_all | solution.py:406
  88.1 0.7 broadcast_in_dim.15
  88.8 12.7 %all-to-all-start.4 = ((bf16[16,48,128]{2,1,0:T(8,128)(2,1)}), bf16[16,48,128]{2,1,0:T(8,128)(2,1)S(1)}, u32[]{:S(2)}, u32[]{:S(2)}) async-start(bf16[16,48,128]{2,1,0:T(8,128)(2,1)} %broadcast_in_dim.15), calls=%async_computation.4 | async-start | bytes 393216 | tf_op jit(solution)/shard_map/all_to_all | solution.py:416
  101.5 12.9 %all-to-all-done.4 = bf16[16,48,128]{2,1,0:T(8,128)(2,1)S(1)} async-done(((bf16[16,48,128]{2,1,0:T(8,128)(2,1)}), bf16[16,48,128]{2,1,0:T(8,128)(2,1)S(1)}, u32[]{:S(2)}, u32[]{:S(2)}) %all-to-all-start.4) | async-done | bytes 196640 | tf_op jit(solution)/shard_map/all_to_all | solution.py:416
  114.5 5.2 %collective-permute-start.1 = (f32[48,128]{1,0:T(8,128)S(1)}, f32[48,128]{1,0:T(8,128)S(1)}, u32[]{:S(2)}, u32[]{:S(2)}) collective-permute-start(f32[48,128]{1,0:T(8,128)S(1)} %convert_reduce_fusion.mine_ref), channel_id=1, source_target_pairs={{0,16},{16,0},{1,17},{17,1},{2,18},{18,2},{3,19},{19,3},{4,20},{20... | collective-permute-start | bytes 73736 | tf_op jit(solution)/shard_map/ppermute | solution.py:410
  119.7 1.2 fusion.1
  120.8 1.0 finish.1
  (26 shorter events, 0.3 us)
Async XLA Ops:
  0.6 10.4 %copy-start = (f32[3,96,9]{1,0,2:T(4,128)S(1)}, f32[3,96,9]{1,0,2:T(4,128)}, u32[]{:S(2)}) copy-start(f32[3,96,9]{1,0,2:T(4,128)} %param.9) | copy-start | bytes 31108
  0.6 23.3 %all-to-all-start = ((bf16[16,6,8,2,128]{4,3,2,1,0:T(2,128)(2,1)}), bf16[16,6,8,2,128]{4,3,2,1,0:T(2,128)(2,1)S(1)}, u32[]{:S(2)}, u32[]{:S(2)}) async-start(bf16[16,6,8,2,128]{4,3,2,1,0:T(2,128)(2,1)} %bitcast.47), calls=%async_computation | async-start | bytes 786432 | tf_op jit(solution)/shard_map/all_to_all | solution.py:406
  11.0 1.0 copy-start.1
  12.0 1.0 copy-start.4
  12.4 0.7 copy-start.7
  27.6 16.3 %copy-start.5 = (bf16[256,1024]{1,0:T(8,128)(2,1)}, bf16[256,1024]{1,0:T(8,128)(2,1)S(1)}, u32[]{:S(2)}) copy-start(bf16[256,1024]{1,0:T(8,128)(2,1)S(1)} %get-tuple-element.28.field_ref) | copy-start | bytes 1572868
  27.7 16.3 %copy-start.2 = (bf16[96,384]{1,0:T(8,128)(2,1)S(1)}, bf16[96,384]{1,0:T(8,128)(2,1)}, u32[]{:S(2)}) copy-start(bf16[96,384]{1,0:T(8,128)(2,1)} %we.3) | copy-start | bytes 221188
  27.7 16.3 %copy-start.3 = (bf16[384,96]{0,1:T(8,128)(2,1)S(1)}, bf16[384,96]{0,1:T(8,128)(2,1)}, u32[]{:S(2)}) copy-start(bf16[384,96]{0,1:T(8,128)(2,1)} %param.12) | copy-start | bytes 221188
  47.6 16.0 %all-to-all-start.2 = ((bf16[16,96,128]{2,1,0:T(8,128)(2,1)}), bf16[16,96,128]{2,1,0:T(8,128)(2,1)S(1)}, u32[]{:S(2)}, u32[]{:S(2)}) async-start(bf16[16,96,128]{2,1,0:T(8,128)(2,1)} %bitcast.13), calls=%async_computation.2 | async-start | bytes 786432 | tf_op jit(solution)/shard_map/all_to_all | solution.py:406
  54.3 9.3 %copy-start.6 = (bf16[256,1024]{1,0:T(8,128)(2,1)S(1)}, bf16[256,1024]{1,0:T(8,128)(2,1)}, u32[]{:S(2)}) copy-start(bf16[256,1024]{1,0:T(8,128)(2,1)} %copy-done.5) | copy-start | bytes 1572868
  54.3 4.8 %collective-permute-start = (f32[384,96]{1,0:T(8,128)S(1)}, f32[384,96]{1,0:T(8,128)S(1)}, u32[]{:S(2)}, u32[]{:S(2)}) collective-permute-start(f32[384,96]{1,0:T(8,128)S(1)} %get-tuple-element.30), channel_id=1, source_target_pairs={{0,16},{16,0},{1,17},{17,1},{2,18},{18,2},{3,19},{19,3},{4,20},{20... | collective-permute-start | bytes 442376 | tf_op jit(solution)/shard_map/ppermute | solution.py:410
  88.8 25.6 %all-to-all-start.4 = ((bf16[16,48,128]{2,1,0:T(8,128)(2,1)}), bf16[16,48,128]{2,1,0:T(8,128)(2,1)S(1)}, u32[]{:S(2)}, u32[]{:S(2)}) async-start(bf16[16,48,128]{2,1,0:T(8,128)(2,1)} %broadcast_in_dim.15), calls=%async_computation.4 | async-start | bytes 393216 | tf_op jit(solution)/shard_map/all_to_all | solution.py:416
  114.5 6.4 %collective-permute-start.1 = (f32[48,128]{1,0:T(8,128)S(1)}, f32[48,128]{1,0:T(8,128)S(1)}, u32[]{:S(2)}, u32[]{:S(2)}) collective-permute-start(f32[48,128]{1,0:T(8,128)S(1)} %convert_reduce_fusion.mine_ref), channel_id=1, source_target_pairs={{0,16},{16,0},{1,17},{17,1},{2,18},{18,2},{3,19},{19,3},{4,20},{20... | collective-permute-start | bytes 73736 | tf_op jit(solution)/shard_map/ppermute | solution.py:410

commit v11 on v10

--- a/solution.py
+++ b/solution.py
@@ -413,7 +413,7 @@
 def sum_over_chips(terms):
     size = lax.axis_size("zh") * lax.axis_size("y")
     parts = jnp.broadcast_to(terms.astype(BF16)[None], (size,) + terms.shape)
-    return jnp.sum(lax.all_to_all(parts, ("y", "zh"), 0, 0, tiled=True).astype(F32), axis=0)
+    return jnp.sum(lax.all_to_all(parts, ("zh", "y"), 0, 0, tiled=True).astype(F32), axis=0)
 
 
 def per_device(activations, cotangent, depth_kernels, dilations, expand_weight, reduce_weight):

time: 122 us -> 121 us (level)
  waiting for transfers between devices: 28.4 us -> 27.1 us
    all_to_all x1, waiting for transfers between devices: 12.9 us -> 11.6 us  [sum_over_chips(): lax.all_to_all(parts, ('zh', 'y'), 0, 0, tiled=True).astype(F32)]
where the time goes in v11:
time: 121 us; the launch traced here: 120 us
  blocking collectives  35.4 us (29%)
  starting transfers between devices  35.3 us (29%)
  waiting for transfers between devices  27.1 us (22%)
  Pallas kernels  17.9 us (15%)
  local copies, waits for them, and re-layouts  2.37 us (2%)
  other arithmetic  1.33 us (1%)
    all_to_all x2, blocking collectives, swap(): return lax.all_to_all(parts, 'pen', 0, 0, tiled=True)  35.4 us
    all_to_all x2, waiting for transfers between devices, swap(): return lax.all_to_all(parts, 'pen', 0, 0, tiled=True)  14.4 us
    all_to_all x2, starting transfers between devices, swap(): return lax.all_to_all(parts, 'pen', 0, 0, tiled=True)  13.9 us
    all_to_all x1, starting transfers between devices, sum_over_chips(): lax.all_to_all(parts, ('zh', 'y'), 0, 0, tiled=True).astype(F32)  12.7 us
    all_to_all x1, waiting for transfers between devices, sum_over_chips(): lax.all_to_all(parts, ('zh', 'y'), 0, 0, tiled=True).astype(F32)  11.6 us
    ppermute x2, starting transfers between devices, from_other_core(): return lax.ppermute(terms, 'core', [(0, 1), (1, 0)])  8.7 us
    pallas_call x1, Pallas kernels, run_conv_bwd(): pl.pallas_call(conv_bwd, out_shape=shape(GROUPS, PIECE + BH + 8, 128), in...  5.3 us
    pallas_call x1, Pallas kernels, run_conv_fwd(): pl.pallas_call(conv_fwd, out_shape=(shape(ROWS, 128), shape(2, 1024, 128)...  3.69 us
  transfers between devices with their start and end apart: 5, of which 4 were waited for; matrix products, arithmetic and copies ran while one was open for 1% of the time, Pallas kernels for 4%

profile of v11, /device:TPU:1, one launch (start us, length us, event | category | flops | bytes accessed | tf_op | source)
XLA Modules:
  0.0 120.2 jit_solution(9204553046679119513)
XLA Ops:
  0.6 10.4 %all-to-all-start = ((bf16[16,6,8,2,128]{4,3,2,1,0:T(2,128)(2,1)}), bf16[16,6,8,2,128]{4,3,2,1,0:T(2,128)(2,1)S(1)}, u32[]{:S(2)}, u32[]{:S(2)}) async-start(bf16[16,6,8,2,128]{4,3,2,1,0:T(2,128)(2,1)} %bitcast.47), calls=%async_computation | async-start | bytes 786432 | tf_op jit(solution)/shard_map/all_to_all | solution.py:406
  11.1 0.1 dynamic-slice_bitcast_fusion
  11.2 0.1 tile.10
  11.4 0.7 copy-done.1
  12.0 0.3 lay_out.1.cot
  12.4 0.6 copy-done.7
  13.1 0.9 prepare.1
  14.0 9.9 %all-to-all-done = bf16[16,6,8,2,128]{4,3,2,1,0:T(2,128)(2,1)S(1)} async-done(((bf16[16,6,8,2,128]{4,3,2,1,0:T(2,128)(2,1)}), bf16[16,6,8,2,128]{4,3,2,1,0:T(2,128)(2,1)S(1)}, u32[]{:S(2)}, u32[]{:S(2)}) %all-to-all-start) | async-done | bytes 393248 | tf_op jit(solution)/shard_map/all_to_all | solution.py:406
  24.0 3.7 %conv_fwd.1 = (bf16[1536,128]{1,0:T(8,128)(2,1)S(1)}, bf16[2,1024,128]{2,1,0:T(8,128)(2,1)S(1)}, bf16[2,1024,128]{2,1,0:T(8,128)(2,1)S(1)}, bf16[256,1024]{1,0:T(8,128)(2,1)S(1)}) custom-call(s32[4]{0:T(128)S(1)} %pad_add_fusion.dil, bf16[1536,128]{1,0:T(8,128)(2,1)S(1)} %bitcast.36, f32[48,128]{1,0:T(8,128)S(1)} %bitcast.42, ...), custom_call_target="tpu_custom_call" | custom-call | flops 1000000000 | bytes 4000000 | tf_op jit(solution)/shard_map/conv_fwd/pallas_call | solution.py:313
  27.7 16.3 %all_to_all.25 = bf16[16,96,128]{2,1,0:T(8,128)(2,1)S(1)} all-to-all(bf16[16,96,128]{2,1,0:T(8,128)(2,1)S(1)} %bitcast.40), channel_id=1, replica_groups=mesh['zh'=2,'y'=8,'core'=2,'pen'=16] {'pen'}, dimensions={0} | all-to-all | bytes 786432 | tf_op jit(solution)/shard_map/all_to_all | solution.py:406
  44.0 3.6 %middle.1 = bf16[1536,128]{1,0:T(8,128)(2,1)} custom-call(bf16[1536,128]{1,0:T(8,128)(2,1)S(1)} %bitcast.38, bf16[96,2048]{1,0:T(8,128)(2,1)S(1)} %lay_out.1.cot, bf16[96,384]{1,0:T(8,128)(2,1)S(1)} %copy-done.2, bf16[96,384]{1,0:T(8,128)(2,1)S(1)} %bitcast.44), custom_call_target="tpu_custom_call" | custom-call | flops 1000000000 | bytes 4000000 | tf_op jit(solution)/shard_map/middle/pallas_call | solution.py:360
  47.6 3.6 %all-to-all-start.2 = ((bf16[16,96,128]{2,1,0:T(8,128)(2,1)}), bf16[16,96,128]{2,1,0:T(8,128)(2,1)S(1)}, u32[]{:S(2)}, u32[]{:S(2)}) async-start(bf16[16,96,128]{2,1,0:T(8,128)(2,1)} %bitcast.13), calls=%async_computation.2 | async-start | bytes 786432 | tf_op jit(solution)/shard_map/all_to_all | solution.py:406
  51.2 3.1 %weight_terms.1 = (f32[384,96]{1,0:T(8,128)S(1)}, f32[384,96]{1,0:T(8,128)S(1)}) custom-call(s32[1]{0:T(128)} %bitcast.15.core, bf16[1536,128]{1,0:T(8,128)(2,1)S(1)} %bitcast.39, bf16[96,2048]{1,0:T(8,128)(2,1)S(1)} %lay_out.1.cot, bf16[96,384]{1,0:T(8,128)(2,1)S(1)} %copy-done.2, bf16[96,384]{1,0:T(8,128)(2,1)S(1)} %bitcast.45), custom_call_target="tpu_custom_call" | custom-call | flops 1000000000 | bytes 4000000 | tf_op jit(solution)/shard_map/weight_terms/pallas_call | solution.py:373
  54.3 3.8 %collective-permute-start = (f32[384,96]{1,0:T(8,128)S(1)}, f32[384,96]{1,0:T(8,128)S(1)}, u32[]{:S(2)}, u32[]{:S(2)}) collective-permute-start(f32[384,96]{1,0:T(8,128)S(1)} %get-tuple-element.30), channel_id=1, source_target_pairs={{0,16},{16,0},{1,17},{17,1},{2,18},{18,2},{3,19},{19,3},{4,20},{20... | collective-permute-start | bytes 442376 | tf_op jit(solution)/shard_map/ppermute | solution.py:410
  58.1 1.0 collective-permute-done
  59.2 4.4 %all-to-all-done.2 = bf16[16,96,128]{2,1,0:T(8,128)(2,1)S(1)} async-done(((bf16[16,96,128]{2,1,0:T(8,128)(2,1)}), bf16[16,96,128]{2,1,0:T(8,128)(2,1)S(1)}, u32[]{:S(2)}, u32[]{:S(2)}) %all-to-all-start.2) | async-done | bytes 393248 | tf_op jit(solution)/shard_map/all_to_all | solution.py:406
  63.6 5.3 %conv_bwd.1 = bf16[16,128,128]{2,1,0:T(8,128)(2,1)S(1)} custom-call(s32[4]{0:T(128)S(1)} %pad_add_fusion.dil, bf16[1536,128]{1,0:T(8,128)(2,1)S(1)} %bitcast.37, f32[48,128]{1,0:T(8,128)S(1)} %bitcast.43, bf16[256,256]{1,0:T(8,128)(2,1)S(1)} %get-tuple-element.20.hi_ref, bf16[256,256]{1,0:T(8,128)(2,1)S(1)} %get-tuple-element.21.lo_ref, ...), custom_call_target="tpu_custom_call" | custom-call | flops 1000000000 | bytes 4000000 | tf_op jit(solution)/shard_map/conv_bwd/pallas_call | solution.py:327
  68.9 19.0 %all_to_all.26 = bf16[16,128,128]{2,1,0:T(8,128)(2,1)S(1)} all-to-all(bf16[16,128,128]{2,1,0:T(8,128)(2,1)S(1)} %conv_bwd.1), channel_id=1, replica_groups=mesh['zh'=2,'y'=8,'core'=2,'pen'=16] {'pen'}, dimensions={0} | all-to-all | bytes 1048576 | tf_op jit(solution)/shard_map/all_to_all | solution.py:406
  88.1 0.7 broadcast_in_dim.15
  88.8 12.7 %all-to-all-start.4 = ((bf16[16,48,128]{2,1,0:T(8,128)(2,1)}), bf16[16,48,128]{2,1,0:T(8,128)(2,1)S(1)}, u32[]{:S(2)}, u32[]{:S(2)}) async-start(bf16[16,48,128]{2,1,0:T(8,128)(2,1)} %broadcast_in_dim.15), calls=%async_computation.4 | async-start | bytes 393216 | tf_op jit(solution)/shard_map/all_to_all | solution.py:416
  101.5 11.6 %all-to-all-done.4 = bf16[16,48,128]{2,1,0:T(8,128)(2,1)S(1)} async-done(((bf16[16,48,128]{2,1,0:T(8,128)(2,1)}), bf16[16,48,128]{2,1,0:T(8,128)(2,1)S(1)}, u32[]{:S(2)}, u32[]{:S(2)}) %all-to-all-start.4) | async-done | bytes 196640 | tf_op jit(solution)/shard_map/all_to_all | solution.py:416
  113.2 4.9 %collective-permute-start.1 = (f32[48,128]{1,0:T(8,128)S(1)}, f32[48,128]{1,0:T(8,128)S(1)}, u32[]{:S(2)}, u32[]{:S(2)}) collective-permute-start(f32[48,128]{1,0:T(8,128)S(1)} %convert_reduce_fusion.mine_ref), channel_id=1, source_target_pairs={{0,16},{16,0},{1,17},{17,1},{2,18},{18,2},{3,19},{19,3},{4,20},{20... | collective-permute-start | bytes 73736 | tf_op jit(solution)/shard_map/ppermute | solution.py:410
  118.1 1.2 fusion.1
  119.2 1.0 finish.1
  (26 shorter events, 0.3 us)
Async XLA Ops:
  0.6 10.4 %copy-start = (f32[3,96,9]{1,0,2:T(4,128)S(1)}, f32[3,96,9]{1,0,2:T(4,128)}, u32[]{:S(2)}) copy-start(f32[3,96,9]{1,0,2:T(4,128)} %param.9) | copy-start | bytes 31108
  0.6 23.3 %all-to-all-start = ((bf16[16,6,8,2,128]{4,3,2,1,0:T(2,128)(2,1)}), bf16[16,6,8,2,128]{4,3,2,1,0:T(2,128)(2,1)S(1)}, u32[]{:S(2)}, u32[]{:S(2)}) async-start(bf16[16,6,8,2,128]{4,3,2,1,0:T(2,128)(2,1)} %bitcast.47), calls=%async_computation | async-start | bytes 786432 | tf_op jit(solution)/shard_map/all_to_all | solution.py:406
  11.0 1.0 copy-start.1
  12.0 1.0 copy-start.4
  12.4 0.7 copy-start.7
  27.6 16.3 %copy-start.5 = (bf16[256,1024]{1,0:T(8,128)(2,1)}, bf16[256,1024]{1,0:T(8,128)(2,1)S(1)}, u32[]{:S(2)}) copy-start(bf16[256,1024]{1,0:T(8,128)(2,1)S(1)} %get-tuple-element.28.field_ref) | copy-start | bytes 1572868
  27.7 16.3 %copy-start.2 = (bf16[96,384]{1,0:T(8,128)(2,1)S(1)}, bf16[96,384]{1,0:T(8,128)(2,1)}, u32[]{:S(2)}) copy-start(bf16[96,384]{1,0:T(8,128)(2,1)} %we.3) | copy-start | bytes 221188
  27.7 16.3 %copy-start.3 = (bf16[384,96]{0,1:T(8,128)(2,1)S(1)}, bf16[384,96]{0,1:T(8,128)(2,1)}, u32[]{:S(2)}) copy-start(bf16[384,96]{0,1:T(8,128)(2,1)} %param.12) | copy-start | bytes 221188
  47.6 16.0 %all-to-all-start.2 = ((bf16[16,96,128]{2,1,0:T(8,128)(2,1)}), bf16[16,96,128]{2,1,0:T(8,128)(2,1)S(1)}, u32[]{:S(2)}, u32[]{:S(2)}) async-start(bf16[16,96,128]{2,1,0:T(8,128)(2,1)} %bitcast.13), calls=%async_computation.2 | async-start | bytes 786432 | tf_op jit(solution)/shard_map/all_to_all | solution.py:406
  54.3 9.3 %copy-start.6 = (bf16[256,1024]{1,0:T(8,128)(2,1)S(1)}, bf16[256,1024]{1,0:T(8,128)(2,1)}, u32[]{:S(2)}) copy-start(bf16[256,1024]{1,0:T(8,128)(2,1)} %copy-done.5) | copy-start | bytes 1572868
  54.3 4.8 %collective-permute-start = (f32[384,96]{1,0:T(8,128)S(1)}, f32[384,96]{1,0:T(8,128)S(1)}, u32[]{:S(2)}, u32[]{:S(2)}) collective-permute-start(f32[384,96]{1,0:T(8,128)S(1)} %get-tuple-element.30), channel_id=1, source_target_pairs={{0,16},{16,0},{1,17},{17,1},{2,18},{18,2},{3,19},{19,3},{4,20},{20... | collective-permute-start | bytes 442376 | tf_op jit(solution)/shard_map/ppermute | solution.py:410
  88.8 24.4 %all-to-all-start.4 = ((bf16[16,48,128]{2,1,0:T(8,128)(2,1)}), bf16[16,48,128]{2,1,0:T(8,128)(2,1)S(1)}, u32[]{:S(2)}, u32[]{:S(2)}) async-start(bf16[16,48,128]{2,1,0:T(8,128)(2,1)} %broadcast_in_dim.15), calls=%async_computation.4 | async-start | bytes 393216 | tf_op jit(solution)/shard_map/all_to_all | solution.py:416
  113.2 6.1 %collective-permute-start.1 = (f32[48,128]{1,0:T(8,128)S(1)}, f32[48,128]{1,0:T(8,128)S(1)}, u32[]{:S(2)}, u32[]{:S(2)}) collective-permute-start(f32[48,128]{1,0:T(8,128)S(1)} %convert_reduce_fusion.mine_ref), channel_id=1, source_target_pairs={{0,16},{16,0},{1,17},{17,1},{2,18},{18,2},{3,19},{19,3},{4,20},{20... | collective-permute-start | bytes 73736 | tf_op jit(solution)/shard_map/ppermute | solution.py:410
